TPU v7x, 32 devices: a whole 2x2x4 slice. The times are simulated.
32 devices in a mesh: dom: 8 (over y, x, core), feat: 4 (over z).
Axes of the slice: x: 2, y: 2, z: 4, core: 2. Of those that a mesh axis runs over, the one named last changes fastest.
Arguments:
- state: bfloat16 [512, 16384], P('feat', 'dom'), may hold values from -3 to 3
- inputs: bfloat16 [2, 16384], P(None, 'dom'), may hold values from -6 to 6
- adj_tiles: bfloat16 [128, 4, 128, 128], P('dom'), may hold values from -0.25 to 0.25
- adj_cols: int32 [128, 4], P('dom'), may hold values from 0 to 17, as said below
- valid_rows: int32 [8], P('dom'), may hold values from 1024 to 2048, as said below
- cluster_of: int32 [16384], P('dom'), may hold values from 0 to 2047
- w_gates: bfloat16 [3, 512, 4, 512], P(None, 'feat'), may hold values from -0.125 to 0.125
- w_input: bfloat16 [3, 512, 2], P(None, 'feat'), may hold values from -4 to 4
- bias: float32 [3, 512], P(None, 'feat'), may hold values from -4 to 4
- w_value: bfloat16 [8, 64, 64], P('feat'), may hold values from -0.75 to 0.75
- source_emb: float32 [8, 10, 2048], P('feat'), may hold values from -5 to 5
- target_emb: float32 [8, 10, 2048], P('feat'), may hold values from -5 to 5
- coarse_tiles: bfloat16 [16, 2, 128, 128], replicated, may hold values from -0.375 to 0.375
- coarse_cols: int32 [16, 2], replicated, may hold values from 0 to 15
Outputs:
- new_state: bfloat16 [512, 16384], P('feat', 'dom')
Inputs may be any that keep to these rules, and one draw needn't show every extreme that they name: `adj_cols`: for local row tile t of a partition (t counted from 0 in the partition), every entry lies in t to t + 2, the first is t and the last is t + 2. `valid_rows`: some partition has all 2048 rows valid and another exactly half of them.
All inputs are finite; a program needn't handle non-finite values.
Results may differ from a plain program's by a relative error of at most 0.003.
Values may be sent and summed in bfloat16 or wider, within the bound.
No kernel may reach another device: no remote copies, remote signals or barrier semaphores. Data moves between devices by JAX's collectives and lax.ppermute only.
A program may use at most 64 MiB of HBM per device.

v0:
```python
import math

import jax
import jax.numpy as jnp
from jax import lax
from jax.sharding import PartitionSpec as P


def extended_2(array, sides, width):
    for axis, dim in sides:
        peers, length = (lax.axis_size(axis), array.shape[dim])
        up = [(i, (i + 1) % peers) for i in range(peers)]
        down = [(j, i) for i, j in up]
        last = lax.slice_in_dim(array, length - width, length, axis=dim)
        leading = lax.slice_in_dim(array, 0, width, axis=dim)
        before = lax.ppermute(last, axis, up)
        after = lax.ppermute(leading, axis, down)
        array = jnp.concatenate([before, array, after], axis=dim)
    return array


def diffuse(states, adj_tiles, adj_cols, row_mask):
    tile_size = adj_tiles.shape[2]
    channels, row_count = states.shape
    extended = extended_2(states, (("dom", 1),), tile_size)
    extended = extended.reshape(channels, row_count // tile_size + 2, tile_size)
    picked = extended[:, adj_cols]
    result = jnp.einsum("hnkj,nkji->hni", picked, adj_tiles, preferred_element_type=jnp.float32)
    return (result.reshape(channels, row_count) * row_mask).astype(jnp.bfloat16)


def project(pooled, w_value):
    heads_here, head_size = (w_value.shape[0], w_value.shape[1])
    grouped = pooled.reshape(heads_here, head_size, pooled.shape[1])
    return jnp.einsum(
        "hde,hec->hdc", w_value.astype(jnp.float32), grouped, precision=lax.Precision.HIGHEST
    ).astype(jnp.bfloat16)


def attend(source_cols, target_emb, values):
    heads_here, emb_dim, query_count = source_cols.shape
    block_rows = math.gcd(query_count, 512)
    blocks = source_cols.reshape(heads_here, emb_dim, query_count // block_rows, block_rows)
    blocks = jnp.moveaxis(blocks, 2, 0)

    def one_block(source_block):
        scores = jnp.einsum(
            "hei,hej->hij", source_block, target_emb, precision=lax.Precision.HIGHEST
        )
        scores = jnp.maximum(scores, 0.0)
        row_peak = jnp.max(scores, axis=2, keepdims=True)
        raised = jnp.exp(scores - row_peak)
        weights = (raised / jnp.sum(raised, axis=2, keepdims=True)).astype(jnp.bfloat16)
        return jnp.einsum("hdj,hij->hdi", values, weights, preferred_element_type=jnp.float32)

    outputs = lax.map(one_block, blocks)
    outputs = jnp.moveaxis(outputs, 0, 2)
    return outputs.reshape(heads_here, values.shape[1], query_count)


def body(
    state,
    inputs,
    adj_tiles,
    adj_cols,
    valid_rows,
    cluster_of,
    w_gates,
    w_input,
    bias,
    w_value,
    source_emb,
    target_emb,
    coarse_tiles,
    coarse_cols,
):
    channels, row_count = state.shape
    cluster_count = source_emb.shape[2]
    row_mask = (jnp.arange(row_count, dtype=jnp.int32) < valid_rows[0]).astype(jnp.float32)
    masked = (state.astype(jnp.float32) * row_mask).astype(jnp.bfloat16)
    hop_one = diffuse(masked, adj_tiles, adj_cols, row_mask)
    hop_two = diffuse(hop_one, adj_tiles, adj_cols, row_mask)
    member = (cluster_of[:, None] == jnp.arange(cluster_count, dtype=jnp.int32)[None, :]).astype(
        jnp.bfloat16
    )
    cluster_sums = jnp.dot(masked, member, preferred_element_type=jnp.float32)
    counts = jnp.dot(
        row_mask.astype(jnp.bfloat16)[None, :], member, preferred_element_type=jnp.float32
    )
    cluster_sums, counts = (
        lax.psum_scatter(
            cluster_sums.astype(jnp.bfloat16), "dom", scatter_dimension=1, tiled=True
        ).astype(jnp.float32),
        lax.psum_scatter(
            counts.astype(jnp.bfloat16), "dom", scatter_dimension=1, tiled=True
        ).astype(jnp.float32),
    )
    pooled = cluster_sums / jnp.maximum(counts, 1.0)
    share_count = pooled.shape[1]
    own_values = project(pooled, w_value)
    all_values = lax.all_gather(own_values, "dom", axis=2, tiled=True)
    source_cols = lax.dynamic_slice_in_dim(
        source_emb, lax.axis_index("dom") * share_count, share_count, 2
    )
    attended = attend(source_cols, target_emb, all_values)
    own_coarse = (pooled + attended.reshape(channels, share_count)).astype(jnp.bfloat16)
    coarse_attn = lax.all_gather(own_coarse, "dom", axis=1, tiled=True)
    tile_size = coarse_tiles.shape[2]
    coarse_grid = coarse_attn.reshape(channels, cluster_count // tile_size, tile_size)
    picked = coarse_grid[:, coarse_cols]
    coarse_terms = jnp.einsum(
        "hnkj,nkji->hni", picked, coarse_tiles, preferred_element_type=jnp.float32
    )
    coarse = (
        coarse_attn.astype(jnp.float32) + coarse_terms.reshape(channels, cluster_count)
    ).astype(jnp.bfloat16)
    unpooled = jnp.take(coarse, cluster_of, axis=1)
    features = jnp.stack([masked, hop_one, hop_two, unpooled])
    gate_sums = jnp.einsum(
        "ghkc,kcr->ghr",
        w_gates,
        lax.all_gather(features, "feat", axis=1, tiled=True),
        preferred_element_type=jnp.float32,
    )
    input_terms = (
        jnp.einsum("ghf,fr->ghr", w_input, inputs, preferred_element_type=jnp.float32)
        + bias[:, :, None]
    )
    update = jax.nn.sigmoid(input_terms[0] + gate_sums[0])
    reset = jax.nn.sigmoid(input_terms[1] + gate_sums[1])
    candidate = jnp.tanh(input_terms[2] + reset * gate_sums[2])
    fresh_state = (update * masked.astype(jnp.float32) + (1.0 - update) * candidate) * row_mask
    return fresh_state.astype(jnp.bfloat16)


def solution(mesh):
    return jax.shard_map(
        body,
        mesh=mesh,
        in_specs=(
            P("feat", "dom"),
            P(None, "dom"),
            P("dom", None, None, None),
            P("dom", None),
            P("dom"),
            P("dom"),
            P(None, "feat", None, None),
            P(None, "feat", None),
            P(None, "feat"),
            P("feat", None, None),
            P("feat", None, None),
            P("feat", None, None),
            P(),
            P(),
        ),
        out_specs=P("feat", "dom"),
        check_vma=False,
    )
```

profile of v0, /device:TPU:0, one launch (start us, length us, event | category | flops | bytes accessed | tf_op | source)
XLA Modules:
  0.0 299.1 jit_solution(8015840832279791821)
XLA Ops:
  7.4 1.1 multiply_convert_fusion.3
  8.5 0.5 collective-permute-start
  9.0 2.9 collective-permute-start.1
  12.0 3.8 %fusion.1 = f32[1,2048]{1,0:T(1,128)S(1)} fusion(bf16[2048,1]{0,1:T(2,128)(2,1)S(1)} %reshape.207, s32[2048]{0:T(1024)} %param.19), kind=kOutput, calls=%fused_computation.6 | convolution fusion | flops 12582912 | bytes 20480 | tf_op jit(solution)/shard_map/dot_general | solution.py:87
  15.8 1.1 reshape_bitcast_fusion
  17.0 0.0 reduce-scatter.7.cloned.1.call-update
  17.0 0.0 copy-start.12
  17.0 0.0 reduce-scatter.5.cloned.1.call-start
  17.1 4.5 %fusion.11 = bf16[128,2048]{1,0:T(8,128)(2,1)} fusion(bf16[128,2048]{1,0:T(8,128)(2,1)S(1)} %multiply_convert_fusion.3, s32[2048]{0:T(1024)S(1)} %copy-done.10), kind=kOutput, calls=%fused_computation.18 | convolution fusion | flops 1078198272 | bytes 1056768 | tf_op jit(solution)/shard_map/dot_general | solution.py:86
  21.6 0.0 reduce-scatter.5.cloned.1.call-update
  21.6 0.2 all-gather.2.cloned.1.call-start
  21.9 0.9 fusion.66
  22.8 0.1 copy.56
  22.9 0.1 reshape.167
  23.0 0.7 constant_dynamic-slice_fusion
  23.7 3.5 %fusion.32 = f32[2,256,2048]{2,1,0:T(8,128)S(1)} fusion(f32[2,10,2048]{2,0,1:T(2,128)S(1)} %copy-done.7, f32[2,10,256]{2,0,1:T(2,128)S(1)} %constant_dynamic-slice_fusion), kind=kOutput, calls=%fused_computation.54 | convolution fusion | flops 125829120 | bytes 4378624 | tf_op jit(solution)/shard_map/while/body/eval_jaxpr/hei,hej->hij/dot_general | solution.py:47
  27.2 1.1 fusion.50
  28.4 0.8 copy-done.5
  29.2 0.1 copy.67
  29.3 0.1 reshape.183
  29.4 0.9 pad_maximum_fusion.1
  30.3 1.4 copy.55
  31.6 0.3 copy.57
  32.0 2.2 gather_fusion
  34.1 2.3 fusion.51
  36.5 1.3 copy.85
  37.8 1.3 multiply_convert_fusion.1
  39.1 0.8 copy-done.6
  40.0 0.1 collective-permute-start.2
  40.0 2.6 collective-permute-start.3
  42.6 9.7 %reduce-scatter.7.cloned.1.call-done = bf16[256,1]{1,0:T(8,128)(2,1)} async-done(((bf16[2048,1]{1,0:T(8,128)(2,1)}), bf16[256,1]{1,0:T(8,128)(2,1)}) %reduce-scatter.7.cloned.1.call-update) | async-done | bytes 528
  52.3 0.8 maximum_bitcast_fusion
  53.2 0.1 copy.94
  53.3 1.3 copy.84
  54.6 1.1 pad_maximum_fusion.2
  55.7 0.3 copy.61
  56.0 0.3 copy.62
  56.3 2.2 gather_fusion.1
  58.5 3.4 %fusion.52 = f32[16,128,128,1]{1,2,3,0:T(8,128)} fusion(bf16[128,16,4,128]{3,0,2,1:T(8,128)(2,1)} %bitcast.98, bf16[16,4,128,128]{3,2,1,0:T(8,128)(2,1)S(1)} %copy-done), kind=kOutput, calls=%fused_computation.80 | convolution fusion | flops 268435456 | bytes 5242880 | tf_op jit(solution)/shard_map/hnkj,nkji->hni/dot_general | solution.py:28
  61.9 2.6 copy.86
  64.5 2.4 multiply_convert_fusion.2
  66.9 23.0 %reduce-scatter.5.cloned.1.call-done = bf16[128,256]{1,0:T(8,128)(2,1)} async-done(((bf16[128,2048]{1,0:T(8,128)(2,1)}), bf16[128,256]{1,0:T(8,128)(2,1)}) %reduce-scatter.5.cloned.1.call-update) | async-done | bytes 65552 | tf_op jit(solution)/shard_map/reduce_scatter | solution.py:91
  89.9 0.9 convert_divide_fusion
  90.8 0.2 fusion.15
  91.0 10.8 %all_gather.9 = bf16[2,64,2048]{2,1,0:T(8,128)(2,1)S(1)} all-gather(bf16[2,64,256]{2,1,0:T(8,128)(2,1)S(1)} %fusion.15), channel_id=1, replica_groups=mesh['dom'=8,'feat'=4] {'dom'}, dimensions={2}, use_global_device_ids=true | all-gather | bytes 589824 | tf_op jit(solution)/shard_map/all_gather | solution.py:101
  101.8 3.7 %fusion.13 = f32[2,64,256]{2,1,0:T(8,128)S(1)} fusion(bf16[2,64,2048]{2,1,0:T(8,128)(2,1)S(1)} %all_gather.9, f32[2,256]{1,0:T(2,128)S(1)} %fusion.50, f32[2,256,2048]{2,1,0:T(8,128)} %copy-done.5), kind=kOutput, calls=%fused_computation.21 | convolution fusion | flops 138414592 | bytes 4851712 | tf_op jit(solution)/shard_map/while/body/eval_jaxpr/hdj,hij->hdi/dot_general | solution.py:54
  105.6 10.6 %all_gather.10 = bf16[128,2048]{1,0:T(8,128)(2,1)S(1)} all-gather(bf16[128,256]{1,0:T(8,128)(2,1)S(1)} %fusion.38), channel_id=1, replica_groups=mesh['dom'=8,'feat'=4] {'dom'}, dimensions={1}, use_global_device_ids=true | all-gather | bytes 589824 | tf_op jit(solution)/shard_map/all_gather | solution.py:107
  116.1 0.1 copy_bitcast_fusion
  116.3 1.7 gather_fusion.2
  118.0 3.0 %fusion.53 = f32[16,128,128,1]{1,2,3,0:T(8,128)} fusion(bf16[128,16,2,128]{3,0,2,1:T(8,128)(2,1)} %bitcast.100, bf16[16,2,128,128]{3,2,1,0:T(8,128)(2,1)} %param.26), kind=kOutput, calls=%fused_computation.81 | convolution fusion | flops 134217728 | bytes 3145728 | tf_op jit(solution)/shard_map/hnkj,nkji->hni/dot_general | solution.py:111
  121.0 2.6 copy.87
  123.5 1.3 add_convert_fusion
  124.9 0.3 copy.71
  125.1 6.2 %gather_fusion.3 = bf16[2048,128]{1,0:T(8,128)(2,1)S(1)} fusion(bf16[128,2048]{0,1:T(8,128)(2,1)S(1)} %copy.71, s32[2048]{0:T(1024)S(1)} %fusion.42), kind=kCustom, calls=%fused_computation.3 | custom fusion | bytes 1056768 | tf_op jit(solution)/shard_map/jit(_take)/gather | solution.py:117
  131.3 0.2 copy.72
  131.5 0.1 bitcast_select_fusion
  131.6 3.1 %pad_maximum_fusion = bf16[4,128,2048]{2,1,0:T(8,128)(2,1)} fusion(bf16[1,128,2048]{2,1,0:T(8,128)(2,1)S(1)} %bitcast_select_fusion, bf16[1,128,2048]{2,1,0:T(8,128)(2,1)} %get-tuple-element.25, bf16[1,128,2048]{2,1,0:T(8,128)(2,1)} %get-tuple-element.24, bf16[1,128,2048]{2,1,0:T(8,128)(2,1)} %fusion.66), kind=kLoop, calls=%fused_computation.19 | loop fusion | flops 3145728 | bytes 4194304 | tf_op jit(solution)/shard_map/stack | solution.py:118
  134.7 0.0 all-gather.2.cloned.1.call-update
  134.7 0.7 copy-done.11
  135.4 0.0 copy-done.14
  135.4 2.4 convolution_add_fusion
  137.8 146.8 %all-gather.2.cloned.1.call-done = bf16[4,512,2048]{2,1,0:T(8,128)(2,1)} async-done(((bf16[4,128,2048]{2,1,0:T(8,128)(2,1)}), bf16[4,512,2048]{2,1,0:T(8,128)(2,1)}) %all-gather.2.cloned.1.call-update) | async-done | bytes 8388624 | tf_op jit(solution)/shard_map/all_gather | solution.py:122
  284.5 6.4 %fusion.8 = f32[3,128,2048]{2,1,0:T(8,128)S(1)} fusion(bf16[4,512,2048]{2,1,0:T(8,128)(2,1)} %all-gather.2.cloned.1.call-done, bf16[3,128,4,512]{3,2,1,0:T(4,128)(2,1)} %param.20), kind=kOutput, calls=%fused_computation.17 | convolution fusion | flops 3221225472 | bytes 13107200 | tf_op jit(solution)/shard_map/ghkc,kcr->ghr/dot_general | solution.py:119
  291.0 1.5 fusion.22
  (44 shorter events, 0.2 us)
Async XLA Ops:
  6.5 27.6 %copy-start = (bf16[16,4,128,128]{3,2,1,0:T(8,128)(2,1)S(1)}, bf16[16,4,128,128]{3,2,1,0:T(8,128)(2,1)}, u32[]{:S(2)}) copy-start(bf16[16,4,128,128]{3,2,1,0:T(8,128)(2,1)} %param.16) | copy-start | bytes 6291460
  6.5 45.8 %reduce-scatter.7.cloned.1.call-start = ((), (), s32[]{:S(2)}) async-start(), calls=%async_computation.4 | async-start | bytes 589824
  8.5 20.8 %collective-permute-start = (bf16[128,128]{1,0:T(8,128)(2,1)S(1)}, bf16[128,128]{1,0:T(8,128)(2,1)S(1)}, u32[]{:S(2)}, u32[]{:S(2)}) collective-permute-start(bf16[128,128]{1,0:T(8,128)(2,1)S(1)} %get-tuple-element.20), channel_id=1, source_target_pairs={{0,4},{4,8},{8,12},{12,16},{16,20},{20,24},{24,28},{28,0},{1,5},{5... | collective-permute-start | bytes 98312 | tf_op jit(solution)/shard_map/ppermute | solution.py:16
  9.0 20.4 %collective-permute-start.1 = (bf16[128,128]{1,0:T(8,128)(2,1)S(1)}, bf16[128,128]{1,0:T(8,128)(2,1)S(1)}, u32[]{:S(2)}, u32[]{:S(2)}) collective-permute-start(bf16[128,128]{1,0:T(8,128)(2,1)S(1)} %get-tuple-element.22), channel_id=1, source_target_pairs={{4,0},{8,4},{12,8},{16,12},{20,16},{24,20},{28,24},{0,28},{5,1},{9... | collective-permute-start | bytes 98312 | tf_op jit(solution)/shard_map/ppermute | solution.py:17
  12.0 5.1 %copy-start.10 = (s32[2048]{0:T(1024)S(1)}, s32[2048]{0:T(1024)}, u32[]{:S(2)}) copy-start(s32[2048]{0:T(1024)} %param.19) | copy-start | bytes 24580
  17.0 4.9 %copy-start.2 = (bf16[128,2048]{1,0:T(8,128)(2,1)S(1)}, bf16[128,2048]{1,0:T(8,128)(2,1)}, u32[]{:S(2)}) copy-start(bf16[128,2048]{1,0:T(8,128)(2,1)} %param.14) | copy-start | bytes 1572868
  17.0 5.8 %copy-start.12 = (s32[16,4]{0,1:T(4,128)S(1)}, s32[16,4]{0,1:T(4,128)}, u32[]{:S(2)}) copy-start(s32[16,4]{0,1:T(4,128)} %param.17) | copy-start | bytes 772
  17.0 6.7 %copy-start.7 = (f32[2,10,2048]{2,0,1:T(2,128)S(1)}, f32[2,10,2048]{2,0,1:T(2,128)}, u32[]{:S(2)}) copy-start(f32[2,10,2048]{2,0,1:T(2,128)} %param.25) | copy-start | bytes 491524
  17.0 72.9 %reduce-scatter.5.cloned.1.call-start = ((), (), s32[]{:S(2)}) async-start(), calls=%async_computation.2 | async-start | bytes 589824 | tf_op jit(solution)/shard_map/reduce_scatter | solution.py:91
  21.6 262.9 %all-gather.2.cloned.1.call-start = ((), (), s32[]{:S(2)}) async-start(), calls=%async_computation.3 | async-start | bytes 10485760 | tf_op jit(solution)/shard_map/all_gather | solution.py:122
  27.2 2.0 copy-start.5
  27.2 2.0 copy-start.15
  39.1 0.8 copy-start.6
  40.0 14.6 %collective-permute-start.2 = (bf16[128,128]{1,0:T(8,128)(2,1)S(1)}, bf16[128,128]{1,0:T(8,128)(2,1)S(1)}, u32[]{:S(2)}, u32[]{:S(2)}) collective-permute-start(bf16[128,128]{1,0:T(8,128)(2,1)S(1)} %get-tuple-element.13), channel_id=1, source_target_pairs={{0,4},{4,8},{8,12},{12,16},{16,20},{20,24},{24,28},{28,0},{1,5},{5... | collective-permute-start | bytes 98312 | tf_op jit(solution)/shard_map/ppermute | solution.py:16
  40.0 14.6 %collective-permute-start.3 = (bf16[128,128]{1,0:T(8,128)(2,1)S(1)}, bf16[128,128]{1,0:T(8,128)(2,1)S(1)}, u32[]{:S(2)}, u32[]{:S(2)}) collective-permute-start(bf16[128,128]{1,0:T(8,128)(2,1)S(1)} %get-tuple-element.14), channel_id=1, source_target_pairs={{4,0},{8,4},{12,8},{16,12},{20,16},{24,20},{28,24},{0,28},{5,1},{9... | collective-permute-start | bytes 98312 | tf_op jit(solution)/shard_map/ppermute | solution.py:17
  61.9 2.6 copy-start.4
  64.5 26.2 %copy-start.9 = (bf16[2,64,64]{2,1,0:T(8,128)(2,1)S(1)}, bf16[2,64,64]{2,1,0:T(8,128)(2,1)}, u32[]{:S(2)}) copy-start(bf16[2,64,64]{2,1,0:T(8,128)(2,1)} %param.23) | copy-start | bytes 49156
  101.8 3.7 %copy-start.8 = (bf16[128,256]{1,0:T(8,128)(2,1)S(1)}, bf16[128,256]{1,0:T(8,128)(2,1)}, u32[]{:S(2)}) copy-start(bf16[128,256]{1,0:T(8,128)(2,1)} %reduce-scatter.5.cloned.1.call-done) | copy-start | bytes 196612
  134.7 0.7 copy-start.11
  134.7 0.7 copy-start.13
  134.7 0.7 copy-start.14
  137.8 153.2 %copy-start.3 = (bf16[128,2048]{1,0:T(8,128)(2,1)S(1)}, bf16[128,2048]{1,0:T(8,128)(2,1)}, u32[]{:S(2)}) copy-start(bf16[128,2048]{1,0:T(8,128)(2,1)} %param.14) | copy-start | bytes 1572868
  284.5 6.5 %copy-start.1 = (f32[3,128,2048]{2,1,0:T(8,128)S(1)}, f32[3,128,2048]{2,1,0:T(8,128)}, u32[]{:S(2)}) copy-start(f32[3,128,2048]{2,1,0:T(8,128)} %convolution_add_fusion) | copy-start | bytes 9437188
Sparse Core Ops, SparseCore 0:
  17.1 35.1 reduce-scatter.6
  55.7 34.1 reduce-scatter.4
  134.8 149.6 all-gather.1
where the time goes:
time: 300 us; the launch traced here: 299 us
  waiting for transfers between devices  179 us (60%)
  matrix products  33.2 us (11%)
  local copies, waits for them, and re-layouts  27.7 us (9%)
  blocking collectives  21.4 us (7%)
  other arithmetic  16.7 us (6%)
  between operations  14.2 us (5%)
  starting transfers between devices  6.41 us (2%)
    all_gather x1, waiting for transfers between devices, body(): lax.all_gather(features, 'feat', axis=1, tiled=True)  147 us
    reduce_scatter x1, waiting for transfers between devices, body(): lax.psum_scatter(cluster_sums.astype(jnp.bfloat16), 'dom', scatter_dimens...  23 us
    all_gather x1, blocking collectives, body(): all_values = lax.all_gather(own_values, 'dom', axis=2, tiled=True)  10.8 us
    all_gather x1, blocking collectives, body(): coarse_attn = lax.all_gather(own_coarse, 'dom', axis=1, tiled=True)  10.6 us
    unnamed x4, waiting for transfers between devices  9.72 us
    dot_general x1, matrix products, body(): jnp.einsum('ghkc,kcr->ghr', w_gates, lax.all_gather(features, 'feat', axi...  6.45 us
    gather x2, local copies, waits for them, and re-layouts, body(): unpooled = jnp.take(coarse, cluster_of, axis=1)  6.4 us
  transfers between devices with their start and end apart: 7, of which 3 were waited for; matrix products, arithmetic and copies ran while one was open for 14% of the time, Pallas kernels for 0%

commit v1 on v0

v1 whole, which is shorter than its diff:
```python
import functools

import jax
import jax.numpy as jnp
from jax import lax
from jax.experimental import pallas as pl
from jax.experimental.pallas import tpu as pltpu
from jax.sharding import PartitionSpec as P

BF = jnp.bfloat16
F32 = jnp.float32
VMEM = pl.BlockSpec(memory_space=pltpu.VMEM)
SMEM = pl.BlockSpec(memory_space=pltpu.SMEM)
COUNT_ROWS = 16


def call(kernel, outs, ins, scratch=(), flops=0, bytes_accessed=0, mib=40):
    specs = [SMEM if x.dtype == jnp.int32 and x.ndim == 1 else VMEM for x in ins]
    return pl.pallas_call(
        kernel,
        out_shape=outs,
        in_specs=specs,
        out_specs=jax.tree.map(lambda _: VMEM, outs),
        scratch_shapes=list(scratch),
        compiler_params=pltpu.CompilerParams(vmem_limit_bytes=mib * 2**20),
        cost_estimate=pl.CostEstimate(
            flops=int(flops), bytes_accessed=int(bytes_accessed), transcendentals=0
        ),
    )(*ins)


def one_hot(ids, first, width):
    rel = jnp.clip(ids - first, -1, width).astype(F32).astype(BF)
    rows = lax.broadcasted_iota(jnp.int32, (width, ids.shape[1]), 0).astype(F32).astype(BF)
    return jnp.where(rel == rows, jnp.ones((), BF), jnp.zeros((), BF))


def sums_kernel(share, meta, state, ids, *outs_and_scratch):
    *outs, lhs = outs_and_scratch
    channels, sensors = state.shape
    lhs[:channels] = state[...]
    lhs[channels:] = jnp.ones((COUNT_ROWS, sensors), BF)
    position = lax.broadcasted_iota(jnp.int32, (1, sensors), 1)
    own = jnp.where(position < meta[1], ids[...], -1)
    for b, out in enumerate(outs):
        hot = one_hot(own, (meta[0] ^ b) * share, share)
        sums = lax.dot_general(lhs[...], hot, (((1,), (1,)), ((), ())), preferred_element_type=F32)
        out[:channels] = sums[:channels].astype(BF)
        counts = sums[channels:]
        high = jnp.floor(counts * (1.0 / 256.0))
        row = lax.broadcasted_iota(jnp.int32, counts.shape, 0)
        out[channels:] = jnp.where(row == 0, high, counts - 256.0 * high).astype(BF)


def split3(x):
    high = x.astype(BF)
    rest = x - high.astype(F32)
    mid = rest.astype(BF)
    return high, mid, (rest - mid.astype(F32)).astype(BF)


def pool_kernel(pieces, w_value, *refs):
    blocks, (pooled, values) = refs[:pieces], refs[pieces:]
    channels = pooled.shape[0]
    total = blocks[0][...].astype(F32)
    for ref in blocks[1:]:
        total = total + ref[...].astype(F32)
    counts = 256.0 * total[channels : channels + 1] + total[channels + 1 : channels + 2]
    mean = total[:channels] / jnp.maximum(counts, 1.0)
    pooled[...] = mean
    heads, size = w_value.shape[0], w_value.shape[1]
    for h in range(heads):
        out = jnp.zeros((size, mean.shape[1]), F32)
        for part in split3(mean[h * size : (h + 1) * size]):
            out = out + jnp.dot(w_value[h], part, preferred_element_type=F32)
        values[h * size : (h + 1) * size] = out.astype(BF)


def weights_kernel(share, source, target, weights):
    heads, _, clusters = target.shape
    for h in range(heads):
        s_hi, s_mid, s_lo = split3(source[h])
        t_hi, t_mid, t_lo = split3(target[h])
        left = jnp.concatenate([t_hi, t_hi, t_mid, t_hi, t_lo, t_mid], axis=0)
        right = jnp.concatenate([s_hi, s_mid, s_hi, s_lo, s_hi, s_mid], axis=0)
        scores = lax.dot_general(left, right, (((0,), (0,)), ((), ())), preferred_element_type=F32)
        scores = jnp.maximum(scores, 0.0)
        raised = jnp.exp(scores - jnp.max(scores, axis=0, keepdims=True))
        scale = 1.0 / jnp.sum(raised, axis=0, keepdims=True)
        weights[h] = (raised * scale).astype(BF)


def attend_kernel(values, weights, pooled, out):
    heads, _, share = weights.shape
    parts, channels, _ = values.shape
    size = channels // heads
    for h in range(heads):
        rows = slice(h * size, (h + 1) * size)
        every = jnp.concatenate([values[p, rows] for p in range(parts)], axis=1)
        attended = jnp.dot(every, weights[h], preferred_element_type=F32)
        out[rows] = (pooled[rows] + attended).astype(BF)


def fold_kernel(blocks, *refs):
    parts, (w, out) = refs[:blocks], refs[blocks:]
    coarse = jnp.concatenate([r[...] for r in parts], axis=0)
    out[...] = jnp.dot(w[...], coarse, preferred_element_type=F32).astype(BF)


def hop_kernel(blocks, tile, meta, cols, *refs):
    parts = refs[:blocks]
    left, right, adj, adj_left, adj_right, w, out, ext, one, two = refs[blocks:]
    channels, rows = parts[0].shape
    total = channels * blocks
    tiles = rows // tile
    position = lax.broadcasted_iota(jnp.int32, (1, rows), 1)
    keep = position < meta[1]
    ext[:, : 2 * tile] = left[...]
    ext[:, 2 * tile + rows :] = right[...]
    for k, part in enumerate(parts):
        ext[k * channels : (k + 1) * channels, 2 * tile : 2 * tile + rows] = jnp.where(
            keep, part[...], jnp.zeros((), BF)
        )

    def pick(ref, at):
        return jnp.concatenate(
            [ref[:, pl.ds(pl.multiple_of(a * tile, tile), tile)] for a in at], axis=1
        )

    kb = adj.shape[1]
    stack = lambda a: a.reshape(kb * tile, tile)
    first = pick(ext, [cols[tiles * kb + k] for k in range(kb)])
    one[:, :tile] = jnp.dot(first, stack(adj_left[...]), preferred_element_type=F32).astype(BF)
    last = pick(ext, [cols[tiles * kb + kb + k] + tiles + 1 for k in range(kb)])
    one[:, (tiles + 1) * tile :] = jnp.dot(
        last, stack(adj_right[...]), preferred_element_type=F32
    ).astype(BF)

    def hop(source, shift, target, t):
        picked = pick(source, [cols[t * kb + k] + shift for k in range(kb)])
        made = jnp.dot(picked, stack(adj[t]), preferred_element_type=F32)
        spot = lax.broadcasted_iota(jnp.int32, (1, tile), 1) + t * tile
        return jnp.where(spot < meta[1], made, 0.0).astype(BF)

    def step_one(t, _):
        one[:, pl.ds(pl.multiple_of((t + 1) * tile, tile), tile)] = hop(ext, 1, one, t)
        return 0

    lax.fori_loop(0, tiles, step_one, 0, unroll=2)

    def step_two(t, _):
        two[:, pl.ds(pl.multiple_of(t * tile, tile), tile)] = hop(one, 0, two, t)
        return 0

    lax.fori_loop(0, tiles, step_two, 0, unroll=2)
    width = 2 * tile

    def gates(c, _):
        at = lambda s: pl.ds(pl.multiple_of(c * width + s, tile), width)
        acc = jnp.dot(w[0], ext[:, at(2 * tile)], preferred_element_type=F32)
        acc = acc + jnp.dot(w[1], one[:, at(tile)], preferred_element_type=F32)
        acc = acc + jnp.dot(w[2], two[:, at(0)], preferred_element_type=F32)
        out[:, at(0)] = acc
        return 0

    lax.fori_loop(0, rows // width, gates, 0)


def final_kernel(places, n_given, share, tile, meta, ccols, *refs):
    given = refs[:n_given]
    ctiles, ids, partial, terms, inputs, state, out, coarse, mixed = refs[n_given:]
    outputs = coarse.shape[0]
    clusters = coarse.shape[1]
    for ref, src, dst, rows, b, absolute in places:
        owner = b if absolute else meta[0] ^ b
        at = pl.ds(pl.multiple_of(owner * share, share), share)
        coarse[dst : dst + rows, at] = given[ref][src : src + rows]
    kc = ctiles.shape[1]

    def mix(t, _):
        picked = jnp.concatenate(
            [
                coarse[:, pl.ds(pl.multiple_of(ccols[t * kc + k] * tile, tile), tile)]
                for k in range(kc)
            ],
            axis=1,
        )
        at = pl.ds(pl.multiple_of(t * tile, tile), tile)
        made = jnp.dot(picked, ctiles[t].reshape(kc * tile, tile), preferred_element_type=F32)
        mixed[:, at] = (coarse[:, at].astype(F32) + made).astype(BF)
        return 0

    lax.fori_loop(0, clusters // tile, mix, 0, unroll=2)
    sensors = state.shape[1]
    channels = state.shape[0]
    width = 2 * tile

    def step(c, _):
        at = pl.ds(pl.multiple_of(c * width, width), width)
        own = ids[:, at]
        hot = jnp.concatenate(
            [one_hot(own, f, share) for f in range(0, clusters, share)], axis=0
        )
        sums = partial[:, at] + jnp.dot(mixed[...], hot, preferred_element_type=F32)
        x = inputs[:, at].astype(F32)
        given_terms = terms[:, 2:3] + terms[:, 0:1] * x[0:1] + terms[:, 1:2] * x[1:2]
        update = jax.nn.sigmoid(given_terms[:channels] + sums[:channels])
        reset = jax.nn.sigmoid(
            given_terms[channels : 2 * channels] + sums[channels : 2 * channels]
        )
        candidate = jnp.tanh(given_terms[2 * channels :] + reset * sums[2 * channels :])
        old = state[:, at].astype(F32)
        spot = lax.broadcasted_iota(jnp.int32, (1, width), 1) + c * width
        new = update * old + (1.0 - update) * candidate
        out[:, at] = jnp.where(spot < meta[1], new, 0.0).astype(BF)
        return 0

    lax.fori_loop(0, sensors // width, step, 0)


def flip(n, b):
    return [(i, i ^ b) for i in range(n)]


def shifts(array, axis):
    n = lax.axis_size(axis)
    return [array] + [
        lax.ppermute(array, axis, [((i + k) % n, i) for i in range(n)]) for k in range(1, n)
    ]


def gather_dom(block):
    n = lax.axis_size("dom")
    rows = block.shape[0]
    send = lambda x, b: lax.ppermute(x, "dom", flip(n, b))
    if n != 8:
        every = lax.all_gather(block, "dom", axis=0, tiled=True)
        return [every], [(0, b * rows, 0, rows, b, True) for b in range(n)]
    half = rows // 2
    beside = send(block, 2)
    behind = send(block, 4)
    core = send(block, 1)
    top = send(beside[:half], 4)
    bottom = send(behind[half:], 2)
    other = send(jnp.concatenate([beside, behind, top, bottom], axis=0), 1)
    places = [
        (0, 0, 0, rows, 0, False),
        (1, 0, 0, rows, 1, False),
        (2, 0, 0, rows, 2, False),
        (3, 0, 0, rows, 4, False),
        (4, 0, 0, half, 6, False),
        (5, 0, half, half, 6, False),
        (6, 0, 0, rows, 3, False),
        (6, rows, 0, rows, 5, False),
        (6, 2 * rows, 0, rows, 7, False),
    ]
    return [block, core, beside, behind, top, bottom, other], places


def body(
    state,
    inputs,
    adj_tiles,
    adj_cols,
    valid_rows,
    cluster_of,
    w_gates,
    w_input,
    bias,
    w_value,
    source_emb,
    target_emb,
    coarse_tiles,
    coarse_cols,
):
    channels, rows = state.shape
    clusters = source_emb.shape[2]
    n_dom, n_feat = lax.axis_size("dom"), lax.axis_size("feat")
    share = clusters // n_dom
    tiles, kb, tile, _ = adj_tiles.shape
    me, feat = lax.axis_index("dom"), lax.axis_index("feat")
    meta = jnp.stack([me.astype(jnp.int32), valid_rows[0]])
    ids = cluster_of[None, :]
    total = channels * n_feat
    outputs = 3 * channels
    sds = jax.ShapeDtypeStruct

    blocks = shifts(state, "feat")

    pieces = call(
        functools.partial(sums_kernel, share),
        [sds((channels + COUNT_ROWS, share), BF)] * n_dom,
        [meta, state, ids],
        [pltpu.VMEM((channels + COUNT_ROWS, rows), BF)],
        flops=2 * channels * rows * clusters * 3,
        bytes_accessed=8 * channels * rows,
    )
    arrived = [pieces[0]] + [lax.ppermute(pieces[b], "dom", flip(n_dom, b)) for b in range(1, n_dom)]
    pooled, values = call(
        functools.partial(pool_kernel, n_dom),
        [sds((channels, share), F32), sds((channels, share), BF)],
        [w_value] + arrived,
    )
    pad = [(0, 0), (0, -source_emb.shape[1] % 16), (0, 0)]
    source = lax.dynamic_slice_in_dim(source_emb, me * share, share, 2)
    weights = call(
        functools.partial(weights_kernel, share),
        sds((source.shape[0], clusters, share), BF),
        [jnp.pad(source, pad), jnp.pad(target_emb, pad)],
        flops=source.shape[0] * clusters * share * 4000,
    )
    every_value = lax.all_gather(values, "dom", axis=0)
    own_coarse = call(attend_kernel, sds((channels, share), BF), [every_value, weights, pooled])
    coarse_blocks = shifts(own_coarse, "feat")

    w = jnp.transpose(w_gates, (2, 0, 1, 3)).reshape(4, outputs, total)
    w = lax.dynamic_slice_in_dim(jnp.concatenate([w, w], axis=2), feat * channels, total, 2)
    folded = call(
        functools.partial(fold_kernel, n_feat),
        sds((outputs, share), BF),
        coarse_blocks + [w[3]],
    )
    given, places = gather_dom(folded)

    up = [(i, (i + 1) % n_dom) for i in range(n_dom)]
    down = [(j, i) for i, j in up]
    spot = jnp.arange(rows, dtype=jnp.int32)
    keep = (spot < valid_rows[0]).astype(BF)

    def edge(t):
        made = adj_tiles[t] * keep[t * tile : (t + 1) * tile]
        offsets = (adj_cols[t] - t).astype(BF)
        offsets = jnp.broadcast_to(offsets[:, None, None], (kb, 16, tile))
        return jnp.concatenate([made, offsets], axis=1)

    from_left = lax.ppermute(edge(tiles - 1), "dom", up)
    from_right = lax.ppermute(edge(0), "dom", down)
    cols = jnp.concatenate(
        [
            adj_cols.reshape(-1),
            from_left[:, tile, 0].astype(jnp.int32),
            from_right[:, tile, 0].astype(jnp.int32),
        ]
    )
    tail = jnp.concatenate([x[:, rows - 2 * tile :] for x in blocks], axis=0)
    head = jnp.concatenate([x[:, : 2 * tile] for x in blocks], axis=0)
    left = lax.ppermute(tail * keep[rows - 2 * tile :], "dom", up)
    right = lax.ppermute(head * keep[: 2 * tile], "dom", down)
    partial = call(
        functools.partial(hop_kernel, n_feat, tile),
        sds((outputs, rows), F32),
        [meta, cols]
        + blocks
        + [left, right, adj_tiles, from_left[:, :tile], from_right[:, :tile], w[:3]],
        [
            pltpu.VMEM((total, rows + 4 * tile), BF),
            pltpu.VMEM((total, rows + 2 * tile), BF),
            pltpu.VMEM((total, rows), BF),
        ],
        flops=2 * total * rows * (4 * kb * tile + 3 * outputs),
        bytes_accessed=8 * total * rows,
    )

    terms = jnp.concatenate(
        [w_input.reshape(outputs, -1).astype(F32), bias.reshape(outputs, 1)], axis=1
    )
    return call(
        functools.partial(final_kernel, places, len(given), share, tile),
        sds((channels, rows), BF),
        [meta, coarse_cols.reshape(-1)]
        + given
        + [coarse_tiles, ids, partial, terms, inputs, state],
        [pltpu.VMEM((outputs, clusters), BF)] * 2,
        flops=2 * outputs * rows * clusters,
        bytes_accessed=8 * outputs * rows,
    )


def solution(mesh):
    return jax.shard_map(
        body,
        mesh=mesh,
        in_specs=(
            P("feat", "dom"),
            P(None, "dom"),
            P("dom", None, None, None),
            P("dom", None),
            P("dom"),
            P("dom"),
            P(None, "feat", None, None),
            P(None, "feat", None),
            P(None, "feat"),
            P("feat", None, None),
            P("feat", None, None),
            P("feat", None, None),
            P(),
            P(),
        ),
        out_specs=P("feat", "dom"),
        check_vma=False,
    )
```

time: 300 us -> 120 us (0.40)
  waiting for transfers between devices: 179 us -> 34.8 us
  matrix products: 33.2 us -> 0 us
  Pallas kernels: 0 us -> 28.6 us
  starting transfers between devices: 6.41 us -> 29.2 us
  local copies, waits for them, and re-layouts: 27.7 us -> 10.9 us
  between operations: 14.2 us -> 1.15 us
  blocking collectives: 21.4 us -> 8.85 us
  other arithmetic: 16.7 us -> 5.89 us
    all_gather x1 -> x0, waiting for transfers between devices: 147 us -> none  [body(): lax.all_gather(features, 'feat', axis=1, tiled=True)]
    ppermute x4 -> x23, waiting for transfers between devices: 0.01 us -> 34.8 us  [the longest x6 30.1 us: shifts(): lax.ppermute(array, axis, [((i + k) % n, i) for i in range(n)])]
    dot_general x10 -> x0, matrix products: 33.2 us -> none  [the longest x1 6.45 us: body(): jnp.einsum('ghkc,kcr->ghr', w_gates, lax.all_gather(features, 'feat', axi...]
    pallas_call x0 -> x7, Pallas kernels: none -> 28.6 us  [call(): pl.pallas_call(kernel, out_shape=outs, in_specs=specs, out_specs=jax.tree...]
    ppermute x4 -> x23, starting transfers between devices: 6.14 us -> 29.2 us  [the longest x6 12.5 us: shifts(): lax.ppermute(array, axis, [((i + k) % n, i) for i in range(n)])]
    reduce_scatter x1 -> x0, waiting for transfers between devices: 23 us -> none  [body(): lax.psum_scatter(cluster_sums.astype(jnp.bfloat16), 'dom', scatter_dimens...]
    all_gather x2 -> x1, blocking collectives: 21.4 us -> 8.85 us  [body(): every_value = lax.all_gather(values, 'dom', axis=0)]
    gather x5 -> x0, local copies, waits for them, and re-layouts: 12.4 us -> none  [the longest x2 6.4 us: body(): unpooled = jnp.take(coarse, cluster_of, axis=1)]
  transfers between devices with their start and end apart: 7 -> 23, of which waited for: 3 -> 5; matrix products, arithmetic and copies ran while one was open for 14% -> 12% of each run, Pallas kernels for 0% -> 14%
where the time goes in v1:
time: 120 us; the launch traced here: 119 us
  waiting for transfers between devices  34.8 us (29%)
  starting transfers between devices  29.2 us (24%)
  Pallas kernels  28.6 us (24%)
  local copies, waits for them, and re-layouts  10.9 us (9%)
  blocking collectives  8.85 us (7%)
  other arithmetic  5.89 us (5%)
    ppermute x6, waiting for transfers between devices, shifts(): lax.ppermute(array, axis, [((i + k) % n, i) for i in range(n)])  30.1 us
    pallas_call x7, Pallas kernels, call(): pl.pallas_call(kernel, out_shape=outs, in_specs=specs, out_specs=jax.tree...  28.6 us
    ppermute x6, starting transfers between devices, shifts(): lax.ppermute(array, axis, [((i + k) % n, i) for i in range(n)])  12.5 us
    all_gather x1, blocking collectives, body(): every_value = lax.all_gather(values, 'dom', axis=0)  8.85 us
    ppermute x7, starting transfers between devices, body(): lax.ppermute(pieces[b], 'dom', flip(n_dom, b))  7.72 us
    ppermute x1, waiting for transfers between devices, body(): left = lax.ppermute(tail * keep[rows - 2 * tile:], 'dom', up)  4.63 us
    ppermute x6, starting transfers between devices, gather_dom(): send = lambda x, b: lax.ppermute(x, 'dom', flip(n, b))  4.39 us
    unnamed x35, local copies, waits for them, and re-layouts  3.25 us
  transfers between devices with their start and end apart: 23, of which 5 were waited for; matrix products, arithmetic and copies ran while one was open for 12% of the time, Pallas kernels for 14%

profile of v1, /device:TPU:0, one launch (start us, length us, event | category | flops | bytes accessed | tf_op | source)
XLA Modules:
  0.0 119.4 jit_solution(8860978144321360809)
XLA Ops:
  0.7 0.1 pad_add_fusion.meta
  0.8 1.0 copy-done.3
  1.8 0.7 copy-done.6
  2.5 3.4 %shard_map.136 = (bf16[144,256]{1,0:T(8,128)(2,1)S(1)}, bf16[144,256]{1,0:T(8,128)(2,1)S(1)}, bf16[144,256]{1,0:T(8,128)(2,1)S(1)}, bf16[144,256]{1,0:T(8,128)(2...) custom-call(s32[2]{0:T(128)S(1)} %pad_add_fusion.meta, ...), custom_call_target="tpu_custom_call" | custom-call | flops 3221225472 | bytes 2097152 | tf_op jit(solution)/shard_map/pallas_call | solution.py:19
  5.9 0.5 collective-permute-start
  6.4 2.6 %collective-permute-start.1 = (bf16[144,256]{1,0:T(8,128)(2,1)S(1)}, bf16[144,256]{1,0:T(8,128)(2,1)S(1)}, u32[]{:S(2)}, u32[]{:S(2)}) collective-permute-start(bf16[144,256]{1,0:T(8,128)(2,1)S(1)} %get-tuple-element.17), channel_id=1, source_target_pairs={{0,8},{4,12},{8,0},{12,4},{16,24},{20,28},{24,16},{28,20},{1,9},{5... | collective-permute-start | bytes 221192 | tf_op jit(solution)/shard_map/ppermute | solution.py:298
  9.0 0.1 collective-permute-start.2
  9.1 1.8 %collective-permute-start.3 = (bf16[144,256]{1,0:T(8,128)(2,1)S(1)}, bf16[144,256]{1,0:T(8,128)(2,1)S(1)}, u32[]{:S(2)}, u32[]{:S(2)}) collective-permute-start(bf16[144,256]{1,0:T(8,128)(2,1)S(1)} %get-tuple-element.19), channel_id=1, source_target_pairs={{0,16},{4,20},{8,24},{12,28},{16,0},{20,4},{24,8},{28,12},{1,17},{... | collective-permute-start | bytes 221192 | tf_op jit(solution)/shard_map/ppermute | solution.py:298
  10.9 0.1 slice_reduce_fusion
  11.1 0.1 copy.37
  11.3 2.9 %copy.38 = bf16[4,3,128,512]{3,2,1,0:T(8,128)(2,1)} copy(bf16[4,3,128,512]{3,0,2,1:T(4,128)(2,1)} %bitcast.26) | data formatting | bytes 3145728 | tf_op jit(solution)/shard_map/transpose | solution.py:316
  14.2 2.0 %fusion = bf16[4,384,512]{2,1,0:T(8,128)(2,1)S(1)} fusion(s32[]{:T(128)S(6)} %select_n.7, bf16[4,384,512]{2,1,0:T(8,128)(2,1)} %bitcast.25), kind=kLoop, calls=%fused_computation.2 | loop fusion | flops 3145728 | bytes 3145732 | tf_op jit(solution)/shard_map/concatenate | solution.py:317
  16.2 1.2 copy-done.9
  17.4 2.2 %shard_map.138.weights = bf16[2,2048,256]{2,1,0:T(8,128)(2,1)S(1)} custom-call(f32[2,16,256]{2,1,0:T(8,128)S(1)} %pad.8.source, f32[2,16,2048]{2,1,0:T(8,128)S(1)} %pad.9.target), custom_call_target="tpu_custom_call" | custom-call | flops 4194304000 | tf_op jit(solution)/shard_map/pallas_call | solution.py:19
  19.6 1.0 bitcast_multiply_fusion.1
  20.6 0.1 broadcast_in_dim.8
  20.7 2.7 %collective-permute-start.5 = (bf16[144,256]{1,0:T(8,128)(2,1)S(1)}, bf16[144,256]{1,0:T(8,128)(2,1)S(1)}, u32[]{:S(2)}, u32[]{:S(2)}) collective-permute-start(bf16[144,256]{1,0:T(8,128)(2,1)S(1)} %get-tuple-element.21), channel_id=1, source_target_pairs={{0,24},{4,28},{8,16},{12,20},{16,8},{20,12},{24,0},{28,4},{1,25},{... | collective-permute-start | bytes 221192 | tf_op jit(solution)/shard_map/ppermute | solution.py:298
  23.4 0.1 collective-permute-start.6
  23.5 0.2 fusion.4
  23.7 1.7 %collective-permute-start.20 = (bf16[128,2048]{1,0:T(8,128)(2,1)S(1)}, bf16[128,2048]{1,0:T(8,128)(2,1)S(1)}, u32[]{:S(2)}, u32[]{:S(2)}) collective-permute-start(bf16[128,2048]{1,0:T(8,128)(2,1)S(1)} %copy-done.4), channel_id=1, source_target_pairs={{3,0},{0,1},{1,2},{2,3},{7,4},{4,5},{5,6},{6,7},{11,8},{8,9},{9,10... | collective-permute-start | bytes 1572872 | tf_op jit(solution)/shard_map/ppermute | solution.py:228
  25.4 2.7 %collective-permute-start.19 = (bf16[128,2048]{1,0:T(8,128)(2,1)S(1)}, bf16[128,2048]{1,0:T(8,128)(2,1)}, u32[]{:S(2)}, u32[]{:S(2)}) collective-permute-start(bf16[128,2048]{1,0:T(8,128)(2,1)S(1)} %copy-done.4), channel_id=1, source_target_pairs={{2,0},{3,1},{0,2},{1,3},{6,4},{7,5},{4,6},{5,7},{10,8},{11,9},{8,1... | collective-permute-start | bytes 1572872 | tf_op jit(solution)/shard_map/ppermute | solution.py:228
  28.1 1.8 %collective-permute-start.17 = (bf16[4,144,128]{2,1,0:T(8,128)(2,1)S(1)}, bf16[4,144,128]{2,1,0:T(8,128)(2,1)}, u32[]{:S(2)}, u32[]{:S(2)}) collective-permute-start(bf16[4,144,128]{2,1,0:T(8,128)(2,1)S(1)} %pad_maximum_fusion.2), channel_id=1, source_target_pairs={{4,0},{8,4},{12,8},{16,12},{20,16},{24,20},{28,24},{0,28},{5,1},{9... | collective-permute-start | bytes 442376 | tf_op jit(solution)/shard_map/ppermute | solution.py:337
  29.9 0.3 shard_map.137
  30.2 8.8 %all-gather = bf16[1024,256]{1,0:T(8,128)(2,1)S(1)} all-gather(bf16[128,256]{1,0:T(8,128)(2,1)S(1)} %get-tuple-element.23), channel_id=2, replica_groups=mesh['dom'=8,'feat'=4] {'dom'}, dimensions={0}, use_global_device_ids=true | all-gather | bytes 589824 | tf_op jit(solution)/shard_map/all_gather | solution.py:312
  39.1 0.5 shard_map.139.refs_0_
  39.6 0.5 collective-permute-start.9
  40.1 2.6 %collective-permute-start.8 = (bf16[128,256]{1,0:T(8,128)(2,1)S(1)}, bf16[128,256]{1,0:T(8,128)(2,1)S(1)}, u32[]{:S(2)}, u32[]{:S(2)}) collective-permute-start(bf16[128,256]{1,0:T(8,128)(2,1)S(1)} %shard_map.139.refs_0_), channel_id=1, source_target_pairs={{2,0},{3,1},{0,2},{1,3},{6,4},{7,5},{4,6},{5,7},{10,8},{11,9},{8,1... | collective-permute-start | bytes 196616 | tf_op jit(solution)/shard_map/ppermute | solution.py:228
  42.7 0.1 broadcast_in_dim.7
  42.8 0.7 pad_maximum_fusion.1
  43.5 9.6 %collective-permute-done.9.refs_3_ = bf16[128,256]{1,0:T(8,128)(2,1)S(1)} collective-permute-done((bf16[128,256]{1,0:T(8,128)(2,1)S(1)}, bf16[128,256]{1,0:T(8,128)(2,1)S(1)}, u32[]{:S(2)}, u32[]{:S(2)}) %collective-permute-start.9) | collective-permute-done | bytes 65568 | tf_op jit(solution)/shard_map/ppermute | solution.py:228
  53.1 13.6 %collective-permute-done.8.refs_2_ = bf16[128,256]{1,0:T(8,128)(2,1)S(1)} collective-permute-done((bf16[128,256]{1,0:T(8,128)(2,1)S(1)}, bf16[128,256]{1,0:T(8,128)(2,1)S(1)}, u32[]{:S(2)}, u32[]{:S(2)}) %collective-permute-start.8) | collective-permute-done | bytes 65568 | tf_op jit(solution)/shard_map/ppermute | solution.py:228
  66.6 1.6 %collective-permute-start.7 = (bf16[128,256]{1,0:T(8,128)(2,1)S(1)}, bf16[128,256]{1,0:T(8,128)(2,1)S(1)}, u32[]{:S(2)}, u32[]{:S(2)}) collective-permute-start(bf16[128,256]{1,0:T(8,128)(2,1)S(1)} %shard_map.139.refs_0_), channel_id=1, source_target_pairs={{1,0},{2,1},{3,2},{0,3},{5,4},{6,5},{7,6},{4,7},{9,8},{10,9},{11,1... | collective-permute-start | bytes 196616 | tf_op jit(solution)/shard_map/ppermute | solution.py:228
  68.2 0.1 copy.39
  68.3 1.3 %slice.114.refs_9_ = bf16[3,384,512]{2,1,0:T(8,128)(2,1)S(1)} slice(bf16[4,384,512]{2,1,0:T(8,128)(2,1)} %copy-done.9), slice={[0:3], [0:384], [0:512]} | slice | bytes 2359296 | tf_op jit(solution)/shard_map/slice | solution.py:354
  69.7 0.1 copy.35
  69.7 0.1 reshape.38.ccols
  69.8 0.1 reshape.40
  69.9 0.1 copy.41.refs_10_
  70.1 0.8 collective-permute-done.7.refs_1_
  70.9 0.3 shard_map.140.refs_0_
  71.2 1.6 %collective-permute-start.12 = (bf16[384,256]{1,0:T(8,128)(2,1)S(1)}, bf16[384,256]{1,0:T(8,128)(2,1)S(1)}, u32[]{:S(2)}, u32[]{:S(2)}) collective-permute-start(bf16[384,256]{1,0:T(8,128)(2,1)S(1)} %shard_map.140.refs_0_), channel_id=1, source_target_pairs={{0,16},{4,20},{8,24},{12,28},{16,0},{20,4},{24,8},{28,12},{1,17},{... | collective-permute-start | bytes 589832 | tf_op jit(solution)/shard_map/ppermute | solution.py:235
  72.7 1.5 %collective-permute-start.11 = (bf16[384,256]{1,0:T(8,128)(2,1)S(1)}, bf16[384,256]{1,0:T(8,128)(2,1)S(1)}, u32[]{:S(2)}, u32[]{:S(2)}) collective-permute-start(bf16[384,256]{1,0:T(8,128)(2,1)S(1)} %shard_map.140.refs_0_), channel_id=1, source_target_pairs={{0,8},{4,12},{8,0},{12,4},{16,24},{20,28},{24,16},{28,20},{1,9},{5... | collective-permute-start | bytes 589832 | tf_op jit(solution)/shard_map/ppermute | solution.py:235
  74.2 0.9 fusion.2
  75.1 3.4 %collective-permute-start.18 = (bf16[128,2048]{1,0:T(8,128)(2,1)S(1)}, bf16[128,2048]{1,0:T(8,128)(2,1)S(1)}, u32[]{:S(2)}, u32[]{:S(2)}) collective-permute-start(bf16[128,2048]{1,0:T(8,128)(2,1)S(1)} %copy-done.4), channel_id=1, source_target_pairs={{1,0},{2,1},{3,2},{0,3},{5,4},{6,5},{7,6},{4,7},{9,8},{10,9},{11,1... | collective-permute-start | bytes 1572872 | tf_op jit(solution)/shard_map/ppermute | solution.py:228
  78.5 0.9 fusion.3
  79.4 0.1 collective-permute-start.10
  79.5 0.6 collective-permute-start.14
  80.1 0.6 collective-permute-start.13
  80.7 0.9 fusion.7
  81.6 0.0 copy-start.2
  81.6 6.1 %collective-permute-done.18.refs_1_ = bf16[128,2048]{1,0:T(8,128)(2,1)S(1)} collective-permute-done((bf16[128,2048]{1,0:T(8,128)(2,1)S(1)}, bf16[128,2048]{1,0:T(8,128)(2,1)S(1)}, u32[]{:S(2)}, u32[]{:S(2)}) %collective-permute-start.18) | collective-permute-done | bytes 524320 | tf_op jit(solution)/shard_map/ppermute | solution.py:228
  87.7 0.1 maximum_multiply_fusion
  87.8 0.1 collective-permute-start.21
  87.9 0.1 maximum_multiply_fusion.1
  87.9 2.7 %collective-permute-start.22 = (bf16[512,256]{1,0:T(8,128)(2,1)S(1)}, bf16[512,256]{1,0:T(8,128)(2,1)S(1)}, u32[]{:S(2)}, u32[]{:S(2)}) collective-permute-start(bf16[512,256]{1,0:T(8,128)(2,1)S(1)} %maximum_multiply_fusion.1), channel_id=1, source_target_pairs={{4,0},{8,4},{12,8},{16,12},{20,16},{24,20},{28,24},{0,28},{5,1},{9... | collective-permute-start | bytes 786440 | tf_op jit(solution)/shard_map/ppermute | solution.py:348
  90.6 0.1 pad_add_fusion.1.cols
  90.7 0.9 slice.113.refs_8_
  91.6 0.9 slice.112.refs_7_
  92.6 0.0 copy-start.7
  92.6 0.0 copy-start.8
  92.6 0.1 collective-permute-start.15
  92.7 4.6 %collective-permute-done.21.refs_4_ = bf16[512,256]{1,0:T(8,128)(2,1)S(1)} collective-permute-done((bf16[512,256]{1,0:T(8,128)(2,1)S(1)}, bf16[512,256]{1,0:T(8,128)(2,1)S(1)}, u32[]{:S(2)}, u32[]{:S(2)}) %collective-permute-start.21) | collective-permute-done | bytes 262176 | tf_op jit(solution)/shard_map/ppermute | solution.py:347
  97.3 13.0 %shard_map.141.refs_9_ = f32[384,2048]{1,0:T(8,128)S(1)} custom-call(s32[2]{0:T(128)S(1)} %pad_add_fusion.meta, s32[72]{0:T(128)S(1)} %pad_add_fusion.1.cols, bf16[128,2048]{1,0:T(8,128)(2,1)S(1)} %copy-done.4, bf16[128,2048]{1,0:T(8,128)(2,1)S(1)} %collective-permute-done.18.refs_1_, bf16[128,2048]{1,0:T(8,128)(2,1)} %collective-permute-done.19.refs_2_, ...), custom_call_target="tpu_custom_call" | custom-call | flops 6710886400 | bytes 8388608 | tf_op jit(solution)/shard_map/pallas_call | solution.py:19
  110.4 9.0 %shard_map.142 = bf16[128,2048]{1,0:T(8,128)(2,1)} custom-call(s32[2]{0:T(128)S(1)} %pad_add_fusion.meta, s32[32]{0:T(128)S(1)} %reshape.38.ccols, bf16[384,256]{1,0:T(8,128)(2,1)S(1)} %shard_map.140.refs_0_, bf16[384,256]{1,0:T(8,128)(2,1)S(1)} %collective-permute-done.10.refs_1_, bf16[384,256]{1,0:T(8,128)(2,1)S(1)} %collective-permute-done.11.refs_2_, ...), custom_call_target="tpu_custom_call" | custom-call | flops 3221225472 | bytes 6291456 | tf_op jit(solution)/shard_map/pallas_call | solution.py:19
  (63 shorter events, 0.3 us)
Async XLA Ops:
  0.0 11.1 %copy-start = (f32[2,10,2048]{2,0,1:T(2,128)S(1)}, f32[2,10,2048]{2,0,1:T(2,128)}, u32[]{:S(2)}) copy-start(f32[2,10,2048]{2,0,1:T(2,128)} %param.24) | copy-start | bytes 491524
  0.8 1.0 copy-start.3
  1.8 0.7 copy-start.6
  2.5 8.4 %copy-start.11 = (s32[16,4]{0,1:T(4,128)S(1)}, s32[16,4]{0,1:T(4,128)}, u32[]{:S(2)}) copy-start(s32[16,4]{0,1:T(4,128)} %param.17) | copy-start | bytes 772
  2.5 8.5 %copy-start.13 = (bf16[3,128,2]{1,2,0:T(2,128)(2,1)S(1)}, bf16[3,128,2]{1,2,0:T(2,128)(2,1)}, u32[]{:S(2)}) copy-start(bf16[3,128,2]{1,2,0:T(2,128)(2,1)} %param.21) | copy-start | bytes 4612
  2.5 8.6 %copy-start.10 = (f32[2,10,2048]{2,0,1:T(2,128)S(1)}, f32[2,10,2048]{2,0,1:T(2,128)}, u32[]{:S(2)}) copy-start(f32[2,10,2048]{2,0,1:T(2,128)} %param.25) | copy-start | bytes 491524
  5.9 14.8 %collective-permute-start = (bf16[144,256]{1,0:T(8,128)(2,1)S(1)}, bf16[144,256]{1,0:T(8,128)(2,1)S(1)}, u32[]{:S(2)}, u32[]{:S(2)}) collective-permute-start(bf16[144,256]{1,0:T(8,128)(2,1)S(1)} %get-tuple-element.16), channel_id=1, source_target_pairs={{0,4},{4,0},{8,12},{12,8},{16,20},{20,16},{24,28},{28,24},{1,5},{5... | collective-permute-start | bytes 221192 | tf_op jit(solution)/shard_map/ppermute | solution.py:298
  6.4 17.0 %collective-permute-start.1 = (bf16[144,256]{1,0:T(8,128)(2,1)S(1)}, bf16[144,256]{1,0:T(8,128)(2,1)S(1)}, u32[]{:S(2)}, u32[]{:S(2)}) collective-permute-start(bf16[144,256]{1,0:T(8,128)(2,1)S(1)} %get-tuple-element.17), channel_id=1, source_target_pairs={{0,8},{4,12},{8,0},{12,4},{16,24},{20,28},{24,16},{28,20},{1,9},{5... | collective-permute-start | bytes 221192 | tf_op jit(solution)/shard_map/ppermute | solution.py:298
  9.0 14.7 %collective-permute-start.2 = (bf16[144,256]{1,0:T(8,128)(2,1)S(1)}, bf16[144,256]{1,0:T(8,128)(2,1)S(1)}, u32[]{:S(2)}, u32[]{:S(2)}) collective-permute-start(bf16[144,256]{1,0:T(8,128)(2,1)S(1)} %get-tuple-element.18), channel_id=1, source_target_pairs={{0,12},{4,8},{8,4},{12,0},{16,28},{20,24},{24,20},{28,16},{1,13},{... | collective-permute-start | bytes 221192 | tf_op jit(solution)/shard_map/ppermute | solution.py:298
  9.1 16.4 %collective-permute-start.3 = (bf16[144,256]{1,0:T(8,128)(2,1)S(1)}, bf16[144,256]{1,0:T(8,128)(2,1)S(1)}, u32[]{:S(2)}, u32[]{:S(2)}) collective-permute-start(bf16[144,256]{1,0:T(8,128)(2,1)S(1)} %get-tuple-element.19), channel_id=1, source_target_pairs={{0,16},{4,20},{8,24},{12,28},{16,0},{20,4},{24,8},{28,12},{1,17},{... | collective-permute-start | bytes 221192 | tf_op jit(solution)/shard_map/ppermute | solution.py:298
  10.8 17.2 %collective-permute-start.4 = (bf16[144,256]{1,0:T(8,128)(2,1)S(1)}, bf16[144,256]{1,0:T(8,128)(2,1)S(1)}, u32[]{:S(2)}, u32[]{:S(2)}) collective-permute-start(bf16[144,256]{1,0:T(8,128)(2,1)S(1)} %get-tuple-element.20), channel_id=1, source_target_pairs={{0,20},{4,16},{8,28},{12,24},{16,4},{20,0},{24,12},{28,8},{1,21},{... | collective-permute-start | bytes 221192 | tf_op jit(solution)/shard_map/ppermute | solution.py:298
  16.2 1.2 copy-start.9
  17.4 6.4 %copy-start.4 = (bf16[128,2048]{1,0:T(8,128)(2,1)S(1)}, bf16[128,2048]{1,0:T(8,128)(2,1)}, u32[]{:S(2)}) copy-start(bf16[128,2048]{1,0:T(8,128)(2,1)} %refs_12_.1) | copy-start | bytes 1572868
  17.4 12.5 %copy-start.1 = (bf16[2,64,64]{2,1,0:T(8,128)(2,1)S(1)}, bf16[2,64,64]{2,1,0:T(8,128)(2,1)}, u32[]{:S(2)}) copy-start(bf16[2,64,64]{2,1,0:T(8,128)(2,1)} %w_value.1) | copy-start | bytes 49156
  20.7 9.2 %collective-permute-start.5 = (bf16[144,256]{1,0:T(8,128)(2,1)S(1)}, bf16[144,256]{1,0:T(8,128)(2,1)S(1)}, u32[]{:S(2)}, u32[]{:S(2)}) collective-permute-start(bf16[144,256]{1,0:T(8,128)(2,1)S(1)} %get-tuple-element.21), channel_id=1, source_target_pairs={{0,24},{4,28},{8,16},{12,20},{16,8},{20,12},{24,0},{28,4},{1,25},{... | collective-permute-start | bytes 221192 | tf_op jit(solution)/shard_map/ppermute | solution.py:298
  23.4 6.5 %collective-permute-start.6 = (bf16[144,256]{1,0:T(8,128)(2,1)S(1)}, bf16[144,256]{1,0:T(8,128)(2,1)S(1)}, u32[]{:S(2)}, u32[]{:S(2)}) collective-permute-start(bf16[144,256]{1,0:T(8,128)(2,1)S(1)} %get-tuple-element.22), channel_id=1, source_target_pairs={{0,28},{4,24},{8,20},{12,16},{16,12},{20,8},{24,4},{28,0},{1,29},{... | collective-permute-start | bytes 221192 | tf_op jit(solution)/shard_map/ppermute | solution.py:298
  23.7 56.4 %collective-permute-start.20 = (bf16[128,2048]{1,0:T(8,128)(2,1)S(1)}, bf16[128,2048]{1,0:T(8,128)(2,1)S(1)}, u32[]{:S(2)}, u32[]{:S(2)}) collective-permute-start(bf16[128,2048]{1,0:T(8,128)(2,1)S(1)} %copy-done.4), channel_id=1, source_target_pairs={{3,0},{0,1},{1,2},{2,3},{7,4},{4,5},{5,6},{6,7},{11,8},{8,9},{9,10... | collective-permute-start | bytes 1572872 | tf_op jit(solution)/shard_map/ppermute | solution.py:228
  25.4 55.3 %collective-permute-start.19 = (bf16[128,2048]{1,0:T(8,128)(2,1)S(1)}, bf16[128,2048]{1,0:T(8,128)(2,1)}, u32[]{:S(2)}, u32[]{:S(2)}) collective-permute-start(bf16[128,2048]{1,0:T(8,128)(2,1)S(1)} %copy-done.4), channel_id=1, source_target_pairs={{2,0},{3,1},{0,2},{1,3},{6,4},{7,5},{4,6},{5,7},{10,8},{11,9},{8,1... | collective-permute-start | bytes 1572872 | tf_op jit(solution)/shard_map/ppermute | solution.py:228
  28.1 44.7 %collective-permute-start.17 = (bf16[4,144,128]{2,1,0:T(8,128)(2,1)S(1)}, bf16[4,144,128]{2,1,0:T(8,128)(2,1)}, u32[]{:S(2)}, u32[]{:S(2)}) collective-permute-start(bf16[4,144,128]{2,1,0:T(8,128)(2,1)S(1)} %pad_maximum_fusion.2), channel_id=1, source_target_pairs={{4,0},{8,4},{12,8},{16,12},{20,16},{24,20},{28,24},{0,28},{5,1},{9... | collective-permute-start | bytes 442376 | tf_op jit(solution)/shard_map/ppermute | solution.py:337
  39.1 4.4 %copy-start.12 = (f32[3,128]{1,0:T(4,128)S(1)}, f32[3,128]{1,0:T(4,128)}, u32[]{:S(2)}) copy-start(f32[3,128]{1,0:T(4,128)} %param.22) | copy-start | bytes 4612
  39.6 30.1 %copy-start.14 = (s32[16,2]{0,1:T(2,128)S(1)}, s32[16,2]{0,1:T(2,128)}, u32[]{:S(2)}) copy-start(s32[16,2]{0,1:T(2,128)} %param.27) | copy-start | bytes 388
  39.6 13.5 %collective-permute-start.9 = (bf16[128,256]{1,0:T(8,128)(2,1)S(1)}, bf16[128,256]{1,0:T(8,128)(2,1)S(1)}, u32[]{:S(2)}, u32[]{:S(2)}) collective-permute-start(bf16[128,256]{1,0:T(8,128)(2,1)S(1)} %shard_map.139.refs_0_), channel_id=1, source_target_pairs={{3,0},{0,1},{1,2},{2,3},{7,4},{4,5},{5,6},{6,7},{11,8},{8,9},{9,10... | collective-permute-start | bytes 196616 | tf_op jit(solution)/shard_map/ppermute | solution.py:228
  40.1 26.6 %collective-permute-start.8 = (bf16[128,256]{1,0:T(8,128)(2,1)S(1)}, bf16[128,256]{1,0:T(8,128)(2,1)S(1)}, u32[]{:S(2)}, u32[]{:S(2)}) collective-permute-start(bf16[128,256]{1,0:T(8,128)(2,1)S(1)} %shard_map.139.refs_0_), channel_id=1, source_target_pairs={{2,0},{3,1},{0,2},{1,3},{6,4},{7,5},{4,6},{5,7},{10,8},{11,9},{8,1... | collective-permute-start | bytes 196616 | tf_op jit(solution)/shard_map/ppermute | solution.py:228
  53.1 22.0 %collective-permute-start.16 = (bf16[4,144,128]{2,1,0:T(8,128)(2,1)}, bf16[4,144,128]{2,1,0:T(8,128)(2,1)}, u32[]{:S(2)}, u32[]{:S(2)}) collective-permute-start(bf16[4,144,128]{2,1,0:T(8,128)(2,1)} %pad_maximum_fusion.1), channel_id=1, source_target_pairs={{0,4},{4,8},{8,12},{12,16},{16,20},{20,24},{24,28},{28,0},{1,5},{5... | collective-permute-start | bytes 442376 | tf_op jit(solution)/shard_map/ppermute | solution.py:336
  66.6 4.3 %collective-permute-start.7 = (bf16[128,256]{1,0:T(8,128)(2,1)S(1)}, bf16[128,256]{1,0:T(8,128)(2,1)S(1)}, u32[]{:S(2)}, u32[]{:S(2)}) collective-permute-start(bf16[128,256]{1,0:T(8,128)(2,1)S(1)} %shard_map.139.refs_0_), channel_id=1, source_target_pairs={{1,0},{2,1},{3,2},{0,3},{5,4},{6,5},{7,6},{4,7},{9,8},{10,9},{11,1... | collective-permute-start | bytes 196616 | tf_op jit(solution)/shard_map/ppermute | solution.py:228
  71.2 8.3 %collective-permute-start.12 = (bf16[384,256]{1,0:T(8,128)(2,1)S(1)}, bf16[384,256]{1,0:T(8,128)(2,1)S(1)}, u32[]{:S(2)}, u32[]{:S(2)}) collective-permute-start(bf16[384,256]{1,0:T(8,128)(2,1)S(1)} %shard_map.140.refs_0_), channel_id=1, source_target_pairs={{0,16},{4,20},{8,24},{12,28},{16,0},{20,4},{24,8},{28,12},{1,17},{... | collective-permute-start | bytes 589832 | tf_op jit(solution)/shard_map/ppermute | solution.py:235
  72.7 6.8 %collective-permute-start.11 = (bf16[384,256]{1,0:T(8,128)(2,1)S(1)}, bf16[384,256]{1,0:T(8,128)(2,1)S(1)}, u32[]{:S(2)}, u32[]{:S(2)}) collective-permute-start(bf16[384,256]{1,0:T(8,128)(2,1)S(1)} %shard_map.140.refs_0_), channel_id=1, source_target_pairs={{0,8},{4,12},{8,0},{12,4},{16,24},{20,28},{24,16},{28,20},{1,9},{5... | collective-permute-start | bytes 589832 | tf_op jit(solution)/shard_map/ppermute | solution.py:235
  75.1 12.6 %collective-permute-start.18 = (bf16[128,2048]{1,0:T(8,128)(2,1)S(1)}, bf16[128,2048]{1,0:T(8,128)(2,1)S(1)}, u32[]{:S(2)}, u32[]{:S(2)}) collective-permute-start(bf16[128,2048]{1,0:T(8,128)(2,1)S(1)} %copy-done.4), channel_id=1, source_target_pairs={{1,0},{2,1},{3,2},{0,3},{5,4},{6,5},{7,6},{4,7},{9,8},{10,9},{11,1... | collective-permute-start | bytes 1572872 | tf_op jit(solution)/shard_map/ppermute | solution.py:228
  79.4 30.9 %collective-permute-start.10 = (bf16[384,256]{1,0:T(8,128)(2,1)S(1)}, bf16[384,256]{1,0:T(8,128)(2,1)S(1)}, u32[]{:S(2)}, u32[]{:S(2)}) collective-permute-start(bf16[384,256]{1,0:T(8,128)(2,1)S(1)} %shard_map.140.refs_0_), channel_id=1, source_target_pairs={{0,4},{4,0},{8,12},{12,8},{16,20},{20,16},{24,28},{28,24},{1,5},{5... | collective-permute-start | bytes 589832 | tf_op jit(solution)/shard_map/ppermute | solution.py:235
  79.5 13.0 %collective-permute-start.14 = (bf16[192,256]{1,0:T(8,128)(2,1)S(1)}, bf16[192,256]{1,0:T(8,128)(2,1)S(1)}, u32[]{:S(2)}, u32[]{:S(2)}) collective-permute-start(bf16[192,256]{1,0:T(8,128)(2,1)S(1)} %slice.99), channel_id=1, source_target_pairs={{0,8},{4,12},{8,0},{12,4},{16,24},{20,28},{24,16},{28,20},{1,9},{5... | collective-permute-start | bytes 294920 | tf_op jit(solution)/shard_map/ppermute | solution.py:235
  80.1 12.4 %collective-permute-start.13 = (bf16[192,256]{1,0:T(8,128)(2,1)S(1)}, bf16[192,256]{1,0:T(8,128)(2,1)S(1)}, u32[]{:S(2)}, u32[]{:S(2)}) collective-permute-start(bf16[192,256]{1,0:T(8,128)(2,1)S(1)} %slice.98), channel_id=1, source_target_pairs={{0,16},{4,20},{8,24},{12,28},{16,0},{20,4},{24,8},{28,12},{1,17},{... | collective-permute-start | bytes 294920 | tf_op jit(solution)/shard_map/ppermute | solution.py:235
  81.6 15.7 %copy-start.2 = (bf16[16,4,128,128]{3,2,1,0:T(8,128)(2,1)S(1)}, bf16[16,4,128,128]{3,2,1,0:T(8,128)(2,1)}, u32[]{:S(2)}) copy-start(bf16[16,4,128,128]{3,2,1,0:T(8,128)(2,1)} %refs_6_.1) | copy-start | bytes 6291460
  87.8 9.5 %collective-permute-start.21 = (bf16[512,256]{1,0:T(8,128)(2,1)S(1)}, bf16[512,256]{1,0:T(8,128)(2,1)S(1)}, u32[]{:S(2)}, u32[]{:S(2)}) collective-permute-start(bf16[512,256]{1,0:T(8,128)(2,1)S(1)} %maximum_multiply_fusion), channel_id=1, source_target_pairs={{0,4},{4,8},{8,12},{12,16},{16,20},{20,24},{24,28},{28,0},{1,5},{5... | collective-permute-start | bytes 786440 | tf_op jit(solution)/shard_map/ppermute | solution.py:347
  87.9 9.4 %collective-permute-start.22 = (bf16[512,256]{1,0:T(8,128)(2,1)S(1)}, bf16[512,256]{1,0:T(8,128)(2,1)S(1)}, u32[]{:S(2)}, u32[]{:S(2)}) collective-permute-start(bf16[512,256]{1,0:T(8,128)(2,1)S(1)} %maximum_multiply_fusion.1), channel_id=1, source_target_pairs={{4,0},{8,4},{12,8},{16,12},{20,16},{24,20},{28,24},{0,28},{5,1},{9... | collective-permute-start | bytes 786440 | tf_op jit(solution)/shard_map/ppermute | solution.py:348
  92.6 17.8 %copy-start.5 = (bf16[16,2,128,128]{3,2,1,0:T(8,128)(2,1)S(1)}, bf16[16,2,128,128]{3,2,1,0:T(8,128)(2,1)}, u32[]{:S(2)}) copy-start(bf16[16,2,128,128]{3,2,1,0:T(8,128)(2,1)} %refs_7_.1) | copy-start | bytes 3145732
  92.6 17.8 %copy-start.7 = (s32[2048]{0:T(1024)S(1)}, s32[2048]{0:T(1024)}, u32[]{:S(2)}) copy-start(s32[2048]{0:T(1024)} %param.19) | copy-start | bytes 24580
  92.6 17.8 %copy-start.8 = (bf16[2,2048]{1,0:T(2,128)(2,1)S(1)}, bf16[2,2048]{1,0:T(2,128)(2,1)}, u32[]{:S(2)}) copy-start(bf16[2,2048]{1,0:T(2,128)(2,1)} %refs_11_.1) | copy-start | bytes 24580
  92.6 17.7 %collective-permute-start.15 = (bf16[1152,256]{1,0:T(8,128)(2,1)S(1)}, bf16[1152,256]{1,0:T(8,128)(2,1)S(1)}, u32[]{:S(2)}, u32[]{:S(2)}) collective-permute-start(bf16[1152,256]{1,0:T(8,128)(2,1)S(1)} %pad_maximum_fusion), channel_id=1, source_target_pairs={{0,4},{4,0},{8,12},{12,8},{16,20},{20,16},{24,28},{28,24},{1,5},{5... | collective-permute-start | bytes 1769480 | tf_op jit(solution)/shard_map/ppermute | solution.py:235

commit v2 on v1

--- a/solution.py
+++ b/solution.py
@@ -14,7 +14,7 @@
 COUNT_ROWS = 16
 
 
-def call(kernel, outs, ins, scratch=(), flops=0, bytes_accessed=0, mib=40):
+def call(kernel, outs, ins, scratch=(), flops=0, bytes_accessed=0, mib=16):
     specs = [SMEM if x.dtype == jnp.int32 and x.ndim == 1 else VMEM for x in ins]
     return pl.pallas_call(
         kernel,
@@ -35,21 +35,43 @@
     return jnp.where(rel == rows, jnp.ones((), BF), jnp.zeros((), BF))
 
 
-def sums_kernel(share, meta, state, ids, *outs_and_scratch):
-    *outs, lhs = outs_and_scratch
+def split_counts(rows, counts):
+    high = jnp.floor(counts * (1.0 / 256.0))
+    row = lax.broadcasted_iota(jnp.int32, (rows, counts.shape[1]), 0)
+    return jnp.where(row == 0, high, counts - 256.0 * high).astype(BF)
+
+
+def join_counts(rows):
+    return 256.0 * rows[0:1] + rows[1:2]
+
+
+def sums_kernel(share, meta, state, ids, kept, sent, lhs):
     channels, sensors = state.shape
     lhs[:channels] = state[...]
     lhs[channels:] = jnp.ones((COUNT_ROWS, sensors), BF)
     position = lax.broadcasted_iota(jnp.int32, (1, sensors), 1)
     own = jnp.where(position < meta[1], ids[...], -1)
-    for b, out in enumerate(outs):
-        hot = one_hot(own, (meta[0] ^ b) * share, share)
-        sums = lax.dot_general(lhs[...], hot, (((1,), (1,)), ((), ())), preferred_element_type=F32)
-        out[:channels] = sums[:channels].astype(BF)
-        counts = sums[channels:]
-        high = jnp.floor(counts * (1.0 / 256.0))
-        row = lax.broadcasted_iota(jnp.int32, counts.shape, 0)
-        out[channels:] = jnp.where(row == 0, high, counts - 256.0 * high).astype(BF)
+    for e in range(kept.shape[0]):
+        for other in (1, 0):
+            hot = one_hot(own, (meta[0] ^ (2 * e + other)) * share, share)
+            sums = lax.dot_general(
+                lhs[...], hot, (((1,), (1,)), ((), ())), preferred_element_type=F32
+            )
+            if other:
+                sent[e, :channels] = sums[:channels].astype(BF)
+                sent[e, channels:] = split_counts(COUNT_ROWS, sums[channels:])
+            else:
+                kept[e] = sums
+
+
+def pair_kernel(kept, arrived, own, *outs):
+    channels = own.shape[0] - COUNT_ROWS
+    for e, out in enumerate((own,) + outs):
+        came = arrived[e].astype(F32)
+        sums = kept[e, :channels] + came[:channels]
+        counts = kept[e, channels:] + join_counts(came[channels:])
+        out[:channels] = sums.astype(out.dtype)
+        out[channels:] = split_counts(COUNT_ROWS, counts).astype(out.dtype)
 
 
 def split3(x):
@@ -65,7 +87,7 @@
     total = blocks[0][...].astype(F32)
     for ref in blocks[1:]:
         total = total + ref[...].astype(F32)
-    counts = 256.0 * total[channels : channels + 1] + total[channels + 1 : channels + 2]
+    counts = join_counts(total[channels:])
     mean = total[:channels] / jnp.maximum(counts, 1.0)
     pooled[...] = mean
     heads, size = w_value.shape[0], w_value.shape[1]
@@ -101,69 +123,92 @@
         out[rows] = (pooled[rows] + attended).astype(BF)
 
 
-def fold_kernel(blocks, *refs):
-    parts, (w, out) = refs[:blocks], refs[blocks:]
-    coarse = jnp.concatenate([r[...] for r in parts], axis=0)
-    out[...] = jnp.dot(w[...], coarse, preferred_element_type=F32).astype(BF)
-
-
-def hop_kernel(blocks, tile, meta, cols, *refs):
+def fold_kernel(blocks, meta, *refs):
+    parts, (w, out, coarse) = refs[:blocks], refs[blocks:]
+    channels = parts[0].shape[0]
+    for k, part in enumerate(parts):
+        coarse[pl.ds(pl.multiple_of((meta[2] ^ k) * channels, channels), channels)] = part[...]
+    out[...] = jnp.dot(w[...], coarse[...], preferred_element_type=F32).astype(BF)
+
+
+def band_kernel(meta, cols, adj, band, edge_last, edge_first, total):
+    tiles, kb, tile, _ = adj.shape
+
+    def step(t, _):
+        spot = lax.broadcasted_iota(jnp.int32, (1, tile), 1) + t * tile
+        total[: 2 * tile] = jnp.zeros((2 * tile, tile), F32)
+        total[2 * tile :] = adj[t, kb - 1].astype(F32)
+        for k in range(kb - 1):
+            at = pl.ds(pl.multiple_of((cols[t * kb + k] - t) * tile, tile), tile)
+            total[at] = total[at] + adj[t, k].astype(F32)
+        band[t] = jnp.where(spot < meta[1], total[...], 0.0).astype(BF)
+        return 0
+
+    lax.fori_loop(0, tiles, step, 0)
+    half = 3 * tile // 2
+    for edge, t in ((edge_last, tiles - 1), (edge_first, 0)):
+        edge[:, :tile] = band[t, :half]
+        edge[:, tile:] = band[t, half:]
+
+
+def pair_weights(tile, a, b):
+    none = jnp.zeros((tile, tile), BF)
+    return jnp.concatenate(
+        [jnp.concatenate([a, none], axis=0), jnp.concatenate([none, b], axis=0)], axis=1
+    )
+
+
+def hop_one_kernel(blocks, tile, meta, *refs):
     parts = refs[:blocks]
-    left, right, adj, adj_left, adj_right, w, out, ext, one, two = refs[blocks:]
+    left, right, band, ext, one = refs[blocks:]
     channels, rows = parts[0].shape
-    total = channels * blocks
+    total = ext.shape[0]
+    n = total // channels
     tiles = rows // tile
-    position = lax.broadcasted_iota(jnp.int32, (1, rows), 1)
-    keep = position < meta[1]
-    ext[:, : 2 * tile] = left[...]
-    ext[:, 2 * tile + rows :] = right[...]
-    for k, part in enumerate(parts):
-        ext[k * channels : (k + 1) * channels, 2 * tile : 2 * tile + rows] = jnp.where(
-            keep, part[...], jnp.zeros((), BF)
+    half = 3 * tile // 2
+    keep = lax.broadcasted_iota(jnp.int32, (1, rows), 1) < meta[1]
+    ends = slice(0, 2 * tile), slice(2 * tile + rows, 4 * tile + rows)
+    for k in range(n):
+        at = pl.ds(pl.multiple_of((meta[2] ^ k) * channels, channels), channels)
+        part = parts[k][...]
+        if k == 3 and blocks > n:
+            part = jnp.where((meta[2] + 1) % 4 < 2, parts[4][...], part)
+        ext[at, 2 * tile : 2 * tile + rows] = jnp.where(keep, part, jnp.zeros((), BF))
+        for end, beside in zip(ends, (left, right)):
+            ext[at, end] = beside[k * channels : (k + 1) * channels]
+
+    def edge(ref):
+        return jnp.concatenate(
+            [ref[total : total + half, :tile], ref[total : total + half, tile:]], axis=0
         )
 
-    def pick(ref, at):
-        return jnp.concatenate(
-            [ref[:, pl.ds(pl.multiple_of(a * tile, tile), tile)] for a in at], axis=1
-        )
-
-    kb = adj.shape[1]
-    stack = lambda a: a.reshape(kb * tile, tile)
-    first = pick(ext, [cols[tiles * kb + k] for k in range(kb)])
-    one[:, :tile] = jnp.dot(first, stack(adj_left[...]), preferred_element_type=F32).astype(BF)
-    last = pick(ext, [cols[tiles * kb + kb + k] + tiles + 1 for k in range(kb)])
-    one[:, (tiles + 1) * tile :] = jnp.dot(
-        last, stack(adj_right[...]), preferred_element_type=F32
-    ).astype(BF)
-
-    def hop(source, shift, target, t):
-        picked = pick(source, [cols[t * kb + k] + shift for k in range(kb)])
-        made = jnp.dot(picked, stack(adj[t]), preferred_element_type=F32)
-        spot = lax.broadcasted_iota(jnp.int32, (1, tile), 1) + t * tile
-        return jnp.where(spot < meta[1], made, 0.0).astype(BF)
-
-    def step_one(t, _):
-        one[:, pl.ds(pl.multiple_of((t + 1) * tile, tile), tile)] = hop(ext, 1, one, t)
+    def hop(u, a, b):
+        at = lambda width: pl.ds(pl.multiple_of(2 * u * tile, 2 * tile), width)
+        made = jnp.dot(ext[:, at(4 * tile)], pair_weights(tile, a, b), preferred_element_type=F32)
+        one[:, at(2 * tile)] = made.astype(BF)
+
+    hop(0, edge(left), band[0])
+    hop(tiles // 2, band[tiles - 1], edge(right))
+
+    def step(u, _):
+        hop(u, band[2 * u - 1], band[2 * u])
         return 0
 
-    lax.fori_loop(0, tiles, step_one, 0, unroll=2)
-
-    def step_two(t, _):
-        two[:, pl.ds(pl.multiple_of(t * tile, tile), tile)] = hop(one, 0, two, t)
+    lax.fori_loop(1, tiles // 2, step, 0, unroll=True)
+
+
+def hop_two_kernel(tile, ext, one, band, w, out):
+    def step(u, _):
+        at = lambda s, width: pl.ds(pl.multiple_of(2 * u * tile + s, tile), width)
+        weights = pair_weights(tile, band[2 * u], band[2 * u + 1])
+        two = jnp.dot(one[:, at(0, 4 * tile)], weights, preferred_element_type=F32).astype(BF)
+        acc = jnp.dot(w[0], ext[:, at(2 * tile, 2 * tile)], preferred_element_type=F32)
+        acc = acc + jnp.dot(w[1], one[:, at(tile, 2 * tile)], preferred_element_type=F32)
+        acc = acc + jnp.dot(w[2], two, preferred_element_type=F32)
+        out[:, at(0, 2 * tile)] = acc
         return 0
 
-    lax.fori_loop(0, tiles, step_two, 0, unroll=2)
-    width = 2 * tile
-
-    def gates(c, _):
-        at = lambda s: pl.ds(pl.multiple_of(c * width + s, tile), width)
-        acc = jnp.dot(w[0], ext[:, at(2 * tile)], preferred_element_type=F32)
-        acc = acc + jnp.dot(w[1], one[:, at(tile)], preferred_element_type=F32)
-        acc = acc + jnp.dot(w[2], two[:, at(0)], preferred_element_type=F32)
-        out[:, at(0)] = acc
-        return 0
-
-    lax.fori_loop(0, rows // width, gates, 0)
+    lax.fori_loop(0, out.shape[1] // (2 * tile), step, 0, unroll=2)
 
 
 def final_kernel(places, n_given, share, tile, meta, ccols, *refs):
@@ -222,11 +267,18 @@
     return [(i, i ^ b) for i in range(n)]
 
 
-def shifts(array, axis):
-    n = lax.axis_size(axis)
-    return [array] + [
-        lax.ppermute(array, axis, [((i + k) % n, i) for i in range(n)]) for k in range(1, n)
-    ]
+def swap(array, axis, b):
+    return lax.ppermute(array, axis, flip(lax.axis_size(axis), b))
+
+
+def exchange(array):
+    n = lax.axis_size("feat")
+    if n != 4:
+        return [array] + [swap(array, "feat", k) for k in range(1, n)]
+    far = swap(array, "feat", 2)
+    near = swap(array, "feat", 1)
+    inner = lax.ppermute(array, "feat", [(1, 2), (2, 1)])
+    return [array, near, far, inner]
 
 
 def gather_dom(block):
@@ -279,28 +331,39 @@
     share = clusters // n_dom
     tiles, kb, tile, _ = adj_tiles.shape
     me, feat = lax.axis_index("dom"), lax.axis_index("feat")
-    meta = jnp.stack([me.astype(jnp.int32), valid_rows[0]])
+    meta = jnp.stack([me.astype(jnp.int32), valid_rows[0], feat.astype(jnp.int32)])
     ids = cluster_of[None, :]
     total = channels * n_feat
     outputs = 3 * channels
     sds = jax.ShapeDtypeStruct
 
-    blocks = shifts(state, "feat")
-
-    pieces = call(
+    kept, sent = call(
         functools.partial(sums_kernel, share),
-        [sds((channels + COUNT_ROWS, share), BF)] * n_dom,
+        [
+            sds((n_dom // 2, channels + COUNT_ROWS, share), F32),
+            sds((n_dom // 2, channels + COUNT_ROWS, share), BF),
+        ],
         [meta, state, ids],
         [pltpu.VMEM((channels + COUNT_ROWS, rows), BF)],
         flops=2 * channels * rows * clusters * 3,
         bytes_accessed=8 * channels * rows,
     )
-    arrived = [pieces[0]] + [lax.ppermute(pieces[b], "dom", flip(n_dom, b)) for b in range(1, n_dom)]
-    pooled, values = call(
-        functools.partial(pool_kernel, n_dom),
-        [sds((channels, share), F32), sds((channels, share), BF)],
-        [w_value] + arrived,
-    )
+    sent, state_late = lax.optimization_barrier((sent, state))
+    blocks = exchange(state_late)
+    pieces = call(
+        pair_kernel,
+        [sds((channels + COUNT_ROWS, share), F32)]
+        + [sds((channels + COUNT_ROWS, share), BF)] * (n_dom // 2 - 1),
+        [kept, lax.ppermute(sent, "dom", flip(n_dom, 1))],
+    )
+    pieces, source_emb, target_emb, w_gates, adj_tiles, w_input, coarse_cols = (
+        lax.optimization_barrier(
+            (pieces, source_emb, target_emb, w_gates, adj_tiles, w_input, coarse_cols)
+        )
+    )
+    arrived = [pieces[0]] + [
+        lax.ppermute(pieces[e], "dom", flip(n_dom, 2 * e)) for e in range(1, n_dom // 2)
+    ]
     pad = [(0, 0), (0, -source_emb.shape[1] % 16), (0, 0)]
     source = lax.dynamic_slice_in_dim(source_emb, me * share, share, 2)
     weights = call(
@@ -309,65 +372,73 @@
         [jnp.pad(source, pad), jnp.pad(target_emb, pad)],
         flops=source.shape[0] * clusters * share * 4000,
     )
+    w = jnp.transpose(w_gates, (2, 0, 1, 3)).reshape(4, outputs, total)
+    w_own, w_coarse = w[:3], w[3]
+    band, edge_last, edge_first = call(
+        band_kernel,
+        [sds((tiles, 3 * tile, tile), BF)] + [sds((3 * tile // 2, 2 * tile), BF)] * 2,
+        [meta, adj_cols.reshape(-1), adj_tiles],
+        [pltpu.VMEM((3 * tile, tile), F32)],
+        flops=10**9,
+    )
+    terms = jnp.concatenate(
+        [w_input.reshape(outputs, -1).astype(F32), bias.reshape(outputs, 1)], axis=1
+    )
+    coarse_at = coarse_cols.reshape(-1)
+    ready = (weights, w_own, w_coarse, band, edge_last, edge_first, terms, coarse_at)
+    arrived, ready = lax.optimization_barrier((arrived, ready))
+    weights, w_own, w_coarse, band, edge_last, edge_first, terms, coarse_at = ready
+    pooled, values = call(
+        functools.partial(pool_kernel, n_dom // 2),
+        [sds((channels, share), F32), sds((channels, share), BF)],
+        [w_value] + arrived,
+    )
     every_value = lax.all_gather(values, "dom", axis=0)
+    if n_feat == 4:
+        every_value, blocks[2] = lax.optimization_barrier((every_value, blocks[2]))
+        blocks.append(lax.ppermute(blocks[2], "feat", [(1, 0), (2, 3)]))
     own_coarse = call(attend_kernel, sds((channels, share), BF), [every_value, weights, pooled])
-    coarse_blocks = shifts(own_coarse, "feat")
-
-    w = jnp.transpose(w_gates, (2, 0, 1, 3)).reshape(4, outputs, total)
-    w = lax.dynamic_slice_in_dim(jnp.concatenate([w, w], axis=2), feat * channels, total, 2)
+    coarse_blocks = [own_coarse] + [swap(own_coarse, "feat", k) for k in range(1, n_feat)]
+    coarse_blocks, blocks = lax.optimization_barrier((coarse_blocks, blocks))
     folded = call(
         functools.partial(fold_kernel, n_feat),
         sds((outputs, share), BF),
-        coarse_blocks + [w[3]],
+        [meta] + coarse_blocks + [w_coarse],
+        [pltpu.VMEM((total, share), BF)],
     )
     given, places = gather_dom(folded)
 
     up = [(i, (i + 1) % n_dom) for i in range(n_dom)]
     down = [(j, i) for i, j in up]
-    spot = jnp.arange(rows, dtype=jnp.int32)
-    keep = (spot < valid_rows[0]).astype(BF)
-
-    def edge(t):
-        made = adj_tiles[t] * keep[t * tile : (t + 1) * tile]
-        offsets = (adj_cols[t] - t).astype(BF)
-        offsets = jnp.broadcast_to(offsets[:, None, None], (kb, 16, tile))
-        return jnp.concatenate([made, offsets], axis=1)
-
-    from_left = lax.ppermute(edge(tiles - 1), "dom", up)
-    from_right = lax.ppermute(edge(0), "dom", down)
-    cols = jnp.concatenate(
-        [
-            adj_cols.reshape(-1),
-            from_left[:, tile, 0].astype(jnp.int32),
-            from_right[:, tile, 0].astype(jnp.int32),
-        ]
-    )
-    tail = jnp.concatenate([x[:, rows - 2 * tile :] for x in blocks], axis=0)
-    head = jnp.concatenate([x[:, : 2 * tile] for x in blocks], axis=0)
-    left = lax.ppermute(tail * keep[rows - 2 * tile :], "dom", up)
-    right = lax.ppermute(head * keep[: 2 * tile], "dom", down)
+    keep = (jnp.arange(rows, dtype=jnp.int32) < valid_rows[0]).astype(BF)
+
+    def edge_of(lanes, weights):
+        ends = [x[:, lanes] for x in blocks]
+        if n_feat == 4:
+            ends[3:] = [jnp.where((feat == 0) | (feat == 3), ends[4], ends[3])]
+        return jnp.concatenate([x * keep[lanes] for x in ends] + [weights], axis=0)
+
+    left = lax.ppermute(edge_of(slice(rows - 2 * tile, rows), edge_last), "dom", up)
+    right = lax.ppermute(edge_of(slice(0, 2 * tile), edge_first), "dom", down)
+    ext, one = call(
+        functools.partial(hop_one_kernel, len(blocks), tile),
+        [sds((total, rows + 4 * tile), BF), sds((total, rows + 2 * tile), BF)],
+        [meta] + blocks + [left, right, band],
+        flops=2 * total * rows * kb * tile,
+        bytes_accessed=8 * total * rows,
+    )
     partial = call(
-        functools.partial(hop_kernel, n_feat, tile),
+        functools.partial(hop_two_kernel, tile),
         sds((outputs, rows), F32),
-        [meta, cols]
-        + blocks
-        + [left, right, adj_tiles, from_left[:, :tile], from_right[:, :tile], w[:3]],
-        [
-            pltpu.VMEM((total, rows + 4 * tile), BF),
-            pltpu.VMEM((total, rows + 2 * tile), BF),
-            pltpu.VMEM((total, rows), BF),
-        ],
-        flops=2 * total * rows * (4 * kb * tile + 3 * outputs),
+        [ext, one, band, w_own],
+        flops=2 * total * rows * (kb * tile + 3 * outputs),
         bytes_accessed=8 * total * rows,
     )
 
-    terms = jnp.concatenate(
-        [w_input.reshape(outputs, -1).astype(F32), bias.reshape(outputs, 1)], axis=1
-    )
     return call(
         functools.partial(final_kernel, places, len(given), share, tile),
         sds((channels, rows), BF),
-        [meta, coarse_cols.reshape(-1)]
+        [meta, coarse_at]
         + given
         + [coarse_tiles, ids, partial, terms, inputs, state],
         [pltpu.VMEM((outputs, clusters), BF)] * 2,

time: 120 us -> 99.6 us (0.83)
  waiting for transfers between devices: 34.8 us -> 20.4 us
  starting transfers between devices: 29.2 us -> 22.7 us
    ppermute x17 -> x13, waiting for transfers between devices: 34.8 us -> 12 us  [the longest x5 11.9 us: swap(): return lax.ppermute(array, axis, flip(lax.axis_size(axis), b))]
    ppermute x6, waiting for transfers between devices: 0.02 us -> 8.49 us  [gather_dom(): send = lambda x, b: lax.ppermute(x, 'dom', flip(n, b))]
    ppermute x17 -> x13, starting transfers between devices: 24.8 us -> 17.9 us  [the longest x5 11.1 us: swap(): return lax.ppermute(array, axis, flip(lax.axis_size(axis), b))]
    unnamed x0 -> x4, other arithmetic: none -> 4.53 us
    slice x10 -> x3, local copies, waits for them, and re-layouts: 4.22 us -> 1.14 us  [the longest x2 1.13 us: body(): w_own, w_coarse = (w[:3], w[3])]
    transpose x1 -> x0, local copies, waits for them, and re-layouts: 2.91 us -> none  [body(): w = jnp.transpose(w_gates, (2, 0, 1, 3)).reshape(4, outputs, total)]
    concatenate x4 -> x0, other arithmetic: 2.75 us -> none  [the longest x1 1.99 us: body(): jnp.concatenate([w, w], axis=2)]
    optimization_barrier x0 -> x5, local copies, waits for them, and re-layouts: none -> 2.03 us  [the longest x4 1.2 us: body(): lax.optimization_barrier((pieces, source_emb, target_emb, w_gates, adj_ti...]
  transfers between devices with their start and end apart: 23 -> 19, of which waited for: 5 -> 3; matrix products, arithmetic and copies ran while one was open for 12% -> 12% of each run, Pallas kernels for 14% -> 14%
where the time goes in v2:
time: 99.6 us; the launch traced here: 99 us
  Pallas kernels  28.8 us (29%)
  starting transfers between devices  22.7 us (23%)
  waiting for transfers between devices  20.4 us (20%)
  local copies, waits for them, and re-layouts  10.1 us (10%)
  blocking collectives  9.87 us (10%)
  other arithmetic  6.09 us (6%)
  between operations  1.04 us (1%)
    pallas_call x10, Pallas kernels, call(): pl.pallas_call(kernel, out_shape=outs, in_specs=specs, out_specs=jax.tree...  28.8 us
    ppermute x5, waiting for transfers between devices, swap(): return lax.ppermute(array, axis, flip(lax.axis_size(axis), b))  11.9 us
    ppermute x5, starting transfers between devices, swap(): return lax.ppermute(array, axis, flip(lax.axis_size(axis), b))  11.1 us
    all_gather x1, blocking collectives, body(): every_value = lax.all_gather(values, 'dom', axis=0)  9.87 us
    ppermute x6, waiting for transfers between devices, gather_dom(): send = lambda x, b: lax.ppermute(x, 'dom', flip(n, b))  8.49 us
    ppermute x6, starting transfers between devices, gather_dom(): send = lambda x, b: lax.ppermute(x, 'dom', flip(n, b))  4.79 us
    unnamed x58, local copies, waits for them, and re-layouts  4.75 us
    unnamed x4, other arithmetic  4.53 us
  transfers between devices with their start and end apart: 19, of which 3 were waited for; matrix products, arithmetic and copies ran while one was open for 12% of the time, Pallas kernels for 14%

profile of v2, /device:TPU:0, one launch (start us, length us, event | category | flops | bytes accessed | tf_op | source)
XLA Modules:
  0.0 99.0 jit_solution(5849610167196135289)
XLA Ops:
  0.7 0.1 pad_add_fusion.meta
  0.7 0.7 copy-done.17
  1.4 3.9 %shard_map.136 = (f32[4,144,256]{2,1,0:T(8,128)S(1)}, bf16[4,144,256]{2,1,0:T(8,128)(2,1)S(1)}) custom-call(s32[3]{0:T(128)S(1)} %pad_add_fusion.meta, bf16[128,2048]{1,0:T(8,128)(2,1)} %refs_12_.1, s32[1,2048]{1,0:T(1,128)S(1)} %bitcast.23), custom_call_target="tpu_custom_call" | custom-call | flops 3221225472 | bytes 2097152 | tf_op jit(solution)/shard_map/pallas_call | solution.py:19
  5.4 0.5 collective-permute-start
  5.9 3.7 %collective-permute-start.4 = (bf16[128,2048]{1,0:T(8,128)(2,1)}, bf16[128,2048]{1,0:T(8,128)(2,1)S(1)}, u32[]{:S(2)}, u32[]{:S(2)}) collective-permute-start(bf16[128,2048]{1,0:T(8,128)(2,1)} %refs_12_.1), channel_id=1, source_target_pairs={{0,2},{1,3},{2,0},{3,1},{4,6},{5,7},{6,4},{7,5},{8,10},{9,11},{10,... | collective-permute-start | bytes 1572872 | tf_op jit(solution)/shard_map/ppermute | solution.py:271
  9.6 1.6 %collective-permute-start.8 = (bf16[128,2048]{1,0:T(8,128)(2,1)}, bf16[128,2048]{1,0:T(8,128)(2,1)S(1)}, u32[]{:S(2)}, u32[]{:S(2)}) collective-permute-start(bf16[128,2048]{1,0:T(8,128)(2,1)} %refs_12_.1), channel_id=1, source_target_pairs={{0,1},{1,0},{2,3},{3,2},{4,5},{5,4},{6,7},{7,6},{8,9},{9,8},{10,11... | collective-permute-start | bytes 1572872 | tf_op jit(solution)/shard_map/ppermute | solution.py:271
  11.1 0.1 copy.38
  11.2 0.1 reshape.18.cols
  11.3 0.0 copy-start.20
  11.3 0.0 collective-permute-done.arrived
  11.4 0.7 shard_map.137
  12.1 0.1 copy.35
  12.2 0.1 copy.36
  12.3 0.4 copy-done.6
  12.8 0.1 copy-done.20
  12.8 0.3 copy.45
  13.2 1.1 %slice.75 = bf16[3,3,128,512]{3,2,1,0:T(8,128)(2,1)} slice(bf16[4,3,128,512]{3,2,1,0:T(8,128)(2,1)S(1)} %bitcast.25), slice={[0:3], [0:3], [0:128], [0:512]} | slice | bytes 2359296 | tf_op jit(solution)/shard_map/slice | solution.py:376
  14.3 1.5 %collective-permute-start.1 = (bf16[144,256]{1,0:T(8,128)(2,1)}, bf16[144,256]{1,0:T(8,128)(2,1)}, u32[]{:S(2)}, u32[]{:S(2)}) collective-permute-start(bf16[144,256]{1,0:T(8,128)(2,1)} %get-tuple-element.61), channel_id=1, source_target_pairs={{0,8},{4,12},{8,0},{12,4},{16,24},{20,28},{24,16},{28,20},{1,9},{5... | collective-permute-start | bytes 221192 | tf_op jit(solution)/shard_map/ppermute | solution.py:365
  15.8 1.5 %collective-permute-start.2 = (bf16[144,256]{1,0:T(8,128)(2,1)}, bf16[144,256]{1,0:T(8,128)(2,1)}, u32[]{:S(2)}, u32[]{:S(2)}) collective-permute-start(bf16[144,256]{1,0:T(8,128)(2,1)} %get-tuple-element.62), channel_id=1, source_target_pairs={{0,16},{4,20},{8,24},{12,28},{16,0},{20,4},{24,8},{28,12},{1,17},{... | collective-permute-start | bytes 221192 | tf_op jit(solution)/shard_map/ppermute | solution.py:365
  17.3 0.5 collective-permute-start.3
  17.8 2.2 %shard_map.138.weights = bf16[2,2048,256]{2,1,0:T(8,128)(2,1)S(1)} custom-call(f32[2,16,256]{2,1,0:T(8,128)S(1)} %pad.8.source, f32[2,16,2048]{2,1,0:T(8,128)S(1)} %pad.9.target), custom_call_target="tpu_custom_call" | custom-call | flops 4194304000 | tf_op jit(solution)/shard_map/pallas_call | solution.py:19
  20.0 0.6 pad_maximum_fusion.1
  20.7 0.7 copy.40
  21.3 0.8 reshape.20.ccols
  22.1 0.0 copy-start.15
  22.1 1.6 %copy-done.15 = bf16[16,4,128,128]{3,2,1,0:T(8,128)(2,1)S(1)} copy-done((bf16[16,4,128,128]{3,2,1,0:T(8,128)(2,1)S(1)}, bf16[16,4,128,128]{3,2,1,0:T(8,128)(2,1)}, u32[]{:S(2)}) %copy-start.15) | copy-done | bytes 2097176
  23.7 1.3 %shard_map.139 = (bf16[16,384,128]{2,1,0:T(8,128)(2,1)S(1)}, bf16[192,256]{1,0:T(8,128)(2,1)S(1)}, bf16[192,256]{1,0:T(8,128)(2,1)S(1)}) custom-call(s32[3]{0:T(128)S(1)} %pad_add_fusion.meta, s32[64]{0:T(128)S(1)} %reshape.18.cols, bf16[16,4,128,128]{3,2,1,0:T(8,128)(2,1)S(1)} %copy-done.15), custom_call_target="tpu_custom_call" | custom-call | flops 1000000000 | tf_op jit(solution)/shard_map/pallas_call | solution.py:19
  25.1 1.2 %copy-done = bf16[16,384,128]{2,1,0:T(8,128)(2,1)} copy-done((bf16[16,384,128]{2,1,0:T(8,128)(2,1)}, bf16[16,384,128]{2,1,0:T(8,128)(2,1)S(1)}, u32[]{:S(2)}) %copy-start) | copy-done | bytes 1572888
  26.3 1.5 %collective-permute-start.9 = (bf16[128,2048]{1,0:T(8,128)(2,1)}, bf16[128,2048]{1,0:T(8,128)(2,1)}, u32[]{:S(2)}, u32[]{:S(2)}) collective-permute-start(bf16[128,2048]{1,0:T(8,128)(2,1)} %refs_12_.1), channel_id=1, source_target_pairs={{1,2},{2,1},{5,6},{6,5},{9,10},{10,9},{13,14},{14,13},{17,18},{18,... | collective-permute-start | bytes 1572872 | tf_op jit(solution)/shard_map/ppermute | solution.py:280
  27.7 0.0 collective-permute-done.2.refs_2_
  27.7 0.0 collective-permute-done.3.refs_3_
  27.7 1.2 %shard_map.140 = (f32[128,256]{1,0:T(8,128)S(1)}, bf16[128,256]{1,0:T(8,128)(2,1)S(1)}) custom-call(bf16[2,64,64]{2,1,0:T(8,128)(2,1)S(1)} %copy-done.14, f32[144,256]{1,0:T(8,128)S(1)} %copy-done.7, bf16[144,256]{1,0:T(8,128)(2,1)} %collective-permute-done.1.refs_1_, bf16[144,256]{1,0:T(8,128)(2,1)} %collective-permute-done.2.refs_2_, ...), custom_call_target="tpu_custom_call" | custom-call | tf_op jit(solution)/shard_map/pallas_call | solution.py:19
  28.9 9.9 %all-gather = bf16[1024,256]{1,0:T(8,128)(2,1)S(1)} all-gather(bf16[128,256]{1,0:T(8,128)(2,1)S(1)} %get-tuple-element.78), channel_id=2, replica_groups=mesh['dom'=8,'feat'=4] {'dom'}, dimensions={0}, use_global_device_ids=true | all-gather | bytes 589824 | tf_op jit(solution)/shard_map/all_gather | solution.py:396
  38.8 1.3 %collective-permute-start.10 = (bf16[128,2048]{1,0:T(8,128)(2,1)S(1)}, bf16[128,2048]{1,0:T(8,128)(2,1)}, u32[]{:S(2)}, u32[]{:S(2)}) collective-permute-start(bf16[128,2048]{1,0:T(8,128)(2,1)S(1)} %collective-permute-done.4.refs_2_), channel_id=1, source_target_pairs={{1,0},{2,3},{5,4},{6,7},{9,8},{10,11},{13,12},{14,15},{17,16},{18,... | collective-permute-start | bytes 1572872 | tf_op jit(solution)/shard_map/ppermute | solution.py:399
  40.1 1.1 %shard_map.141.refs_0_ = bf16[128,256]{1,0:T(8,128)(2,1)} custom-call(bf16[8,128,256]{2,1,0:T(8,128)(2,1)S(1)} %bitcast.20, bf16[2,2048,256]{2,1,0:T(8,128)(2,1)S(1)} %shard_map.138.weights, f32[128,256]{1,0:T(8,128)S(1)} %get-tuple-element.82.pooled), custom_call_target="tpu_custom_call" | custom-call | tf_op jit(solution)/shard_map/pallas_call | solution.py:19
  41.2 3.5 %collective-permute-start.5 = (bf16[128,256]{1,0:T(8,128)(2,1)}, bf16[128,256]{1,0:T(8,128)(2,1)S(1)}, u32[]{:S(2)}, u32[]{:S(2)}) collective-permute-start(bf16[128,256]{1,0:T(8,128)(2,1)} %shard_map.141.refs_0_), channel_id=1, source_target_pairs={{0,1},{1,0},{2,3},{3,2},{4,5},{5,4},{6,7},{7,6},{8,9},{9,8},{10,11... | collective-permute-start | bytes 196616 | tf_op jit(solution)/shard_map/ppermute | solution.py:271
  44.7 2.4 %collective-permute-start.7 = (bf16[128,256]{1,0:T(8,128)(2,1)}, bf16[128,256]{1,0:T(8,128)(2,1)S(1)}, u32[]{:S(2)}, u32[]{:S(2)}) collective-permute-start(bf16[128,256]{1,0:T(8,128)(2,1)} %shard_map.141.refs_0_), channel_id=1, source_target_pairs={{0,3},{1,2},{2,1},{3,0},{4,7},{5,6},{6,5},{7,4},{8,11},{9,10},{10,... | collective-permute-start | bytes 196616 | tf_op jit(solution)/shard_map/ppermute | solution.py:271
  47.1 0.0 collective-permute-done.9.refs_3_
  47.2 11.9 %collective-permute-done.5.refs_1_ = bf16[128,256]{1,0:T(8,128)(2,1)S(1)} collective-permute-done((bf16[128,256]{1,0:T(8,128)(2,1)}, bf16[128,256]{1,0:T(8,128)(2,1)S(1)}, u32[]{:S(2)}, u32[]{:S(2)}) %collective-permute-start.5) | collective-permute-done | bytes 65568 | tf_op jit(solution)/shard_map/ppermute | solution.py:271
  59.1 0.0 collective-permute-done.6.refs_2_
  59.1 1.1 %shard_map.142.refs_0_ = bf16[384,256]{1,0:T(8,128)(2,1)S(1)} custom-call(s32[3]{0:T(128)S(1)} %pad_add_fusion.meta, bf16[128,256]{1,0:T(8,128)(2,1)} %shard_map.141.refs_0_, bf16[128,256]{1,0:T(8,128)(2,1)S(1)} %collective-permute-done.5.refs_1_, bf16[128,256]{1,0:T(8,128)(2,1)S(1)} %collective-permute-done.6.refs_2_, ...), custom_call_target="tpu_custom_call" | custom-call | tf_op jit(solution)/shard_map/pallas_call | solution.py:19
  60.2 1.6 %collective-permute-start.12 = (bf16[384,256]{1,0:T(8,128)(2,1)S(1)}, bf16[384,256]{1,0:T(8,128)(2,1)S(1)}, u32[]{:S(2)}, u32[]{:S(2)}) collective-permute-start(bf16[384,256]{1,0:T(8,128)(2,1)S(1)} %shard_map.142.refs_0_), channel_id=1, source_target_pairs={{0,8},{4,12},{8,0},{12,4},{16,24},{20,28},{24,16},{28,20},{1,9},{5... | collective-permute-start | bytes 589832 | tf_op jit(solution)/shard_map/ppermute | solution.py:287
  61.8 0.5 collective-permute-start.13
  62.3 1.6 %multiply_dynamic-update-slice_fusion.3 = (bf16[704,256]{1,0:T(8,128)(2,1)}, bf16[704,256]{1,0:T(8,128)(2,1)}) fusion(bf16[128,2048]{1,0:T(8,128)(2,1)} %refs_12_.1, bf16[256]{0:T(256)(128)(2,1)S(1)} %get-tuple-element.109, bf16[256]{0:T(256)(128)(2,1)S(1)} %get-tuple-element.110), kind=kLoop, calls=%fused_computation.5 | loop fusion | flops 262142 | bytes 263168
  63.9 0.7 multiply_dynamic-update-slice_fusion.2
  64.6 0.7 multiply_dynamic-update-slice_fusion.1
  65.2 1.6 %multiply_dynamic-update-slice_fusion = (bf16[704,256]{1,0:T(8,128)(2,1)}, bf16[704,256]{1,0:T(8,128)(2,1)}) fusion(bf16[704,256]{1,0:T(8,128)(2,1)} %get-tuple-element.103, bf16[128,2048]{1,0:T(8,128)(2,1)} %collective-permute-done.9.refs_3_, bf16[128,2048]{1,0:T(8,128)(2,1)} %collective-permute-done.10.refs_4_, pred[]{:T(512)S(6)} %or.4, ...), kind=kLoop, calls=%fused_computation.2 | loop fusion | flops 327680 | bytes 394241
  66.9 0.6 constant_dynamic-update-slice_fusion.1
  67.5 0.1 collective-permute-start.18
  67.6 1.6 %collective-permute-start.14 = (bf16[192,256]{1,0:T(8,128)(2,1)S(1)}, bf16[192,256]{1,0:T(8,128)(2,1)S(1)}, u32[]{:S(2)}, u32[]{:S(2)}) collective-permute-start(bf16[192,256]{1,0:T(8,128)(2,1)S(1)} %slice.77), channel_id=1, source_target_pairs={{0,16},{4,20},{8,24},{12,28},{16,0},{20,4},{24,8},{28,12},{1,17},{... | collective-permute-start | bytes 294920 | tf_op jit(solution)/shard_map/ppermute | solution.py:287
  69.2 0.6 collective-permute-start.15
  69.8 0.6 constant_dynamic-update-slice_fusion
  70.4 2.4 %collective-permute-done.14.refs_4_ = bf16[192,256]{1,0:T(8,128)(2,1)S(1)} collective-permute-done((bf16[192,256]{1,0:T(8,128)(2,1)S(1)}, bf16[192,256]{1,0:T(8,128)(2,1)S(1)}, u32[]{:S(2)}, u32[]{:S(2)}) %collective-permute-start.14) | collective-permute-done | bytes 98336 | tf_op jit(solution)/shard_map/ppermute | solution.py:287
  72.8 6.1 %collective-permute-done.15.refs_5_ = bf16[192,256]{1,0:T(8,128)(2,1)S(1)} collective-permute-done((bf16[192,256]{1,0:T(8,128)(2,1)S(1)}, bf16[192,256]{1,0:T(8,128)(2,1)S(1)}, u32[]{:S(2)}, u32[]{:S(2)}) %collective-permute-start.15) | collective-permute-done | bytes 98336 | tf_op jit(solution)/shard_map/ppermute | solution.py:287
  78.9 0.9 pad_maximum_fusion
  79.8 0.6 copy-done.8
  80.4 0.8 copy.41.refs_10_
  81.2 0.5 collective-permute-start.11
  81.8 3.1 %shard_map.143 = (bf16[512,2560]{1,0:T(8,128)(2,1)S(1)}, bf16[512,2304]{1,0:T(8,128)(2,1)S(1)}) custom-call(s32[3]{0:T(128)S(1)} %pad_add_fusion.meta, bf16[128,2048]{1,0:T(8,128)(2,1)} %refs_12_.1, bf16[128,2048]{1,0:T(8,128)(2,1)S(1)} %collective-permute-done.8.refs_1_, bf16[128,2048]{1,0:T(8,128)(2,1)S(1)} %collective-permute-done.4.refs_2_, ...), custom_call_target="tpu_custom_call" | custom-call | flops 1073741824 | bytes 8388608 | tf_op jit(solution)/shard_map/pallas_call | solution.py:19
  84.9 0.0 copy-start.16
  84.9 0.0 copy-start.18
  84.9 0.0 copy-start.19
  84.9 4.3 %shard_map.144.refs_9_ = f32[384,2048]{1,0:T(8,128)S(1)} custom-call(bf16[512,2560]{1,0:T(8,128)(2,1)S(1)} %get-tuple-element.97.ext, bf16[512,2304]{1,0:T(8,128)(2,1)S(1)} %get-tuple-element.98.one, bf16[16,384,128]{2,1,0:T(8,128)(2,1)S(1)} %copy-done.1, bf16[3,384,512]{2,1,0:T(8,128)(2,1)S(1)} %bitcast.22), custom_call_target="tpu_custom_call" | custom-call | flops 3489660928 | bytes 8388608 | tf_op jit(solution)/shard_map/pallas_call | solution.py:19
  89.4 9.7 %shard_map.145 = bf16[128,2048]{1,0:T(8,128)(2,1)} custom-call(s32[3]{0:T(128)S(1)} %pad_add_fusion.meta, s32[32]{0:T(128)S(1)} %reshape.20.ccols, bf16[384,256]{1,0:T(8,128)(2,1)S(1)} %copy-done.5, bf16[384,256]{1,0:T(8,128)(2,1)S(1)} %collective-permute-done.11.refs_1_, bf16[384,256]{1,0:T(8,128)(2,1)S(1)} %collective-permute-done.12.refs_2_, ...), custom_call_target="tpu_custom_call" | custom-call | flops 3221225472 | bytes 6291456 | tf_op jit(solution)/shard_map/pallas_call | solution.py:19
  (69 shorter events, 0.2 us)
Async XLA Ops:
  0.7 0.7 copy-start.17
  1.4 9.7 %copy-start.24 = (s32[16,4]{0,1:T(4,128)S(1)}, s32[16,4]{0,1:T(4,128)}, u32[]{:S(2)}) copy-start(s32[16,4]{0,1:T(4,128)} %param.17) | copy-start | bytes 772
  1.4 9.9 %copy-start.25 = (f32[3,128]{1,0:T(4,128)S(1)}, f32[3,128]{1,0:T(4,128)}, u32[]{:S(2)}) copy-start(f32[3,128]{1,0:T(4,128)} %param.22) | copy-start | bytes 4612
  1.4 10.6 %copy-start.21 = (f32[2,10,2048]{2,0,1:T(2,128)S(1)}, f32[2,10,2048]{2,0,1:T(2,128)}, u32[]{:S(2)}) copy-start(f32[2,10,2048]{2,0,1:T(2,128)} %param.24) | copy-start | bytes 491524
  1.4 10.8 %copy-start.22 = (f32[2,10,2048]{2,0,1:T(2,128)S(1)}, f32[2,10,2048]{2,0,1:T(2,128)}, u32[]{:S(2)}) copy-start(f32[2,10,2048]{2,0,1:T(2,128)} %param.25) | copy-start | bytes 491524
  5.4 6.0 %collective-permute-start = (bf16[4,144,256]{2,1,0:T(8,128)(2,1)S(1)}, bf16[4,144,256]{2,1,0:T(8,128)(2,1)S(1)}, u32[]{:S(2)}, u32[]{:S(2)}) collective-permute-start(bf16[4,144,256]{2,1,0:T(8,128)(2,1)S(1)} %get-tuple-element.55), channel_id=1, source_target_pairs={{0,4},{4,0},{8,12},{12,8},{16,20},{20,16},{24,28},{28,24},{1,5},{5... | collective-permute-start | bytes 884744 | tf_op jit(solution)/shard_map/ppermute | solution.py:357
  5.9 32.9 %collective-permute-start.4 = (bf16[128,2048]{1,0:T(8,128)(2,1)}, bf16[128,2048]{1,0:T(8,128)(2,1)S(1)}, u32[]{:S(2)}, u32[]{:S(2)}) collective-permute-start(bf16[128,2048]{1,0:T(8,128)(2,1)} %refs_12_.1), channel_id=1, source_target_pairs={{0,2},{1,3},{2,0},{3,1},{4,6},{5,7},{6,4},{7,5},{8,10},{9,11},{10,... | collective-permute-start | bytes 1572872 | tf_op jit(solution)/shard_map/ppermute | solution.py:271
  9.6 35.1 %collective-permute-start.8 = (bf16[128,2048]{1,0:T(8,128)(2,1)}, bf16[128,2048]{1,0:T(8,128)(2,1)S(1)}, u32[]{:S(2)}, u32[]{:S(2)}) collective-permute-start(bf16[128,2048]{1,0:T(8,128)(2,1)} %refs_12_.1), channel_id=1, source_target_pairs={{0,1},{1,0},{2,3},{3,2},{4,5},{5,4},{6,7},{7,6},{8,9},{9,8},{10,11... | collective-permute-start | bytes 1572872 | tf_op jit(solution)/shard_map/ppermute | solution.py:271
  11.3 1.5 %copy-start.20 = (bf16[3,128,4,512]{3,2,1,0:T(4,128)(2,1)S(1)}, bf16[3,128,4,512]{3,2,1,0:T(4,128)(2,1)}, u32[]{:S(2)}) copy-start(bf16[3,128,4,512]{3,2,1,0:T(4,128)(2,1)} %param.20) | copy-start | bytes 4718596
  12.1 0.7 copy-start.6
  14.3 5.7 %copy-start.26 = (bf16[3,128,2]{1,2,0:T(2,128)(2,1)S(1)}, bf16[3,128,2]{1,2,0:T(2,128)(2,1)}, u32[]{:S(2)}) copy-start(bf16[3,128,2]{1,2,0:T(2,128)(2,1)} %param.21) | copy-start | bytes 4612
  14.3 6.4 %copy-start.27 = (s32[16,2]{0,1:T(2,128)S(1)}, s32[16,2]{0,1:T(2,128)}, u32[]{:S(2)}) copy-start(s32[16,2]{0,1:T(2,128)} %param.27) | copy-start | bytes 388
  14.3 12.0 %collective-permute-start.1 = (bf16[144,256]{1,0:T(8,128)(2,1)}, bf16[144,256]{1,0:T(8,128)(2,1)}, u32[]{:S(2)}, u32[]{:S(2)}) collective-permute-start(bf16[144,256]{1,0:T(8,128)(2,1)} %get-tuple-element.61), channel_id=1, source_target_pairs={{0,8},{4,12},{8,0},{12,4},{16,24},{20,28},{24,16},{28,20},{1,9},{5... | collective-permute-start | bytes 221192 | tf_op jit(solution)/shard_map/ppermute | solution.py:365
  15.8 12.0 %collective-permute-start.2 = (bf16[144,256]{1,0:T(8,128)(2,1)}, bf16[144,256]{1,0:T(8,128)(2,1)}, u32[]{:S(2)}, u32[]{:S(2)}) collective-permute-start(bf16[144,256]{1,0:T(8,128)(2,1)} %get-tuple-element.62), channel_id=1, source_target_pairs={{0,16},{4,20},{8,24},{12,28},{16,0},{20,4},{24,8},{28,12},{1,17},{... | collective-permute-start | bytes 221192 | tf_op jit(solution)/shard_map/ppermute | solution.py:365
  17.3 10.4 %collective-permute-start.3 = (bf16[144,256]{1,0:T(8,128)(2,1)}, bf16[144,256]{1,0:T(8,128)(2,1)}, u32[]{:S(2)}, u32[]{:S(2)}) collective-permute-start(bf16[144,256]{1,0:T(8,128)(2,1)} %get-tuple-element.63), channel_id=1, source_target_pairs={{0,24},{4,28},{8,16},{12,20},{16,8},{20,12},{24,0},{28,4},{1,25},{... | collective-permute-start | bytes 221192 | tf_op jit(solution)/shard_map/ppermute | solution.py:365
  22.1 1.6 %copy-start.15 = (bf16[16,4,128,128]{3,2,1,0:T(8,128)(2,1)S(1)}, bf16[16,4,128,128]{3,2,1,0:T(8,128)(2,1)}, u32[]{:S(2)}) copy-start(bf16[16,4,128,128]{3,2,1,0:T(8,128)(2,1)} %adj) | copy-start | bytes 6291460
  23.7 4.0 %copy-start.7 = (f32[144,256]{1,0:T(8,128)S(1)}, f32[144,256]{1,0:T(8,128)}, u32[]{:S(2)}) copy-start(f32[144,256]{1,0:T(8,128)} %copy-done.6) | copy-start | bytes 442372
  23.7 4.0 %copy-start.14 = (bf16[2,64,64]{2,1,0:T(8,128)(2,1)S(1)}, bf16[2,64,64]{2,1,0:T(8,128)(2,1)}, u32[]{:S(2)}) copy-start(bf16[2,64,64]{2,1,0:T(8,128)(2,1)} %w_value.1) | copy-start | bytes 49156
  25.1 1.2 %copy-start = (bf16[16,384,128]{2,1,0:T(8,128)(2,1)}, bf16[16,384,128]{2,1,0:T(8,128)(2,1)S(1)}, u32[]{:S(2)}) copy-start(bf16[16,384,128]{2,1,0:T(8,128)(2,1)S(1)} %get-tuple-element.96.refs_7_.band) | copy-start | bytes 4718596
  26.2 15.0 %copy-start.10 = (bf16[192,256]{1,0:T(8,128)(2,1)}, bf16[192,256]{1,0:T(8,128)(2,1)S(1)}, u32[]{:S(2)}) copy-start(bf16[192,256]{1,0:T(8,128)(2,1)S(1)} %get-tuple-element.94) | copy-start | bytes 294916
  26.2 15.0 %copy-start.12 = (bf16[192,256]{1,0:T(8,128)(2,1)}, bf16[192,256]{1,0:T(8,128)(2,1)S(1)}, u32[]{:S(2)}) copy-start(bf16[192,256]{1,0:T(8,128)(2,1)S(1)} %get-tuple-element.95) | copy-start | bytes 294916
  26.3 20.9 %collective-permute-start.9 = (bf16[128,2048]{1,0:T(8,128)(2,1)}, bf16[128,2048]{1,0:T(8,128)(2,1)}, u32[]{:S(2)}, u32[]{:S(2)}) collective-permute-start(bf16[128,2048]{1,0:T(8,128)(2,1)} %refs_12_.1), channel_id=1, source_target_pairs={{1,2},{2,1},{5,6},{6,5},{9,10},{10,9},{13,14},{14,13},{17,18},{18,... | collective-permute-start | bytes 1572872 | tf_op jit(solution)/shard_map/ppermute | solution.py:280
  38.8 20.3 %collective-permute-start.10 = (bf16[128,2048]{1,0:T(8,128)(2,1)S(1)}, bf16[128,2048]{1,0:T(8,128)(2,1)}, u32[]{:S(2)}, u32[]{:S(2)}) collective-permute-start(bf16[128,2048]{1,0:T(8,128)(2,1)S(1)} %collective-permute-done.4.refs_2_), channel_id=1, source_target_pairs={{1,0},{2,3},{5,4},{6,7},{9,8},{10,11},{13,12},{14,15},{17,16},{18,... | collective-permute-start | bytes 1572872 | tf_op jit(solution)/shard_map/ppermute | solution.py:399
  41.2 17.8 %collective-permute-start.5 = (bf16[128,256]{1,0:T(8,128)(2,1)}, bf16[128,256]{1,0:T(8,128)(2,1)S(1)}, u32[]{:S(2)}, u32[]{:S(2)}) collective-permute-start(bf16[128,256]{1,0:T(8,128)(2,1)} %shard_map.141.refs_0_), channel_id=1, source_target_pairs={{0,1},{1,0},{2,3},{3,2},{4,5},{5,4},{6,7},{7,6},{8,9},{9,8},{10,11... | collective-permute-start | bytes 196616 | tf_op jit(solution)/shard_map/ppermute | solution.py:271
  44.7 22.2 %copy-start.13 = (bf16[192,256]{1,0:T(8,128)(2,1)S(1)}, bf16[192,256]{1,0:T(8,128)(2,1)}, u32[]{:S(2)}) copy-start(bf16[192,256]{1,0:T(8,128)(2,1)} %copy-done.12) | copy-start | bytes 294916
  44.7 14.4 %collective-permute-start.6 = (bf16[128,256]{1,0:T(8,128)(2,1)}, bf16[128,256]{1,0:T(8,128)(2,1)S(1)}, u32[]{:S(2)}, u32[]{:S(2)}) collective-permute-start(bf16[128,256]{1,0:T(8,128)(2,1)} %shard_map.141.refs_0_), channel_id=1, source_target_pairs={{0,2},{1,3},{2,0},{3,1},{4,6},{5,7},{6,4},{7,5},{8,10},{9,11},{10,... | collective-permute-start | bytes 196616 | tf_op jit(solution)/shard_map/ppermute | solution.py:271
  44.7 14.4 %collective-permute-start.7 = (bf16[128,256]{1,0:T(8,128)(2,1)}, bf16[128,256]{1,0:T(8,128)(2,1)S(1)}, u32[]{:S(2)}, u32[]{:S(2)}) collective-permute-start(bf16[128,256]{1,0:T(8,128)(2,1)} %shard_map.141.refs_0_), channel_id=1, source_target_pairs={{0,3},{1,2},{2,1},{3,0},{4,7},{5,6},{6,5},{7,4},{8,11},{9,10},{10,... | collective-permute-start | bytes 196616 | tf_op jit(solution)/shard_map/ppermute | solution.py:271
  47.1 22.6 %copy-start.11 = (bf16[192,256]{1,0:T(8,128)(2,1)S(1)}, bf16[192,256]{1,0:T(8,128)(2,1)}, u32[]{:S(2)}) copy-start(bf16[192,256]{1,0:T(8,128)(2,1)} %copy-done.10) | copy-start | bytes 294916
  60.2 19.6 %copy-start.4 = (bf16[384,256]{1,0:T(8,128)(2,1)}, bf16[384,256]{1,0:T(8,128)(2,1)S(1)}, u32[]{:S(2)}) copy-start(bf16[384,256]{1,0:T(8,128)(2,1)S(1)} %shard_map.142.refs_0_) | copy-start | bytes 589828
  60.2 7.3 %collective-permute-start.12 = (bf16[384,256]{1,0:T(8,128)(2,1)S(1)}, bf16[384,256]{1,0:T(8,128)(2,1)S(1)}, u32[]{:S(2)}, u32[]{:S(2)}) collective-permute-start(bf16[384,256]{1,0:T(8,128)(2,1)S(1)} %shard_map.142.refs_0_), channel_id=1, source_target_pairs={{0,8},{4,12},{8,0},{12,4},{16,24},{20,28},{24,16},{28,20},{1,9},{5... | collective-permute-start | bytes 589832 | tf_op jit(solution)/shard_map/ppermute | solution.py:287
  61.8 7.4 %collective-permute-start.13 = (bf16[384,256]{1,0:T(8,128)(2,1)S(1)}, bf16[384,256]{1,0:T(8,128)(2,1)S(1)}, u32[]{:S(2)}, u32[]{:S(2)}) collective-permute-start(bf16[384,256]{1,0:T(8,128)(2,1)S(1)} %shard_map.142.refs_0_), channel_id=1, source_target_pairs={{0,16},{4,20},{8,24},{12,28},{16,0},{20,4},{24,8},{28,12},{1,17},{... | collective-permute-start | bytes 589832 | tf_op jit(solution)/shard_map/ppermute | solution.py:287
  62.3 18.1 %copy-start.23 = (f32[384,3]{0,1:T(4,128)S(1)}, f32[384,3]{0,1:T(4,128)}, u32[]{:S(2)}) copy-start(f32[384,3]{0,1:T(4,128)} %pad_maximum_fusion.1) | copy-start | bytes 13828
  63.9 17.9 %copy-start.1 = (bf16[16,384,128]{2,1,0:T(8,128)(2,1)S(1)}, bf16[16,384,128]{2,1,0:T(8,128)(2,1)}, u32[]{:S(2)}) copy-start(bf16[16,384,128]{2,1,0:T(8,128)(2,1)} %copy-done) | copy-start | bytes 4718596
  67.5 14.2 %collective-permute-start.18 = (bf16[704,256]{1,0:T(8,128)(2,1)}, bf16[704,256]{1,0:T(8,128)(2,1)S(1)}, u32[]{:S(2)}, u32[]{:S(2)}) collective-permute-start(bf16[704,256]{1,0:T(8,128)(2,1)} %constant_dynamic-update-slice_fusion.1), channel_id=1, source_target_pairs={{4,0},{8,4},{12,8},{16,12},{20,16},{24,20},{28,24},{0,28},{5,1},{9... | collective-permute-start | bytes 1081352 | tf_op jit(solution)/shard_map/ppermute | solution.py:422
  67.6 5.2 %collective-permute-start.14 = (bf16[192,256]{1,0:T(8,128)(2,1)S(1)}, bf16[192,256]{1,0:T(8,128)(2,1)S(1)}, u32[]{:S(2)}, u32[]{:S(2)}) collective-permute-start(bf16[192,256]{1,0:T(8,128)(2,1)S(1)} %slice.77), channel_id=1, source_target_pairs={{0,16},{4,20},{8,24},{12,28},{16,0},{20,4},{24,8},{28,12},{1,17},{... | collective-permute-start | bytes 294920 | tf_op jit(solution)/shard_map/ppermute | solution.py:287
  69.2 9.8 %collective-permute-start.15 = (bf16[192,256]{1,0:T(8,128)(2,1)S(1)}, bf16[192,256]{1,0:T(8,128)(2,1)S(1)}, u32[]{:S(2)}, u32[]{:S(2)}) collective-permute-start(bf16[192,256]{1,0:T(8,128)(2,1)S(1)} %slice.78), channel_id=1, source_target_pairs={{0,8},{4,12},{8,0},{12,4},{16,24},{20,28},{24,16},{28,20},{1,9},{5... | collective-permute-start | bytes 294920 | tf_op jit(solution)/shard_map/ppermute | solution.py:287
  70.4 11.3 %collective-permute-start.17 = (bf16[704,256]{1,0:T(8,128)(2,1)}, bf16[704,256]{1,0:T(8,128)(2,1)}, u32[]{:S(2)}, u32[]{:S(2)}) collective-permute-start(bf16[704,256]{1,0:T(8,128)(2,1)} %constant_dynamic-update-slice_fusion), channel_id=1, source_target_pairs={{0,4},{4,8},{8,12},{12,16},{16,20},{20,24},{24,28},{28,0},{1,5},{5... | collective-permute-start | bytes 1081352 | tf_op jit(solution)/shard_map/ppermute | solution.py:421
  79.8 0.6 copy-start.8
  80.4 8.9 %collective-permute-start.16 = (bf16[1152,256]{1,0:T(8,128)(2,1)}, bf16[1152,256]{1,0:T(8,128)(2,1)}, u32[]{:S(2)}, u32[]{:S(2)}) collective-permute-start(bf16[1152,256]{1,0:T(8,128)(2,1)} %pad_maximum_fusion), channel_id=1, source_target_pairs={{0,4},{4,0},{8,12},{12,8},{16,20},{20,16},{24,28},{28,24},{1,5},{5... | collective-permute-start | bytes 1769480 | tf_op jit(solution)/shard_map/ppermute | solution.py:287
  81.2 3.6 %copy-start.2 = (bf16[3,3,128,512]{3,2,1,0:T(8,128)(2,1)S(1)}, bf16[3,3,128,512]{3,2,1,0:T(8,128)(2,1)}, u32[]{:S(2)}) copy-start(bf16[3,3,128,512]{3,2,1,0:T(8,128)(2,1)} %slice.75) | copy-start | bytes 3538948
  81.2 8.0 %collective-permute-start.11 = (bf16[384,256]{1,0:T(8,128)(2,1)}, bf16[384,256]{1,0:T(8,128)(2,1)S(1)}, u32[]{:S(2)}, u32[]{:S(2)}) collective-permute-start(bf16[384,256]{1,0:T(8,128)(2,1)} %copy-done.4), channel_id=1, source_target_pairs={{0,4},{4,0},{8,12},{12,8},{16,20},{20,16},{24,28},{28,24},{1,5},{5... | collective-permute-start | bytes 589832 | tf_op jit(solution)/shard_map/ppermute | solution.py:287
  84.9 4.4 %copy-start.3 = (f32[384,3]{1,0:T(8,128)S(1)}, f32[384,3]{1,0:T(8,128)}, u32[]{:S(2)}) copy-start(f32[384,3]{1,0:T(8,128)} %copy.41.refs_10_) | copy-start | bytes 13828
  84.9 4.4 %copy-start.5 = (bf16[384,256]{1,0:T(8,128)(2,1)S(1)}, bf16[384,256]{1,0:T(8,128)(2,1)}, u32[]{:S(2)}) copy-start(bf16[384,256]{1,0:T(8,128)(2,1)} %copy-done.4) | copy-start | bytes 589828
  84.9 4.4 %copy-start.9 = (bf16[192,256]{1,0:T(8,128)(2,1)S(1)}, bf16[192,256]{1,0:T(8,128)(2,1)}, u32[]{:S(2)}) copy-start(bf16[192,256]{1,0:T(8,128)(2,1)} %copy-done.8) | copy-start | bytes 294916
  84.9 4.4 %copy-start.16 = (bf16[16,2,128,128]{3,2,1,0:T(8,128)(2,1)S(1)}, bf16[16,2,128,128]{3,2,1,0:T(8,128)(2,1)}, u32[]{:S(2)}) copy-start(bf16[16,2,128,128]{3,2,1,0:T(8,128)(2,1)} %refs_7_.1) | copy-start | bytes 3145732
  84.9 4.4 %copy-start.18 = (s32[2048]{0:T(1024)S(1)}, s32[2048]{0:T(1024)}, u32[]{:S(2)}) copy-start(s32[2048]{0:T(1024)} %param.19) | copy-start | bytes 24580
  84.9 4.4 %copy-start.19 = (bf16[2,2048]{1,0:T(2,128)(2,1)S(1)}, bf16[2,2048]{1,0:T(2,128)(2,1)}, u32[]{:S(2)}) copy-start(bf16[2,2048]{1,0:T(2,128)(2,1)} %refs_11_.1) | copy-start | bytes 24580

commit v3 on v2

--- a/solution.py
+++ b/solution.py
@@ -131,8 +131,9 @@
     out[...] = jnp.dot(w[...], coarse[...], preferred_element_type=F32).astype(BF)
 
 
-def band_kernel(meta, cols, adj, band, edge_last, edge_first, total):
+def band_kernel(meta, cols, adj, terms, band, edge_last, edge_first, terms_out, total):
     tiles, kb, tile, _ = adj.shape
+    terms_out[...] = terms[...]
 
     def step(t, _):
         spot = lax.broadcasted_iota(jnp.int32, (1, tile), 1) + t * tile
@@ -158,12 +159,30 @@
     )
 
 
-def hop_one_kernel(blocks, tile, meta, *refs):
-    parts = refs[:blocks]
-    left, right, band, ext, one = refs[blocks:]
+def is_end(feat):
+    return (feat + 1) % 4 < 2
+
+
+def edge_kernel(n, tile, meta, *refs):
+    *parts, edge_last, edge_first, last, first = refs
+    channels, rows = parts[0].shape
+    position = lax.broadcasted_iota(jnp.int32, (1, 2 * tile), 1)
+    ends = (last, rows - 2 * tile, edge_last), (first, 0, edge_first)
+    for out, start, weights in ends:
+        keep = position + start < meta[1]
+        for k in range(n):
+            part = parts[k][:, start : start + 2 * tile]
+            if k == 3 and len(parts) > n:
+                other = parts[4][:, start : start + 2 * tile]
+                part = jnp.where(is_end(meta[2]), other, part)
+            out[k * channels : (k + 1) * channels] = jnp.where(keep, part, jnp.zeros((), BF))
+        out[n * channels :] = weights[...]
+
+
+def hop_one_kernel(n, tile, meta, *refs):
+    *parts, left, right, band, ext, one = refs
     channels, rows = parts[0].shape
     total = ext.shape[0]
-    n = total // channels
     tiles = rows // tile
     half = 3 * tile // 2
     keep = lax.broadcasted_iota(jnp.int32, (1, rows), 1) < meta[1]
@@ -171,8 +190,8 @@
     for k in range(n):
         at = pl.ds(pl.multiple_of((meta[2] ^ k) * channels, channels), channels)
         part = parts[k][...]
-        if k == 3 and blocks > n:
-            part = jnp.where((meta[2] + 1) % 4 < 2, parts[4][...], part)
+        if k == 3 and len(parts) > n:
+            part = jnp.where(is_end(meta[2]), parts[4][...], part)
         ext[at, 2 * tile : 2 * tile + rows] = jnp.where(keep, part, jnp.zeros((), BF))
         for end, beside in zip(ends, (left, right)):
             ext[at, end] = beside[k * channels : (k + 1) * channels]
@@ -208,7 +227,7 @@
         out[:, at(0, 2 * tile)] = acc
         return 0
 
-    lax.fori_loop(0, out.shape[1] // (2 * tile), step, 0, unroll=2)
+    lax.fori_loop(0, out.shape[1] // (2 * tile), step, 0, unroll=True)
 
 
 def final_kernel(places, n_given, share, tile, meta, ccols, *refs):
@@ -235,10 +254,10 @@
         mixed[:, at] = (coarse[:, at].astype(F32) + made).astype(BF)
         return 0
 
-    lax.fori_loop(0, clusters // tile, mix, 0, unroll=2)
+    lax.fori_loop(0, clusters // tile, mix, 0, unroll=True)
     sensors = state.shape[1]
     channels = state.shape[0]
-    width = 2 * tile
+    width = 4 * tile
 
     def step(c, _):
         at = pl.ds(pl.multiple_of(c * width, width), width)
@@ -260,7 +279,7 @@
         out[:, at] = jnp.where(spot < meta[1], new, 0.0).astype(BF)
         return 0
 
-    lax.fori_loop(0, sensors // width, step, 0)
+    lax.fori_loop(0, sensors // width, step, 0, unroll=True)
 
 
 def flip(n, b):
@@ -271,27 +290,18 @@
     return lax.ppermute(array, axis, flip(lax.axis_size(axis), b))
 
 
-def exchange(array):
-    n = lax.axis_size("feat")
-    if n != 4:
-        return [array] + [swap(array, "feat", k) for k in range(1, n)]
-    far = swap(array, "feat", 2)
-    near = swap(array, "feat", 1)
-    inner = lax.ppermute(array, "feat", [(1, 2), (2, 1)])
-    return [array, near, far, inner]
-
-
-def gather_dom(block):
+def gather_dom(block, *ready):
     n = lax.axis_size("dom")
     rows = block.shape[0]
-    send = lambda x, b: lax.ppermute(x, "dom", flip(n, b))
+    send = lambda x, b: swap(x, "dom", b)
     if n != 8:
         every = lax.all_gather(block, "dom", axis=0, tiled=True)
-        return [every], [(0, b * rows, 0, rows, b, True) for b in range(n)]
+        return [every], [(0, b * rows, 0, rows, b, True) for b in range(n)], *ready
     half = rows // 2
     beside = send(block, 2)
     behind = send(block, 4)
     core = send(block, 1)
+    (beside, behind), ready = lax.optimization_barrier(((beside, behind), ready))
     top = send(beside[:half], 4)
     bottom = send(behind[half:], 2)
     other = send(jnp.concatenate([beside, behind, top, bottom], axis=0), 1)
@@ -306,7 +316,7 @@
         (6, rows, 0, rows, 5, False),
         (6, 2 * rows, 0, rows, 7, False),
     ]
-    return [block, core, beside, behind, top, bottom, other], places
+    return [block, core, beside, behind, top, bottom, other], places, *ready
 
 
 def body(
@@ -348,22 +358,20 @@
         flops=2 * channels * rows * clusters * 3,
         bytes_accessed=8 * channels * rows,
     )
-    sent, state_late = lax.optimization_barrier((sent, state))
-    blocks = exchange(state_late)
+    line = n_feat == 4
+    sent, state_far = lax.optimization_barrier((sent, state))
+    far = [swap(state_far, "feat", k) for k in range(2, n_feat) if k == 2 or not line]
     pieces = call(
         pair_kernel,
         [sds((channels + COUNT_ROWS, share), F32)]
         + [sds((channels + COUNT_ROWS, share), BF)] * (n_dom // 2 - 1),
-        [kept, lax.ppermute(sent, "dom", flip(n_dom, 1))],
-    )
-    pieces, source_emb, target_emb, w_gates, adj_tiles, w_input, coarse_cols = (
-        lax.optimization_barrier(
-            (pieces, source_emb, target_emb, w_gates, adj_tiles, w_input, coarse_cols)
-        )
-    )
-    arrived = [pieces[0]] + [
-        lax.ppermute(pieces[e], "dom", flip(n_dom, 2 * e)) for e in range(1, n_dom // 2)
-    ]
+        [kept, swap(sent, "dom", 1)],
+    )
+    pieces, state_near, source_emb, target_emb = lax.optimization_barrier(
+        (pieces, state, source_emb, target_emb)
+    )
+    arrived = [pieces[0]] + [swap(pieces[e], "dom", 2 * e) for e in range(1, n_dom // 2)]
+    blocks = [state, swap(state_near, "feat", 1)] + far
     pad = [(0, 0), (0, -source_emb.shape[1] % 16), (0, 0)]
     source = lax.dynamic_slice_in_dim(source_emb, me * share, share, 2)
     weights = call(
@@ -372,56 +380,60 @@
         [jnp.pad(source, pad), jnp.pad(target_emb, pad)],
         flops=source.shape[0] * clusters * share * 4000,
     )
-    w = jnp.transpose(w_gates, (2, 0, 1, 3)).reshape(4, outputs, total)
-    w_own, w_coarse = w[:3], w[3]
-    band, edge_last, edge_first = call(
-        band_kernel,
-        [sds((tiles, 3 * tile, tile), BF)] + [sds((3 * tile // 2, 2 * tile), BF)] * 2,
-        [meta, adj_cols.reshape(-1), adj_tiles],
-        [pltpu.VMEM((3 * tile, tile), F32)],
-        flops=10**9,
-    )
-    terms = jnp.concatenate(
-        [w_input.reshape(outputs, -1).astype(F32), bias.reshape(outputs, 1)], axis=1
-    )
-    coarse_at = coarse_cols.reshape(-1)
-    ready = (weights, w_own, w_coarse, band, edge_last, edge_first, terms, coarse_at)
-    arrived, ready = lax.optimization_barrier((arrived, ready))
-    weights, w_own, w_coarse, band, edge_last, edge_first, terms, coarse_at = ready
+    arrived, weights = lax.optimization_barrier((arrived, weights))
     pooled, values = call(
         functools.partial(pool_kernel, n_dom // 2),
         [sds((channels, share), F32), sds((channels, share), BF)],
         [w_value] + arrived,
     )
     every_value = lax.all_gather(values, "dom", axis=0)
-    if n_feat == 4:
-        every_value, blocks[2] = lax.optimization_barrier((every_value, blocks[2]))
-        blocks.append(lax.ppermute(blocks[2], "feat", [(1, 0), (2, 3)]))
     own_coarse = call(attend_kernel, sds((channels, share), BF), [every_value, weights, pooled])
+
+    own_coarse, w_gates, adj_tiles, w_input, coarse_cols = lax.optimization_barrier(
+        (own_coarse, w_gates, adj_tiles, w_input, coarse_cols)
+    )
     coarse_blocks = [own_coarse] + [swap(own_coarse, "feat", k) for k in range(1, n_feat)]
-    coarse_blocks, blocks = lax.optimization_barrier((coarse_blocks, blocks))
+    if line:
+        own_coarse, blocks[1:3], state_inner = lax.optimization_barrier(
+            (own_coarse, blocks[1:3], state)
+        )
+        outer = lax.ppermute(blocks[2], "feat", [(1, 0), (2, 3)])
+        blocks += [lax.ppermute(state_inner, "feat", [(1, 2), (2, 1)]), outer]
+    w = jnp.transpose(w_gates, (2, 0, 1, 3)).reshape(4, outputs, total)
+    w_own, w_coarse = w[:3], w[3]
+    edge_shape = sds((3 * tile // 2, 2 * tile), BF)
+    terms = jnp.concatenate(
+        [w_input.reshape(outputs, -1).astype(F32), bias.reshape(outputs, 1)], axis=1
+    )
+    band, edge_last, edge_first, terms = call(
+        band_kernel,
+        [sds((tiles, 3 * tile, tile), BF), edge_shape, edge_shape, sds(terms.shape, F32)],
+        [meta, adj_cols.reshape(-1), adj_tiles, terms],
+        [pltpu.VMEM((3 * tile, tile), F32)],
+        flops=10**9,
+    )
+    coarse_at = coarse_cols.reshape(-1)
+    ready = (w_own, w_coarse, band, terms, coarse_at)
+    coarse_blocks, ready = lax.optimization_barrier((coarse_blocks, ready))
+    w_own, w_coarse, band, terms, coarse_at = ready
+    message = sds((total + 3 * tile // 2, 2 * tile), BF)
+    last, first = call(
+        functools.partial(edge_kernel, n_feat, tile),
+        [message, message],
+        [meta] + blocks + [edge_last, edge_first],
+    )
     folded = call(
         functools.partial(fold_kernel, n_feat),
         sds((outputs, share), BF),
         [meta] + coarse_blocks + [w_coarse],
         [pltpu.VMEM((total, share), BF)],
     )
-    given, places = gather_dom(folded)
-
+    given, places, last, first = gather_dom(folded, last, first)
     up = [(i, (i + 1) % n_dom) for i in range(n_dom)]
-    down = [(j, i) for i, j in up]
-    keep = (jnp.arange(rows, dtype=jnp.int32) < valid_rows[0]).astype(BF)
-
-    def edge_of(lanes, weights):
-        ends = [x[:, lanes] for x in blocks]
-        if n_feat == 4:
-            ends[3:] = [jnp.where((feat == 0) | (feat == 3), ends[4], ends[3])]
-        return jnp.concatenate([x * keep[lanes] for x in ends] + [weights], axis=0)
-
-    left = lax.ppermute(edge_of(slice(rows - 2 * tile, rows), edge_last), "dom", up)
-    right = lax.ppermute(edge_of(slice(0, 2 * tile), edge_first), "dom", down)
+    left = lax.ppermute(last, "dom", up)
+    right = lax.ppermute(first, "dom", [(j, i) for i, j in up])
     ext, one = call(
-        functools.partial(hop_one_kernel, len(blocks), tile),
+        functools.partial(hop_one_kernel, n_feat, tile),
         [sds((total, rows + 4 * tile), BF), sds((total, rows + 2 * tile), BF)],
         [meta] + blocks + [left, right, band],
         flops=2 * total * rows * kb * tile,
@@ -434,7 +446,6 @@
         flops=2 * total * rows * (kb * tile + 3 * outputs),
         bytes_accessed=8 * total * rows,
     )
-
     return call(
         functools.partial(final_kernel, places, len(given), share, tile),
         sds((channels, rows), BF),

time: 99.6 us -> 80.2 us (0.81)
  other arithmetic: 6.09 us -> 0.13 us
  local copies, waits for them, and re-layouts: 10.1 us -> 4.56 us
  Pallas kernels: 28.8 us -> 23.7 us
  waiting for transfers between devices: 20.4 us -> 16.9 us
  starting transfers between devices: 22.7 us -> 24.4 us
    ppermute x5 -> x15, starting transfers between devices: 11.1 us -> 19.8 us  [swap(): return lax.ppermute(array, axis, flip(lax.axis_size(axis), b))]
    ppermute x5 -> x15, waiting for transfers between devices: 11.9 us -> 4.18 us  [swap(): return lax.ppermute(array, axis, flip(lax.axis_size(axis), b))]
    ppermute x14 -> x4, starting transfers between devices: 11.6 us -> 4.62 us  [the longest x1 2.64 us: body(): right = lax.ppermute(first, 'dom', [(j, i) for i, j in up])]
    pallas_call x10 -> x11, Pallas kernels: 28.8 us -> 23.7 us  [call(): pl.pallas_call(kernel, out_shape=outs, in_specs=specs, out_specs=jax.tree...]
    unnamed x4 -> x0, other arithmetic: 4.53 us -> none
    ppermute x14 -> x4, waiting for transfers between devices: 8.51 us -> 12.8 us  [the longest x1 6.54 us: body(): outer = lax.ppermute(blocks[2], 'feat', [(1, 0), (2, 3)])]
    unnamed x58 -> x30, local copies, waits for them, and re-layouts: 4.75 us -> 2.43 us
    optimization_barrier x5 -> x4, local copies, waits for them, and re-layouts: 2.03 us -> 0.61 us  [the longest x2 0.4 us: body(): lax.optimization_barrier((own_coarse, w_gates, adj_tiles, w_input, coarse...]
  transfers between devices with their start and end apart: 19 -> 19, of which waited for: 3 -> 5; matrix products, arithmetic and copies ran while one was open for 12% -> 3% of each run, Pallas kernels for 14% -> 16%
where the time goes in v3:
time: 80.2 us; the launch traced here: 79.8 us
  starting transfers between devices  24.4 us (30%)
  Pallas kernels  23.7 us (30%)
  waiting for transfers between devices  16.9 us (21%)
  blocking collectives  9.01 us (11%)
  local copies, waits for them, and re-layouts  4.56 us (6%)
  between operations  1.06 us (1%)
    pallas_call x11, Pallas kernels, call(): pl.pallas_call(kernel, out_shape=outs, in_specs=specs, out_specs=jax.tree...  23.7 us
    ppermute x15, starting transfers between devices, swap(): return lax.ppermute(array, axis, flip(lax.axis_size(axis), b))  19.8 us
    all_gather x1, blocking collectives, body(): every_value = lax.all_gather(values, 'dom', axis=0)  9.01 us
    ppermute x1, waiting for transfers between devices, body(): outer = lax.ppermute(blocks[2], 'feat', [(1, 0), (2, 3)])  6.54 us
    ppermute x1, waiting for transfers between devices, body(): left = lax.ppermute(last, 'dom', up)  6.21 us
    ppermute x15, waiting for transfers between devices, swap(): return lax.ppermute(array, axis, flip(lax.axis_size(axis), b))  4.18 us
    ppermute x1, starting transfers between devices, body(): right = lax.ppermute(first, 'dom', [(j, i) for i, j in up])  2.64 us
    unnamed x30, local copies, waits for them, and re-layouts  2.43 us
  transfers between devices with their start and end apart: 19, of which 5 were waited for; matrix products, arithmetic and copies ran while one was open for 3% of the time, Pallas kernels for 16%

profile of v3, /device:TPU:0, one launch (start us, length us, event | category | flops | bytes accessed | tf_op | source)
XLA Modules:
  0.0 79.8 jit_solution(6571425555390223072)
XLA Ops:
  0.7 0.1 pad_add_fusion.meta
  0.7 0.7 copy-done.4
  1.4 3.9 %shard_map.136 = (f32[4,144,256]{2,1,0:T(8,128)S(1)}, bf16[4,144,256]{2,1,0:T(8,128)(2,1)S(1)}) custom-call(s32[3]{0:T(128)S(1)} %pad_add_fusion.meta, bf16[128,2048]{1,0:T(8,128)(2,1)} %refs_12_.1, s32[1,2048]{1,0:T(1,128)S(1)} %bitcast.21), custom_call_target="tpu_custom_call" | custom-call | flops 3221225472 | bytes 2097152 | tf_op jit(solution)/shard_map/pallas_call | solution.py:19
  5.4 0.5 collective-permute-start
  5.9 3.7 %collective-permute-start.11 = (bf16[128,2048]{1,0:T(8,128)(2,1)}, bf16[128,2048]{1,0:T(8,128)(2,1)S(1)}, u32[]{:S(2)}, u32[]{:S(2)}) collective-permute-start(bf16[128,2048]{1,0:T(8,128)(2,1)} %refs_12_.1), channel_id=1, source_target_pairs={{0,2},{1,3},{2,0},{3,1},{4,6},{5,7},{6,4},{7,5},{8,10},{9,11},{10,... | collective-permute-start | bytes 1572872 | tf_op jit(solution)/shard_map/ppermute | solution.py:290
  9.6 0.1 copy.38
  9.6 0.1 reshape.16.cols
  9.7 0.0 collective-permute-done.arrived
  9.8 0.1 shard_map.137
  9.8 0.1 copy.35
  10.0 1.6 %collective-permute-start.10 = (bf16[128,2048]{1,0:T(8,128)(2,1)}, bf16[128,2048]{1,0:T(8,128)(2,1)S(1)}, u32[]{:S(2)}, u32[]{:S(2)}) collective-permute-start(bf16[128,2048]{1,0:T(8,128)(2,1)} %refs_12_.1), channel_id=1, source_target_pairs={{0,1},{1,0},{2,3},{3,2},{4,5},{5,4},{6,7},{7,6},{8,9},{9,8},{10,11... | collective-permute-start | bytes 1572872 | tf_op jit(solution)/shard_map/ppermute | solution.py:290
  11.6 0.1 copy.36
  11.8 0.0 copy-start.1
  11.8 1.6 %collective-permute-start.1 = (bf16[144,256]{1,0:T(8,128)(2,1)S(1)}, bf16[144,256]{1,0:T(8,128)(2,1)S(1)}, u32[]{:S(2)}, u32[]{:S(2)}) collective-permute-start(bf16[144,256]{1,0:T(8,128)(2,1)S(1)} %get-tuple-element.64), channel_id=1, source_target_pairs={{0,8},{4,12},{8,0},{12,4},{16,24},{20,28},{24,16},{28,20},{1,9},{5... | collective-permute-start | bytes 221192 | tf_op jit(solution)/shard_map/ppermute | solution.py:290
  13.3 1.5 %collective-permute-start.2 = (bf16[144,256]{1,0:T(8,128)(2,1)S(1)}, bf16[144,256]{1,0:T(8,128)(2,1)S(1)}, u32[]{:S(2)}, u32[]{:S(2)}) collective-permute-start(bf16[144,256]{1,0:T(8,128)(2,1)S(1)} %get-tuple-element.65), channel_id=1, source_target_pairs={{0,16},{4,20},{8,24},{12,28},{16,0},{20,4},{24,8},{28,12},{1,17},{... | collective-permute-start | bytes 221192 | tf_op jit(solution)/shard_map/ppermute | solution.py:290
  14.8 0.5 collective-permute-start.3
  15.3 2.2 %shard_map.138.weights = bf16[2,2048,256]{2,1,0:T(8,128)(2,1)S(1)} custom-call(f32[2,16,256]{2,1,0:T(8,128)S(1)} %pad.8.source, f32[2,16,2048]{2,1,0:T(8,128)S(1)} %pad.9.target), custom_call_target="tpu_custom_call" | custom-call | flops 4194304000 | tf_op jit(solution)/shard_map/pallas_call | solution.py:19
  17.6 0.0 collective-permute-done.1.refs_1_
  17.6 0.1 collective-permute-done.2.refs_2_
  17.7 2.4 %collective-permute-done.3.refs_3_ = bf16[144,256]{1,0:T(8,128)(2,1)S(1)} collective-permute-done((bf16[144,256]{1,0:T(8,128)(2,1)S(1)}, bf16[144,256]{1,0:T(8,128)(2,1)S(1)}, u32[]{:S(2)}, u32[]{:S(2)}) %collective-permute-start.3) | collective-permute-done | bytes 73760 | tf_op jit(solution)/shard_map/ppermute | solution.py:290
  20.1 0.2 shard_map.139
  20.3 0.0 copy-start.7
  20.4 9.0 %all-gather = bf16[1024,256]{1,0:T(8,128)(2,1)S(1)} all-gather(bf16[128,256]{1,0:T(8,128)(2,1)S(1)} %get-tuple-element.73), channel_id=2, replica_groups=mesh['dom'=8,'feat'=4] {'dom'}, dimensions={0}, use_global_device_ids=true | all-gather | bytes 589824 | tf_op jit(solution)/shard_map/all_gather | solution.py:389
  29.4 0.5 shard_map.140.refs_0_
  29.9 0.3 copy.45
  30.2 0.0 copy-start.12
  30.2 0.0 copy-start.13
  30.2 1.1 %slice.21 = bf16[3,3,128,512]{3,2,1,0:T(8,128)(2,1)} slice(bf16[4,3,128,512]{3,2,1,0:T(8,128)(2,1)S(1)} %bitcast.23), slice={[0:3], [0:3], [0:128], [0:512]} | slice | bytes 2359296 | tf_op jit(solution)/shard_map/slice | solution.py:403
  31.4 0.5 collective-permute-start.4
  31.9 1.3 %collective-permute-start.5 = (bf16[128,256]{1,0:T(8,128)(2,1)S(1)}, bf16[128,256]{1,0:T(8,128)(2,1)S(1)}, u32[]{:S(2)}, u32[]{:S(2)}) collective-permute-start(bf16[128,256]{1,0:T(8,128)(2,1)S(1)} %shard_map.140.refs_0_), channel_id=1, source_target_pairs={{0,2},{1,3},{2,0},{3,1},{4,6},{5,7},{6,4},{7,5},{8,10},{9,11},{10,... | collective-permute-start | bytes 196616 | tf_op jit(solution)/shard_map/ppermute | solution.py:290
  33.2 2.6 %collective-permute-start.6 = (bf16[128,256]{1,0:T(8,128)(2,1)S(1)}, bf16[128,256]{1,0:T(8,128)(2,1)S(1)}, u32[]{:S(2)}, u32[]{:S(2)}) collective-permute-start(bf16[128,256]{1,0:T(8,128)(2,1)S(1)} %shard_map.140.refs_0_), channel_id=1, source_target_pairs={{0,3},{1,2},{2,1},{3,0},{4,7},{5,6},{6,5},{7,4},{8,11},{9,10},{10,... | collective-permute-start | bytes 196616 | tf_op jit(solution)/shard_map/ppermute | solution.py:290
  35.8 0.0 collective-permute-done.10.refs_1_
  35.8 0.7 collective-permute-start.12
  36.5 1.3 %collective-permute-start.13 = (bf16[128,2048]{1,0:T(8,128)(2,1)S(1)}, bf16[128,2048]{1,0:T(8,128)(2,1)S(1)}, u32[]{:S(2)}, u32[]{:S(2)}) collective-permute-start(bf16[128,2048]{1,0:T(8,128)(2,1)S(1)} %collective-permute-done.11.refs_2_), channel_id=1, source_target_pairs={{1,0},{2,3},{5,4},{6,7},{9,8},{10,11},{13,12},{14,15},{17,16},{18,... | collective-permute-start | bytes 1572872 | tf_op jit(solution)/shard_map/ppermute | solution.py:400
  37.9 0.1 copy.40.terms
  38.0 0.1 copy.41
  38.1 0.1 reshape.18.ccols
  38.2 0.0 copy-start.2
  38.2 1.6 %copy-done.2 = bf16[16,4,128,128]{3,2,1,0:T(8,128)(2,1)S(1)} copy-done((bf16[16,4,128,128]{3,2,1,0:T(8,128)(2,1)S(1)}, bf16[16,4,128,128]{3,2,1,0:T(8,128)(2,1)}, u32[]{:S(2)}) %copy-start.2) | copy-done | bytes 2097176
  39.8 1.3 %shard_map.141 = (bf16[16,384,128]{2,1,0:T(8,128)(2,1)S(1)}, bf16[192,256]{1,0:T(8,128)(2,1)S(1)}, bf16[192,256]{1,0:T(8,128)(2,1)S(1)}, f32[384,3]{1,0:T(8,128)S(1)}) custom-call(s32[3]{0:T(128)S(1)} %pad_add_fusion.meta, s32[64]{0:T(128)S(1)} %reshape.16.cols, bf16[16,4,128,128]{3,2,1,0:T(8,128)(2,1)S(1)} %copy-done.2, f32[384,3]{1,0:T(8,128)S(1)} %copy.40.terms), custom_call_target="tpu_custom_call" | custom-call | flops 1000000000 | tf_op jit(solution)/shard_map/pallas_call | solution.py:19
  41.1 0.0 collective-permute-done.4.refs_1_
  41.1 0.0 collective-permute-done.5.refs_2_
  41.2 0.8 %shard_map.142.refs_0_ = bf16[384,256]{1,0:T(8,128)(2,1)S(1)} custom-call(s32[3]{0:T(128)S(1)} %pad_add_fusion.meta, bf16[128,256]{1,0:T(8,128)(2,1)S(1)} %shard_map.140.refs_0_, bf16[128,256]{1,0:T(8,128)(2,1)S(1)} %collective-permute-done.4.refs_1_, bf16[128,256]{1,0:T(8,128)(2,1)S(1)} %collective-permute-done.5.refs_2_, ...), custom_call_target="tpu_custom_call" | custom-call | tf_op jit(solution)/shard_map/pallas_call | solution.py:19
  42.0 1.6 %collective-permute-start.8 = (bf16[384,256]{1,0:T(8,128)(2,1)S(1)}, bf16[384,256]{1,0:T(8,128)(2,1)S(1)}, u32[]{:S(2)}, u32[]{:S(2)}) collective-permute-start(bf16[384,256]{1,0:T(8,128)(2,1)S(1)} %shard_map.142.refs_0_), channel_id=1, source_target_pairs={{0,8},{4,12},{8,0},{12,4},{16,24},{20,28},{24,16},{28,20},{1,9},{5... | collective-permute-start | bytes 589832 | tf_op jit(solution)/shard_map/ppermute | solution.py:290
  43.6 1.6 %collective-permute-start.9 = (bf16[384,256]{1,0:T(8,128)(2,1)S(1)}, bf16[384,256]{1,0:T(8,128)(2,1)S(1)}, u32[]{:S(2)}, u32[]{:S(2)}) collective-permute-start(bf16[384,256]{1,0:T(8,128)(2,1)S(1)} %shard_map.142.refs_0_), channel_id=1, source_target_pairs={{0,16},{4,20},{8,24},{12,28},{16,0},{20,4},{24,8},{28,12},{1,17},{... | collective-permute-start | bytes 589832 | tf_op jit(solution)/shard_map/ppermute | solution.py:290
  45.2 0.0 collective-permute-done.12.refs_3_
  45.2 6.5 %collective-permute-done.13.refs_4_ = bf16[128,2048]{1,0:T(8,128)(2,1)S(1)} collective-permute-done((bf16[128,2048]{1,0:T(8,128)(2,1)S(1)}, bf16[128,2048]{1,0:T(8,128)(2,1)S(1)}, u32[]{:S(2)}, u32[]{:S(2)}) %collective-permute-start.13) | collective-permute-done | bytes 524320 | tf_op jit(solution)/shard_map/ppermute | solution.py:400
  51.8 1.1 %shard_map.143 = (bf16[704,256]{1,0:T(8,128)(2,1)S(1)}, bf16[704,256]{1,0:T(8,128)(2,1)S(1)}) custom-call(s32[3]{0:T(128)S(1)} %pad_add_fusion.meta, bf16[128,2048]{1,0:T(8,128)(2,1)} %refs_12_.1, bf16[128,2048]{1,0:T(8,128)(2,1)S(1)} %collective-permute-done.10.refs_1_, bf16[128,2048]{1,0:T(8,128)(2,1)S(1)} %collective-permute-done.11.refs_2_, ...), custom_call_target="tpu_custom_call" | custom-call | tf_op jit(solution)/shard_map/pallas_call | solution.py:19
  52.9 0.0 collective-permute-done.9.refs_3_
  52.9 1.6 %collective-permute-start.14 = (bf16[192,256]{1,0:T(8,128)(2,1)S(1)}, bf16[192,256]{1,0:T(8,128)(2,1)S(1)}, u32[]{:S(2)}, u32[]{:S(2)}) collective-permute-start(bf16[192,256]{1,0:T(8,128)(2,1)S(1)} %slice.19), channel_id=1, source_target_pairs={{0,16},{4,20},{8,24},{12,28},{16,0},{20,4},{24,8},{28,12},{1,17},{... | collective-permute-start | bytes 294920 | tf_op jit(solution)/shard_map/ppermute | solution.py:290
  54.5 0.6 collective-permute-start.15
  55.1 0.0 collective-permute-start.17
  55.1 2.6 %collective-permute-start.18 = (bf16[704,256]{1,0:T(8,128)(2,1)S(1)}, bf16[704,256]{1,0:T(8,128)(2,1)S(1)}, u32[]{:S(2)}, u32[]{:S(2)}) collective-permute-start(bf16[704,256]{1,0:T(8,128)(2,1)S(1)} %get-tuple-element.101), channel_id=1, source_target_pairs={{4,0},{8,4},{12,8},{16,12},{20,16},{24,20},{28,24},{0,28},{5,1},{9... | collective-permute-start | bytes 1081352 | tf_op jit(solution)/shard_map/ppermute | solution.py:434
  57.7 0.0 collective-permute-done.14.refs_4_
  57.7 1.6 %collective-permute-done.15.refs_5_ = bf16[192,256]{1,0:T(8,128)(2,1)S(1)} collective-permute-done((bf16[192,256]{1,0:T(8,128)(2,1)S(1)}, bf16[192,256]{1,0:T(8,128)(2,1)S(1)}, u32[]{:S(2)}, u32[]{:S(2)}) %collective-permute-start.15) | collective-permute-done | bytes 98336 | tf_op jit(solution)/shard_map/ppermute | solution.py:290
  59.4 0.1 collective-permute-start.16
  59.5 0.5 collective-permute-start.7
  60.0 6.2 %collective-permute-done.17.refs_5_ = bf16[704,256]{1,0:T(8,128)(2,1)S(1)} collective-permute-done((bf16[704,256]{1,0:T(8,128)(2,1)S(1)}, bf16[704,256]{1,0:T(8,128)(2,1)S(1)}, u32[]{:S(2)}, u32[]{:S(2)}) %collective-permute-start.17) | collective-permute-done | bytes 360480 | tf_op jit(solution)/shard_map/ppermute | solution.py:433
  66.2 2.7 %shard_map.144 = (bf16[512,2560]{1,0:T(8,128)(2,1)S(1)}, bf16[512,2304]{1,0:T(8,128)(2,1)S(1)}) custom-call(s32[3]{0:T(128)S(1)} %pad_add_fusion.meta, bf16[128,2048]{1,0:T(8,128)(2,1)} %refs_12_.1, bf16[128,2048]{1,0:T(8,128)(2,1)S(1)} %collective-permute-done.10.refs_1_, bf16[128,2048]{1,0:T(8,128)(2,1)S(1)} %collective-permute-done.11.refs_2_, ...), custom_call_target="tpu_custom_call" | custom-call | flops 1073741824 | bytes 8388608 | tf_op jit(solution)/shard_map/pallas_call | solution.py:19
  68.9 0.0 copy-start.3
  68.9 0.0 copy-start.5
  68.9 0.0 copy-start.6
  69.0 3.7 %shard_map.145.refs_9_ = f32[384,2048]{1,0:T(8,128)S(1)} custom-call(bf16[512,2560]{1,0:T(8,128)(2,1)S(1)} %get-tuple-element.103.ext, bf16[512,2304]{1,0:T(8,128)(2,1)S(1)} %get-tuple-element.104.one, bf16[16,384,128]{2,1,0:T(8,128)(2,1)S(1)} %get-tuple-element.102.refs_7_.band, bf16[3,384,512]{2,1,0:T(8,128)(2,1)S(1)} %bitcast.20), custom_call_target="tpu_custom_call" | custom-call | flops 3489660928 | bytes 8388608 | tf_op jit(solution)/shard_map/pallas_call | solution.py:19
  72.7 7.1 %shard_map.146 = bf16[128,2048]{1,0:T(8,128)(2,1)} custom-call(s32[3]{0:T(128)S(1)} %pad_add_fusion.meta, s32[32]{0:T(128)S(1)} %reshape.18.ccols, bf16[384,256]{1,0:T(8,128)(2,1)S(1)} %shard_map.142.refs_0_, bf16[384,256]{1,0:T(8,128)(2,1)S(1)} %collective-permute-done.7.refs_1_, bf16[384,256]{1,0:T(8,128)(2,1)S(1)} %collective-permute-done.8.refs_2_, ...), custom_call_target="tpu_custom_call" | custom-call | flops 3221225472 | bytes 6291456 | tf_op jit(solution)/shard_map/pallas_call | solution.py:19
  (34 shorter events, 0.2 us)
Async XLA Ops:
  0.7 0.7 copy-start.4
  1.4 8.1 %copy-start.11 = (f32[3,128]{1,0:T(4,128)S(1)}, f32[3,128]{1,0:T(4,128)}, u32[]{:S(2)}) copy-start(f32[3,128]{1,0:T(4,128)} %param.22) | copy-start | bytes 4612
  1.4 8.1 %copy-start.10 = (s32[16,4]{0,1:T(4,128)S(1)}, s32[16,4]{0,1:T(4,128)}, u32[]{:S(2)}) copy-start(s32[16,4]{0,1:T(4,128)} %param.17) | copy-start | bytes 772
  1.4 8.4 %copy-start.8 = (f32[2,10,2048]{2,0,1:T(2,128)S(1)}, f32[2,10,2048]{2,0,1:T(2,128)}, u32[]{:S(2)}) copy-start(f32[2,10,2048]{2,0,1:T(2,128)} %param.24) | copy-start | bytes 491524
  1.4 10.2 %copy-start.9 = (f32[2,10,2048]{2,0,1:T(2,128)S(1)}, f32[2,10,2048]{2,0,1:T(2,128)}, u32[]{:S(2)}) copy-start(f32[2,10,2048]{2,0,1:T(2,128)} %param.25) | copy-start | bytes 491524
  5.4 4.4 %collective-permute-start = (bf16[4,144,256]{2,1,0:T(8,128)(2,1)S(1)}, bf16[4,144,256]{2,1,0:T(8,128)(2,1)S(1)}, u32[]{:S(2)}, u32[]{:S(2)}) collective-permute-start(bf16[4,144,256]{2,1,0:T(8,128)(2,1)S(1)} %get-tuple-element.58), channel_id=1, source_target_pairs={{0,4},{4,0},{8,12},{12,8},{16,20},{20,16},{24,28},{28,24},{1,5},{5... | collective-permute-start | bytes 884744 | tf_op jit(solution)/shard_map/ppermute | solution.py:290
  5.9 29.9 %collective-permute-start.11 = (bf16[128,2048]{1,0:T(8,128)(2,1)}, bf16[128,2048]{1,0:T(8,128)(2,1)S(1)}, u32[]{:S(2)}, u32[]{:S(2)}) collective-permute-start(bf16[128,2048]{1,0:T(8,128)(2,1)} %refs_12_.1), channel_id=1, source_target_pairs={{0,2},{1,3},{2,0},{3,1},{4,6},{5,7},{6,4},{7,5},{8,10},{9,11},{10,... | collective-permute-start | bytes 1572872 | tf_op jit(solution)/shard_map/ppermute | solution.py:290
  10.0 25.9 %collective-permute-start.10 = (bf16[128,2048]{1,0:T(8,128)(2,1)}, bf16[128,2048]{1,0:T(8,128)(2,1)S(1)}, u32[]{:S(2)}, u32[]{:S(2)}) collective-permute-start(bf16[128,2048]{1,0:T(8,128)(2,1)} %refs_12_.1), channel_id=1, source_target_pairs={{0,1},{1,0},{2,3},{3,2},{4,5},{5,4},{6,7},{7,6},{8,9},{9,8},{10,11... | collective-permute-start | bytes 1572872 | tf_op jit(solution)/shard_map/ppermute | solution.py:290
  11.8 8.3 %copy-start.1 = (bf16[2,64,64]{2,1,0:T(8,128)(2,1)S(1)}, bf16[2,64,64]{2,1,0:T(8,128)(2,1)}, u32[]{:S(2)}) copy-start(bf16[2,64,64]{2,1,0:T(8,128)(2,1)} %w_value.1) | copy-start | bytes 49156
  11.8 5.8 %collective-permute-start.1 = (bf16[144,256]{1,0:T(8,128)(2,1)S(1)}, bf16[144,256]{1,0:T(8,128)(2,1)S(1)}, u32[]{:S(2)}, u32[]{:S(2)}) collective-permute-start(bf16[144,256]{1,0:T(8,128)(2,1)S(1)} %get-tuple-element.64), channel_id=1, source_target_pairs={{0,8},{4,12},{8,0},{12,4},{16,24},{20,28},{24,16},{28,20},{1,9},{5... | collective-permute-start | bytes 221192 | tf_op jit(solution)/shard_map/ppermute | solution.py:290
  13.3 4.4 %collective-permute-start.2 = (bf16[144,256]{1,0:T(8,128)(2,1)S(1)}, bf16[144,256]{1,0:T(8,128)(2,1)S(1)}, u32[]{:S(2)}, u32[]{:S(2)}) collective-permute-start(bf16[144,256]{1,0:T(8,128)(2,1)S(1)} %get-tuple-element.65), channel_id=1, source_target_pairs={{0,16},{4,20},{8,24},{12,28},{16,0},{20,4},{24,8},{28,12},{1,17},{... | collective-permute-start | bytes 221192 | tf_op jit(solution)/shard_map/ppermute | solution.py:290
  14.8 5.3 %collective-permute-start.3 = (bf16[144,256]{1,0:T(8,128)(2,1)S(1)}, bf16[144,256]{1,0:T(8,128)(2,1)S(1)}, u32[]{:S(2)}, u32[]{:S(2)}) collective-permute-start(bf16[144,256]{1,0:T(8,128)(2,1)S(1)} %get-tuple-element.66), channel_id=1, source_target_pairs={{0,24},{4,28},{8,16},{12,20},{16,8},{20,12},{24,0},{28,4},{1,25},{... | collective-permute-start | bytes 221192 | tf_op jit(solution)/shard_map/ppermute | solution.py:290
  20.3 9.5 %copy-start.7 = (bf16[3,128,4,512]{3,2,1,0:T(4,128)(2,1)S(1)}, bf16[3,128,4,512]{3,2,1,0:T(4,128)(2,1)}, u32[]{:S(2)}) copy-start(bf16[3,128,4,512]{3,2,1,0:T(4,128)(2,1)} %param.20) | copy-start | bytes 4718596
  30.2 7.6 %copy-start.12 = (bf16[3,128,2]{1,2,0:T(2,128)(2,1)S(1)}, bf16[3,128,2]{1,2,0:T(2,128)(2,1)}, u32[]{:S(2)}) copy-start(bf16[3,128,2]{1,2,0:T(2,128)(2,1)} %param.21) | copy-start | bytes 4612
  30.2 7.8 %copy-start.13 = (s32[16,2]{0,1:T(2,128)S(1)}, s32[16,2]{0,1:T(2,128)}, u32[]{:S(2)}) copy-start(s32[16,2]{0,1:T(2,128)} %param.27) | copy-start | bytes 388
  31.4 9.8 %collective-permute-start.4 = (bf16[128,256]{1,0:T(8,128)(2,1)S(1)}, bf16[128,256]{1,0:T(8,128)(2,1)S(1)}, u32[]{:S(2)}, u32[]{:S(2)}) collective-permute-start(bf16[128,256]{1,0:T(8,128)(2,1)S(1)} %shard_map.140.refs_0_), channel_id=1, source_target_pairs={{0,1},{1,0},{2,3},{3,2},{4,5},{5,4},{6,7},{7,6},{8,9},{9,8},{10,11... | collective-permute-start | bytes 196616 | tf_op jit(solution)/shard_map/ppermute | solution.py:290
  31.9 9.3 %collective-permute-start.5 = (bf16[128,256]{1,0:T(8,128)(2,1)S(1)}, bf16[128,256]{1,0:T(8,128)(2,1)S(1)}, u32[]{:S(2)}, u32[]{:S(2)}) collective-permute-start(bf16[128,256]{1,0:T(8,128)(2,1)S(1)} %shard_map.140.refs_0_), channel_id=1, source_target_pairs={{0,2},{1,3},{2,0},{3,1},{4,6},{5,7},{6,4},{7,5},{8,10},{9,11},{10,... | collective-permute-start | bytes 196616 | tf_op jit(solution)/shard_map/ppermute | solution.py:290
  33.2 8.0 %collective-permute-start.6 = (bf16[128,256]{1,0:T(8,128)(2,1)S(1)}, bf16[128,256]{1,0:T(8,128)(2,1)S(1)}, u32[]{:S(2)}, u32[]{:S(2)}) collective-permute-start(bf16[128,256]{1,0:T(8,128)(2,1)S(1)} %shard_map.140.refs_0_), channel_id=1, source_target_pairs={{0,3},{1,2},{2,1},{3,0},{4,7},{5,6},{6,5},{7,4},{8,11},{9,10},{10,... | collective-permute-start | bytes 196616 | tf_op jit(solution)/shard_map/ppermute | solution.py:290
  35.8 9.4 %collective-permute-start.12 = (bf16[128,2048]{1,0:T(8,128)(2,1)}, bf16[128,2048]{1,0:T(8,128)(2,1)S(1)}, u32[]{:S(2)}, u32[]{:S(2)}) collective-permute-start(bf16[128,2048]{1,0:T(8,128)(2,1)} %refs_12_.1), channel_id=1, source_target_pairs={{1,2},{2,1},{5,6},{6,5},{9,10},{10,9},{13,14},{14,13},{17,18},{18,... | collective-permute-start | bytes 1572872 | tf_op jit(solution)/shard_map/ppermute | solution.py:401
  36.5 15.2 %collective-permute-start.13 = (bf16[128,2048]{1,0:T(8,128)(2,1)S(1)}, bf16[128,2048]{1,0:T(8,128)(2,1)S(1)}, u32[]{:S(2)}, u32[]{:S(2)}) collective-permute-start(bf16[128,2048]{1,0:T(8,128)(2,1)S(1)} %collective-permute-done.11.refs_2_), channel_id=1, source_target_pairs={{1,0},{2,3},{5,4},{6,7},{9,8},{10,11},{13,12},{14,15},{17,16},{18,... | collective-permute-start | bytes 1572872 | tf_op jit(solution)/shard_map/ppermute | solution.py:400
  38.2 1.6 %copy-start.2 = (bf16[16,4,128,128]{3,2,1,0:T(8,128)(2,1)S(1)}, bf16[16,4,128,128]{3,2,1,0:T(8,128)(2,1)}, u32[]{:S(2)}) copy-start(bf16[16,4,128,128]{3,2,1,0:T(8,128)(2,1)} %adj) | copy-start | bytes 6291460
  42.0 10.9 %collective-permute-start.8 = (bf16[384,256]{1,0:T(8,128)(2,1)S(1)}, bf16[384,256]{1,0:T(8,128)(2,1)S(1)}, u32[]{:S(2)}, u32[]{:S(2)}) collective-permute-start(bf16[384,256]{1,0:T(8,128)(2,1)S(1)} %shard_map.142.refs_0_), channel_id=1, source_target_pairs={{0,8},{4,12},{8,0},{12,4},{16,24},{20,28},{24,16},{28,20},{1,9},{5... | collective-permute-start | bytes 589832 | tf_op jit(solution)/shard_map/ppermute | solution.py:290
  43.6 9.3 %collective-permute-start.9 = (bf16[384,256]{1,0:T(8,128)(2,1)S(1)}, bf16[384,256]{1,0:T(8,128)(2,1)S(1)}, u32[]{:S(2)}, u32[]{:S(2)}) collective-permute-start(bf16[384,256]{1,0:T(8,128)(2,1)S(1)} %shard_map.142.refs_0_), channel_id=1, source_target_pairs={{0,16},{4,20},{8,24},{12,28},{16,0},{20,4},{24,8},{28,12},{1,17},{... | collective-permute-start | bytes 589832 | tf_op jit(solution)/shard_map/ppermute | solution.py:290
  52.9 4.8 %collective-permute-start.14 = (bf16[192,256]{1,0:T(8,128)(2,1)S(1)}, bf16[192,256]{1,0:T(8,128)(2,1)S(1)}, u32[]{:S(2)}, u32[]{:S(2)}) collective-permute-start(bf16[192,256]{1,0:T(8,128)(2,1)S(1)} %slice.19), channel_id=1, source_target_pairs={{0,16},{4,20},{8,24},{12,28},{16,0},{20,4},{24,8},{28,12},{1,17},{... | collective-permute-start | bytes 294920 | tf_op jit(solution)/shard_map/ppermute | solution.py:290
  54.5 4.9 %collective-permute-start.15 = (bf16[192,256]{1,0:T(8,128)(2,1)S(1)}, bf16[192,256]{1,0:T(8,128)(2,1)S(1)}, u32[]{:S(2)}, u32[]{:S(2)}) collective-permute-start(bf16[192,256]{1,0:T(8,128)(2,1)S(1)} %slice.20), channel_id=1, source_target_pairs={{0,8},{4,12},{8,0},{12,4},{16,24},{20,28},{24,16},{28,20},{1,9},{5... | collective-permute-start | bytes 294920 | tf_op jit(solution)/shard_map/ppermute | solution.py:290
  55.1 11.1 %collective-permute-start.17 = (bf16[704,256]{1,0:T(8,128)(2,1)S(1)}, bf16[704,256]{1,0:T(8,128)(2,1)S(1)}, u32[]{:S(2)}, u32[]{:S(2)}) collective-permute-start(bf16[704,256]{1,0:T(8,128)(2,1)S(1)} %get-tuple-element.100), channel_id=1, source_target_pairs={{0,4},{4,8},{8,12},{12,16},{16,20},{20,24},{24,28},{28,0},{1,5},{5... | collective-permute-start | bytes 1081352 | tf_op jit(solution)/shard_map/ppermute | solution.py:433
  55.1 11.1 %collective-permute-start.18 = (bf16[704,256]{1,0:T(8,128)(2,1)S(1)}, bf16[704,256]{1,0:T(8,128)(2,1)S(1)}, u32[]{:S(2)}, u32[]{:S(2)}) collective-permute-start(bf16[704,256]{1,0:T(8,128)(2,1)S(1)} %get-tuple-element.101), channel_id=1, source_target_pairs={{4,0},{8,4},{12,8},{16,12},{20,16},{24,20},{28,24},{0,28},{5,1},{9... | collective-permute-start | bytes 1081352 | tf_op jit(solution)/shard_map/ppermute | solution.py:434
  59.4 9.5 %copy-start = (bf16[3,3,128,512]{3,2,1,0:T(8,128)(2,1)S(1)}, bf16[3,3,128,512]{3,2,1,0:T(8,128)(2,1)}, u32[]{:S(2)}) copy-start(bf16[3,3,128,512]{3,2,1,0:T(8,128)(2,1)} %slice.21) | copy-start | bytes 3538948
  59.4 13.3 %collective-permute-start.16 = (bf16[1152,256]{1,0:T(8,128)(2,1)S(1)}, bf16[1152,256]{1,0:T(8,128)(2,1)S(1)}, u32[]{:S(2)}, u32[]{:S(2)}) collective-permute-start(bf16[1152,256]{1,0:T(8,128)(2,1)S(1)} %pad_maximum_fusion), channel_id=1, source_target_pairs={{0,4},{4,0},{8,12},{12,8},{16,20},{20,16},{24,28},{28,24},{1,5},{5... | collective-permute-start | bytes 1769480 | tf_op jit(solution)/shard_map/ppermute | solution.py:290
  59.5 13.2 %collective-permute-start.7 = (bf16[384,256]{1,0:T(8,128)(2,1)S(1)}, bf16[384,256]{1,0:T(8,128)(2,1)S(1)}, u32[]{:S(2)}, u32[]{:S(2)}) collective-permute-start(bf16[384,256]{1,0:T(8,128)(2,1)S(1)} %shard_map.142.refs_0_), channel_id=1, source_target_pairs={{0,4},{4,0},{8,12},{12,8},{16,20},{20,16},{24,28},{28,24},{1,5},{5... | collective-permute-start | bytes 589832 | tf_op jit(solution)/shard_map/ppermute | solution.py:290
  68.9 3.8 %copy-start.3 = (bf16[16,2,128,128]{3,2,1,0:T(8,128)(2,1)S(1)}, bf16[16,2,128,128]{3,2,1,0:T(8,128)(2,1)}, u32[]{:S(2)}) copy-start(bf16[16,2,128,128]{3,2,1,0:T(8,128)(2,1)} %refs_7_.1) | copy-start | bytes 3145732
  68.9 3.8 %copy-start.5 = (s32[2048]{0:T(1024)S(1)}, s32[2048]{0:T(1024)}, u32[]{:S(2)}) copy-start(s32[2048]{0:T(1024)} %param.19) | copy-start | bytes 24580
  68.9 3.8 %copy-start.6 = (bf16[2,2048]{1,0:T(2,128)(2,1)S(1)}, bf16[2,2048]{1,0:T(2,128)(2,1)}, u32[]{:S(2)}) copy-start(bf16[2,2048]{1,0:T(2,128)(2,1)} %refs_11_.1) | copy-start | bytes 24580

commit v4 on v3

--- a/solution.py
+++ b/solution.py
@@ -175,64 +175,73 @@
             if k == 3 and len(parts) > n:
                 other = parts[4][:, start : start + 2 * tile]
                 part = jnp.where(is_end(meta[2]), other, part)
-            out[k * channels : (k + 1) * channels] = jnp.where(keep, part, jnp.zeros((), BF))
+            at = pl.ds(pl.multiple_of((meta[2] ^ k) * channels, channels), channels)
+            out[at] = jnp.where(keep, part, jnp.zeros((), BF))
         out[n * channels :] = weights[...]
 
 
-def hop_one_kernel(n, tile, meta, *refs):
-    *parts, left, right, band, ext, one = refs
+def hop(source, at, tile, a, b):
+    picked = source[:, at : at + 4 * tile]
+    return jnp.dot(picked, pair_weights(tile, a, b), preferred_element_type=F32).astype(BF)
+
+
+def gate_sums(w, state, one, two):
+    acc = jnp.dot(w[0], state, preferred_element_type=F32)
+    acc = acc + jnp.dot(w[1], one, preferred_element_type=F32)
+    return acc + jnp.dot(w[2], two, preferred_element_type=F32)
+
+
+def inner_kernel(n, tile, meta, *refs):
+    *parts, band, w, out, state_rim, one_rim, own, one = refs
     channels, rows = parts[0].shape
-    total = ext.shape[0]
     tiles = rows // tile
-    half = 3 * tile // 2
+    pair = 2 * tile
     keep = lax.broadcasted_iota(jnp.int32, (1, rows), 1) < meta[1]
-    ends = slice(0, 2 * tile), slice(2 * tile + rows, 4 * tile + rows)
     for k in range(n):
         at = pl.ds(pl.multiple_of((meta[2] ^ k) * channels, channels), channels)
         part = parts[k][...]
         if k == 3 and len(parts) > n:
             part = jnp.where(is_end(meta[2]), parts[4][...], part)
-        ext[at, 2 * tile : 2 * tile + rows] = jnp.where(keep, part, jnp.zeros((), BF))
-        for end, beside in zip(ends, (left, right)):
-            ext[at, end] = beside[k * channels : (k + 1) * channels]
+        own[at] = jnp.where(keep, part, jnp.zeros((), BF))
+    state_rim[:, :pair] = own[:, :pair]
+    state_rim[:, pair:] = own[:, rows - pair :]
+    for u in range(1, tiles // 2):
+        made = hop(own, (2 * u - 2) * tile, tile, band[2 * u - 1], band[2 * u])
+        one[:, (u - 1) * pair : u * pair] = made
+    one_rim[:, :pair] = one[:, :pair]
+    one_rim[:, pair:] = one[:, rows - 2 * pair :]
+    for u in range(1, tiles // 2 - 1):
+        at = (u - 1) * pair
+        two = hop(one, at, tile, band[2 * u], band[2 * u + 1])
+        state = own[:, u * pair : (u + 1) * pair]
+        out[:, at : at + pair] = gate_sums(w, state, one[:, at + tile : at + tile + pair], two)
+
+
+def rim_kernel(tile, left, right, state_rim, one_rim, band, w, out):
+    total = state_rim.shape[0]
+    half = 3 * tile // 2
+    pair = 2 * tile
+    tiles = band.shape[0]
 
     def edge(ref):
         return jnp.concatenate(
             [ref[total : total + half, :tile], ref[total : total + half, tile:]], axis=0
         )
 
-    def hop(u, a, b):
-        at = lambda width: pl.ds(pl.multiple_of(2 * u * tile, 2 * tile), width)
-        made = jnp.dot(ext[:, at(4 * tile)], pair_weights(tile, a, b), preferred_element_type=F32)
-        one[:, at(2 * tile)] = made.astype(BF)
-
-    hop(0, edge(left), band[0])
-    hop(tiles // 2, band[tiles - 1], edge(right))
-
-    def step(u, _):
-        hop(u, band[2 * u - 1], band[2 * u])
-        return 0
-
-    lax.fori_loop(1, tiles // 2, step, 0, unroll=True)
-
-
-def hop_two_kernel(tile, ext, one, band, w, out):
-    def step(u, _):
-        at = lambda s, width: pl.ds(pl.multiple_of(2 * u * tile + s, tile), width)
-        weights = pair_weights(tile, band[2 * u], band[2 * u + 1])
-        two = jnp.dot(one[:, at(0, 4 * tile)], weights, preferred_element_type=F32).astype(BF)
-        acc = jnp.dot(w[0], ext[:, at(2 * tile, 2 * tile)], preferred_element_type=F32)
-        acc = acc + jnp.dot(w[1], one[:, at(tile, 2 * tile)], preferred_element_type=F32)
-        acc = acc + jnp.dot(w[2], two, preferred_element_type=F32)
-        out[:, at(0, 2 * tile)] = acc
-        return 0
-
-    lax.fori_loop(0, out.shape[1] // (2 * tile), step, 0, unroll=True)
+    near = jnp.concatenate([left[:total], state_rim[:, :pair]], axis=1)
+    one = jnp.concatenate([hop(near, 0, tile, edge(left), band[0]), one_rim[:, :pair]], axis=1)
+    two = hop(one, 0, tile, band[0], band[1])
+    out[:, :pair] = gate_sums(w, state_rim[:, :pair], one[:, tile : tile + pair], two)
+    near = jnp.concatenate([state_rim[:, pair:], right[:total]], axis=1)
+    made = hop(near, 0, tile, band[tiles - 1], edge(right))
+    one = jnp.concatenate([one_rim[:, pair:], made], axis=1)
+    two = hop(one, 0, tile, band[tiles - 2], band[tiles - 1])
+    out[:, pair:] = gate_sums(w, state_rim[:, pair:], one[:, tile : tile + pair], two)
 
 
 def final_kernel(places, n_given, share, tile, meta, ccols, *refs):
     given = refs[:n_given]
-    ctiles, ids, partial, terms, inputs, state, out, coarse, mixed = refs[n_given:]
+    ctiles, ids, middle, rim, terms, inputs, state, out, coarse, mixed = refs[n_given:]
     outputs = coarse.shape[0]
     clusters = coarse.shape[1]
     for ref, src, dst, rows, b, absolute in places:
@@ -259,13 +268,19 @@
     channels = state.shape[0]
     width = 4 * tile
 
-    def step(c, _):
-        at = pl.ds(pl.multiple_of(c * width, width), width)
+    pair = 2 * tile
+    for start in range(0, sensors, width):
+        at = slice(start, start + width)
         own = ids[:, at]
         hot = jnp.concatenate(
             [one_hot(own, f, share) for f in range(0, clusters, share)], axis=0
         )
-        sums = partial[:, at] + jnp.dot(mixed[...], hot, preferred_element_type=F32)
+        before = [middle[:, max(start - pair, 0) : min(start + width, sensors - pair) - pair]]
+        if start == 0:
+            before = [rim[:, :pair]] + before
+        if start + width == sensors:
+            before = before + [rim[:, pair:]]
+        sums = jnp.concatenate(before, axis=1) + jnp.dot(mixed[...], hot, preferred_element_type=F32)
         x = inputs[:, at].astype(F32)
         given_terms = terms[:, 2:3] + terms[:, 0:1] * x[0:1] + terms[:, 1:2] * x[1:2]
         update = jax.nn.sigmoid(given_terms[:channels] + sums[:channels])
@@ -274,12 +289,9 @@
         )
         candidate = jnp.tanh(given_terms[2 * channels :] + reset * sums[2 * channels :])
         old = state[:, at].astype(F32)
-        spot = lax.broadcasted_iota(jnp.int32, (1, width), 1) + c * width
+        spot = lax.broadcasted_iota(jnp.int32, (1, width), 1) + start
         new = update * old + (1.0 - update) * candidate
         out[:, at] = jnp.where(spot < meta[1], new, 0.0).astype(BF)
-        return 0
-
-    lax.fori_loop(0, sensors // width, step, 0, unroll=True)
 
 
 def flip(n, b):
@@ -432,26 +444,28 @@
     up = [(i, (i + 1) % n_dom) for i in range(n_dom)]
     left = lax.ppermute(last, "dom", up)
     right = lax.ppermute(first, "dom", [(j, i) for i, j in up])
-    ext, one = call(
-        functools.partial(hop_one_kernel, n_feat, tile),
-        [sds((total, rows + 4 * tile), BF), sds((total, rows + 2 * tile), BF)],
-        [meta] + blocks + [left, right, band],
-        flops=2 * total * rows * kb * tile,
+    pair = 2 * tile
+    middle, state_rim, one_rim = call(
+        functools.partial(inner_kernel, n_feat, tile),
+        [sds((outputs, rows - 2 * pair), F32)] + [sds((total, 2 * pair), BF)] * 2,
+        [meta] + blocks + [band, w_own],
+        [pltpu.VMEM((total, rows), BF), pltpu.VMEM((total, rows - pair), BF)],
+        flops=(4 * total * rows * kb * tile + 6 * total * rows * outputs) // 1,
         bytes_accessed=8 * total * rows,
     )
-    partial = call(
-        functools.partial(hop_two_kernel, tile),
-        sds((outputs, rows), F32),
-        [ext, one, band, w_own],
-        flops=2 * total * rows * (kb * tile + 3 * outputs),
-        bytes_accessed=8 * total * rows,
+    rim = call(
+        functools.partial(rim_kernel, tile),
+        sds((outputs, 2 * pair), F32),
+        [left, right, state_rim, one_rim, band, w_own],
+        flops=30 * total * rows * outputs,
+        bytes_accessed=total * rows,
     )
     return call(
         functools.partial(final_kernel, places, len(given), share, tile),
         sds((channels, rows), BF),
         [meta, coarse_at]
         + given
-        + [coarse_tiles, ids, partial, terms, inputs, state],
+        + [coarse_tiles, ids, middle, rim, terms, inputs, state],
         [pltpu.VMEM((outputs, clusters), BF)] * 2,
         flops=2 * outputs * rows * clusters,
         bytes_accessed=8 * outputs * rows,

time: 80.2 us -> 76.6 us (0.955)
  waiting for transfers between devices: 16.9 us -> 10.6 us
  local copies, waits for them, and re-layouts: 4.56 us -> 6.38 us
    ppermute x1, waiting for transfers between devices: 6.21 us -> 0.01 us  [body(): left = lax.ppermute(last, 'dom', up)]
    ppermute x1, waiting for transfers between devices: 6.54 us -> 3.31 us  [body(): outer = lax.ppermute(blocks[2], 'feat', [(1, 0), (2, 3)])]
    ppermute x15, waiting for transfers between devices: 4.18 us -> 7.31 us  [swap(): return lax.ppermute(array, axis, flip(lax.axis_size(axis), b))]
    slice x2, local copies, waits for them, and re-layouts: 1.16 us -> 0.11 us  [body(): w_own, w_coarse = (w[:3], w[3])]
    unnamed x30 -> x28, local copies, waits for them, and re-layouts: 2.43 us -> 3.34 us
  transfers between devices with their start and end apart: 19 -> 19, of which waited for: 5 -> 5; matrix products, arithmetic and copies ran while one was open for 3% -> 5% of each run, Pallas kernels for 16% -> 18%
where the time goes in v4:
time: 76.6 us; the launch traced here: 75.9 us
  Pallas kernels  24.4 us (32%)
  starting transfers between devices  23.9 us (31%)
  waiting for transfers between devices  10.6 us (14%)
  blocking collectives  8.88 us (12%)
  local copies, waits for them, and re-layouts  6.38 us (8%)
  between operations  1.03 us (1%)
    pallas_call x11, Pallas kernels, call(): pl.pallas_call(kernel, out_shape=outs, in_specs=specs, out_specs=jax.tree...  24.4 us
    ppermute x15, starting transfers between devices, swap(): return lax.ppermute(array, axis, flip(lax.axis_size(axis), b))  19.2 us
    all_gather x1, blocking collectives, body(): every_value = lax.all_gather(values, 'dom', axis=0)  8.88 us
    ppermute x15, waiting for transfers between devices, swap(): return lax.ppermute(array, axis, flip(lax.axis_size(axis), b))  7.31 us
    unnamed x28, local copies, waits for them, and re-layouts  3.34 us
    ppermute x1, waiting for transfers between devices, body(): outer = lax.ppermute(blocks[2], 'feat', [(1, 0), (2, 3)])  3.31 us
    ppermute x1, starting transfers between devices, body(): right = lax.ppermute(first, 'dom', [(j, i) for i, j in up])  2.63 us
  transfers between devices with their start and end apart: 19, of which 5 were waited for; matrix products, arithmetic and copies ran while one was open for 5% of the time, Pallas kernels for 18%

profile of v4, /device:TPU:0, one launch (start us, length us, event | category | flops | bytes accessed | tf_op | source)
XLA Modules:
  0.0 75.9 jit_solution(6743962812762821643)
XLA Ops:
  0.7 0.1 pad_add_fusion.meta
  0.7 0.7 copy-done.3
  1.4 3.9 %shard_map.136 = (f32[4,144,256]{2,1,0:T(8,128)S(1)}, bf16[4,144,256]{2,1,0:T(8,128)(2,1)S(1)}) custom-call(s32[3]{0:T(128)S(1)} %pad_add_fusion.meta, bf16[128,2048]{1,0:T(8,128)(2,1)} %refs_13_.1, s32[1,2048]{1,0:T(1,128)S(1)} %bitcast.22), custom_call_target="tpu_custom_call" | custom-call | flops 3221225472 | bytes 2097152 | tf_op jit(solution)/shard_map/pallas_call | solution.py:19
  5.4 0.0 copy-start.8
  5.4 0.5 collective-permute-start
  5.9 3.7 %collective-permute-start.11 = (bf16[128,2048]{1,0:T(8,128)(2,1)}, bf16[128,2048]{1,0:T(8,128)(2,1)S(1)}, u32[]{:S(2)}, u32[]{:S(2)}) collective-permute-start(bf16[128,2048]{1,0:T(8,128)(2,1)} %refs_13_.1), channel_id=1, source_target_pairs={{0,2},{1,3},{2,0},{3,1},{4,6},{5,7},{6,4},{7,5},{8,10},{9,11},{10,... | collective-permute-start | bytes 1572872 | tf_op jit(solution)/shard_map/ppermute | solution.py:302
  9.6 0.1 copy.38
  9.6 0.1 reshape.16.cols
  9.7 0.0 collective-permute-done.arrived
  9.7 0.1 shard_map.137
  9.8 0.1 copy.35
  10.0 1.6 %collective-permute-start.10 = (bf16[128,2048]{1,0:T(8,128)(2,1)}, bf16[128,2048]{1,0:T(8,128)(2,1)S(1)}, u32[]{:S(2)}, u32[]{:S(2)}) collective-permute-start(bf16[128,2048]{1,0:T(8,128)(2,1)} %refs_13_.1), channel_id=1, source_target_pairs={{0,1},{1,0},{2,3},{3,2},{4,5},{5,4},{6,7},{7,6},{8,9},{9,8},{10,11... | collective-permute-start | bytes 1572872 | tf_op jit(solution)/shard_map/ppermute | solution.py:302
  11.6 0.1 copy.36
  11.8 0.0 copy-start
  11.8 1.6 %collective-permute-start.1 = (bf16[144,256]{1,0:T(8,128)(2,1)S(1)}, bf16[144,256]{1,0:T(8,128)(2,1)S(1)}, u32[]{:S(2)}, u32[]{:S(2)}) collective-permute-start(bf16[144,256]{1,0:T(8,128)(2,1)S(1)} %get-tuple-element.65), channel_id=1, source_target_pairs={{0,8},{4,12},{8,0},{12,4},{16,24},{20,28},{24,16},{28,20},{1,9},{5... | collective-permute-start | bytes 221192 | tf_op jit(solution)/shard_map/ppermute | solution.py:302
  13.3 1.5 %collective-permute-start.2 = (bf16[144,256]{1,0:T(8,128)(2,1)S(1)}, bf16[144,256]{1,0:T(8,128)(2,1)S(1)}, u32[]{:S(2)}, u32[]{:S(2)}) collective-permute-start(bf16[144,256]{1,0:T(8,128)(2,1)S(1)} %get-tuple-element.66), channel_id=1, source_target_pairs={{0,16},{4,20},{8,24},{12,28},{16,0},{20,4},{24,8},{28,12},{1,17},{... | collective-permute-start | bytes 221192 | tf_op jit(solution)/shard_map/ppermute | solution.py:302
  14.8 0.5 collective-permute-start.3
  15.3 2.2 %shard_map.138.weights = bf16[2,2048,256]{2,1,0:T(8,128)(2,1)S(1)} custom-call(f32[2,16,256]{2,1,0:T(8,128)S(1)} %pad.8.source, f32[2,16,2048]{2,1,0:T(8,128)S(1)} %pad.9.target), custom_call_target="tpu_custom_call" | custom-call | flops 4194304000 | tf_op jit(solution)/shard_map/pallas_call | solution.py:19
  17.6 0.0 collective-permute-done.1.refs_1_
  17.6 0.1 collective-permute-done.2.refs_2_
  17.7 2.4 %collective-permute-done.3.refs_3_ = bf16[144,256]{1,0:T(8,128)(2,1)S(1)} collective-permute-done((bf16[144,256]{1,0:T(8,128)(2,1)S(1)}, bf16[144,256]{1,0:T(8,128)(2,1)S(1)}, u32[]{:S(2)}, u32[]{:S(2)}) %collective-permute-start.3) | collective-permute-done | bytes 73760 | tf_op jit(solution)/shard_map/ppermute | solution.py:302
  20.1 0.2 shard_map.139
  20.3 8.9 %all-gather = bf16[1024,256]{1,0:T(8,128)(2,1)S(1)} all-gather(bf16[128,256]{1,0:T(8,128)(2,1)S(1)} %get-tuple-element.74), channel_id=2, replica_groups=mesh['dom'=8,'feat'=4] {'dom'}, dimensions={0}, use_global_device_ids=true | all-gather | bytes 589824 | tf_op jit(solution)/shard_map/all_gather | solution.py:401
  29.2 0.5 shard_map.140.refs_0_
  29.7 0.9 %copy-done.6 = bf16[3,128,4,512]{3,2,1,0:T(4,128)(2,1)S(1)} copy-done((bf16[3,128,4,512]{3,2,1,0:T(4,128)(2,1)S(1)}, bf16[3,128,4,512]{3,2,1,0:T(4,128)(2,1)}, u32[]{:S(2)}) %copy-start.6) | copy-done | bytes 1572888
  30.6 0.3 copy.45
  31.0 0.0 copy-start.11
  31.0 0.0 copy-start.12
  31.0 0.1 slice.21
  31.1 0.5 collective-permute-start.4
  31.6 1.3 %collective-permute-start.5 = (bf16[128,256]{1,0:T(8,128)(2,1)S(1)}, bf16[128,256]{1,0:T(8,128)(2,1)S(1)}, u32[]{:S(2)}, u32[]{:S(2)}) collective-permute-start(bf16[128,256]{1,0:T(8,128)(2,1)S(1)} %shard_map.140.refs_0_), channel_id=1, source_target_pairs={{0,2},{1,3},{2,0},{3,1},{4,6},{5,7},{6,4},{7,5},{8,10},{9,11},{10,... | collective-permute-start | bytes 196616 | tf_op jit(solution)/shard_map/ppermute | solution.py:302
  32.9 2.6 %collective-permute-start.6 = (bf16[128,256]{1,0:T(8,128)(2,1)S(1)}, bf16[128,256]{1,0:T(8,128)(2,1)}, u32[]{:S(2)}, u32[]{:S(2)}) collective-permute-start(bf16[128,256]{1,0:T(8,128)(2,1)S(1)} %shard_map.140.refs_0_), channel_id=1, source_target_pairs={{0,3},{1,2},{2,1},{3,0},{4,7},{5,6},{6,5},{7,4},{8,11},{9,10},{10,... | collective-permute-start | bytes 196616 | tf_op jit(solution)/shard_map/ppermute | solution.py:302
  35.6 0.7 collective-permute-start.12
  36.3 1.3 %collective-permute-start.13 = (bf16[128,2048]{1,0:T(8,128)(2,1)S(1)}, bf16[128,2048]{1,0:T(8,128)(2,1)}, u32[]{:S(2)}, u32[]{:S(2)}) collective-permute-start(bf16[128,2048]{1,0:T(8,128)(2,1)S(1)} %collective-permute-done.11.refs_2_), channel_id=1, source_target_pairs={{1,0},{2,3},{5,4},{6,7},{9,8},{10,11},{13,12},{14,15},{17,16},{18,... | collective-permute-start | bytes 1572872 | tf_op jit(solution)/shard_map/ppermute | solution.py:412
  37.6 0.6 pad_maximum_fusion.1
  38.2 0.8 %copy.40.terms = f32[384,3]{1,0:T(8,128)S(1)} copy(f32[384,3]{0,1:T(4,128)} %pad_maximum_fusion.1) | data formatting | bytes 9216 | tf_op jit(solution)/shard_map/concatenate | solution.py:417
  39.0 0.7 copy.41
  39.7 0.8 %reshape.18.ccols = s32[32]{0:T(128)S(1)} reshape(s32[16,2]{1,0:T(8,128)} %copy.41) | data formatting | bytes 256 | tf_op jit(solution)/shard_map/reshape | solution.py:427
  40.5 0.0 copy-start.1
  40.5 1.6 %copy-done.1 = bf16[16,4,128,128]{3,2,1,0:T(8,128)(2,1)S(1)} copy-done((bf16[16,4,128,128]{3,2,1,0:T(8,128)(2,1)S(1)}, bf16[16,4,128,128]{3,2,1,0:T(8,128)(2,1)}, u32[]{:S(2)}) %copy-start.1) | copy-done | bytes 2097176
  42.1 1.3 %shard_map.141 = (bf16[16,384,128]{2,1,0:T(8,128)(2,1)S(1)}, bf16[192,256]{1,0:T(8,128)(2,1)S(1)}, bf16[192,256]{1,0:T(8,128)(2,1)S(1)}, f32[384,3]{1,0:T(8,128)S(1)}) custom-call(s32[3]{0:T(128)S(1)} %pad_add_fusion.meta, s32[64]{0:T(128)S(1)} %reshape.16.cols, bf16[16,4,128,128]{3,2,1,0:T(8,128)(2,1)S(1)} %copy-done.1, f32[384,3]{1,0:T(8,128)S(1)} %copy.40.terms), custom_call_target="tpu_custom_call" | custom-call | flops 1000000000 | tf_op jit(solution)/shard_map/pallas_call | solution.py:19
  43.4 0.0 collective-permute-done.5.refs_2_
  43.4 0.0 collective-permute-done.6.refs_3_
  43.5 1.1 %shard_map.142.refs_0_ = bf16[384,256]{1,0:T(8,128)(2,1)S(1)} custom-call(s32[3]{0:T(128)S(1)} %pad_add_fusion.meta, bf16[128,256]{1,0:T(8,128)(2,1)S(1)} %shard_map.140.refs_0_, bf16[128,256]{1,0:T(8,128)(2,1)S(1)} %collective-permute-done.4.refs_1_, bf16[128,256]{1,0:T(8,128)(2,1)S(1)} %collective-permute-done.5.refs_2_, ...), custom_call_target="tpu_custom_call" | custom-call | tf_op jit(solution)/shard_map/pallas_call | solution.py:19
  44.6 1.6 %collective-permute-start.8 = (bf16[384,256]{1,0:T(8,128)(2,1)S(1)}, bf16[384,256]{1,0:T(8,128)(2,1)S(1)}, u32[]{:S(2)}, u32[]{:S(2)}) collective-permute-start(bf16[384,256]{1,0:T(8,128)(2,1)S(1)} %shard_map.142.refs_0_), channel_id=1, source_target_pairs={{0,8},{4,12},{8,0},{12,4},{16,24},{20,28},{24,16},{28,20},{1,9},{5... | collective-permute-start | bytes 589832 | tf_op jit(solution)/shard_map/ppermute | solution.py:302
  46.2 2.1 %collective-permute-start.9 = (bf16[384,256]{1,0:T(8,128)(2,1)S(1)}, bf16[384,256]{1,0:T(8,128)(2,1)S(1)}, u32[]{:S(2)}, u32[]{:S(2)}) collective-permute-start(bf16[384,256]{1,0:T(8,128)(2,1)S(1)} %shard_map.142.refs_0_), channel_id=1, source_target_pairs={{0,16},{4,20},{8,24},{12,28},{16,0},{20,4},{24,8},{28,12},{1,17},{... | collective-permute-start | bytes 589832 | tf_op jit(solution)/shard_map/ppermute | solution.py:302
  48.3 0.0 collective-permute-start.7
  48.3 0.0 collective-permute-done.12.refs_3_
  48.3 3.3 %collective-permute-done.13.refs_4_ = bf16[128,2048]{1,0:T(8,128)(2,1)} collective-permute-done((bf16[128,2048]{1,0:T(8,128)(2,1)S(1)}, bf16[128,2048]{1,0:T(8,128)(2,1)}, u32[]{:S(2)}, u32[]{:S(2)}) %collective-permute-start.13) | collective-permute-done | bytes 524320 | tf_op jit(solution)/shard_map/ppermute | solution.py:412
  51.6 1.3 %shard_map.143 = (bf16[704,256]{1,0:T(8,128)(2,1)S(1)}, bf16[704,256]{1,0:T(8,128)(2,1)S(1)}) custom-call(s32[3]{0:T(128)S(1)} %pad_add_fusion.meta, bf16[128,2048]{1,0:T(8,128)(2,1)} %refs_13_.1, bf16[128,2048]{1,0:T(8,128)(2,1)S(1)} %collective-permute-done.10.refs_1_, bf16[128,2048]{1,0:T(8,128)(2,1)S(1)} %collective-permute-done.11.refs_2_, ...), custom_call_target="tpu_custom_call" | custom-call | tf_op jit(solution)/shard_map/pallas_call | solution.py:19
  52.9 0.0 collective-permute-done.9.refs_3_
  52.9 0.1 collective-permute-start.17
  53.0 2.6 %collective-permute-start.18 = (bf16[704,256]{1,0:T(8,128)(2,1)S(1)}, bf16[704,256]{1,0:T(8,128)(2,1)S(1)}, u32[]{:S(2)}, u32[]{:S(2)}) collective-permute-start(bf16[704,256]{1,0:T(8,128)(2,1)S(1)} %get-tuple-element.105), channel_id=1, source_target_pairs={{4,0},{8,4},{12,8},{16,12},{20,16},{24,20},{28,24},{0,28},{5,1},{9... | collective-permute-start | bytes 1081352 | tf_op jit(solution)/shard_map/ppermute | solution.py:446
  55.6 1.6 %collective-permute-start.14 = (bf16[192,256]{1,0:T(8,128)(2,1)S(1)}, bf16[192,256]{1,0:T(8,128)(2,1)S(1)}, u32[]{:S(2)}, u32[]{:S(2)}) collective-permute-start(bf16[192,256]{1,0:T(8,128)(2,1)S(1)} %slice.19), channel_id=1, source_target_pairs={{0,16},{4,20},{8,24},{12,28},{16,0},{20,4},{24,8},{28,12},{1,17},{... | collective-permute-start | bytes 294920 | tf_op jit(solution)/shard_map/ppermute | solution.py:302
  57.2 0.1 collective-permute-start.15
  57.2 5.3 %shard_map.144 = (f32[384,1536]{1,0:T(8,128)S(1)}, bf16[512,512]{1,0:T(8,128)(2,1)S(1)}, bf16[512,512]{1,0:T(8,128)(2,1)S(1)}) custom-call(s32[3]{0:T(128)S(1)} %pad_add_fusion.meta, bf16[128,2048]{1,0:T(8,128)(2,1)} %refs_13_.1, bf16[128,2048]{1,0:T(8,128)(2,1)S(1)} %collective-permute-done.10.refs_1_, ...), custom_call_target="tpu_custom_call" | custom-call | flops 4563402752 | bytes 8388608 | tf_op jit(solution)/shard_map/pallas_call | solution.py:19
  62.5 4.2 %collective-permute-done.15.refs_5_ = bf16[192,256]{1,0:T(8,128)(2,1)S(1)} collective-permute-done((bf16[192,256]{1,0:T(8,128)(2,1)S(1)}, bf16[192,256]{1,0:T(8,128)(2,1)S(1)}, u32[]{:S(2)}, u32[]{:S(2)}) %collective-permute-start.15) | collective-permute-done | bytes 98336 | tf_op jit(solution)/shard_map/ppermute | solution.py:302
  66.7 0.1 collective-permute-start.16
  66.8 0.0 copy-start.2
  66.9 0.0 copy-start.4
  66.9 0.0 copy-start.5
  66.9 1.3 %shard_map.145.refs_10_ = f32[384,512]{1,0:T(8,128)S(1)} custom-call(bf16[704,256]{1,0:T(8,128)(2,1)S(1)} %collective-permute-done.17.left, bf16[704,256]{1,0:T(8,128)(2,1)S(1)} %collective-permute-done.18.right, bf16[512,512]{1,0:T(8,128)(2,1)S(1)} %get-tuple-element.106.state_rim, bf16[512,512]{1,0:T(8,128)(2,1)S(1)} %get-tuple-element.107.one_rim, ...), custom_call_target="tpu_custom_call" | custom-call | flops 12079595520 | bytes 1048576 | tf_op jit(solution)/shard_map/pallas_call | solution.py:19
  68.2 0.6 collective-permute-done.16.refs_6_
  68.8 7.1 %shard_map.146 = bf16[128,2048]{1,0:T(8,128)(2,1)} custom-call(s32[3]{0:T(128)S(1)} %pad_add_fusion.meta, s32[32]{0:T(128)S(1)} %reshape.18.ccols, bf16[384,256]{1,0:T(8,128)(2,1)S(1)} %shard_map.142.refs_0_, bf16[384,256]{1,0:T(8,128)(2,1)S(1)} %collective-permute-done.7.refs_1_, bf16[384,256]{1,0:T(8,128)(2,1)S(1)} %collective-permute-done.8.refs_2_, ...), custom_call_target="tpu_custom_call" | custom-call | flops 3221225472 | bytes 6291456 | tf_op jit(solution)/shard_map/pallas_call | solution.py:19
  (32 shorter events, 0.2 us)
Async XLA Ops:
  0.7 0.7 copy-start.3
  1.4 8.1 %copy-start.10 = (f32[3,128]{1,0:T(4,128)S(1)}, f32[3,128]{1,0:T(4,128)}, u32[]{:S(2)}) copy-start(f32[3,128]{1,0:T(4,128)} %param.22) | copy-start | bytes 4612
  1.4 8.1 %copy-start.9 = (s32[16,4]{0,1:T(4,128)S(1)}, s32[16,4]{0,1:T(4,128)}, u32[]{:S(2)}) copy-start(s32[16,4]{0,1:T(4,128)} %param.17) | copy-start | bytes 772
  1.4 8.4 %copy-start.7 = (f32[2,10,2048]{2,0,1:T(2,128)S(1)}, f32[2,10,2048]{2,0,1:T(2,128)}, u32[]{:S(2)}) copy-start(f32[2,10,2048]{2,0,1:T(2,128)} %param.24) | copy-start | bytes 491524
  5.4 6.2 %copy-start.8 = (f32[2,10,2048]{2,0,1:T(2,128)S(1)}, f32[2,10,2048]{2,0,1:T(2,128)}, u32[]{:S(2)}) copy-start(f32[2,10,2048]{2,0,1:T(2,128)} %param.25) | copy-start | bytes 491524
  5.4 4.4 %collective-permute-start = (bf16[4,144,256]{2,1,0:T(8,128)(2,1)S(1)}, bf16[4,144,256]{2,1,0:T(8,128)(2,1)S(1)}, u32[]{:S(2)}, u32[]{:S(2)}) collective-permute-start(bf16[4,144,256]{2,1,0:T(8,128)(2,1)S(1)} %get-tuple-element.59), channel_id=1, source_target_pairs={{0,4},{4,0},{8,12},{12,8},{16,20},{20,16},{24,28},{28,24},{1,5},{5... | collective-permute-start | bytes 884744 | tf_op jit(solution)/shard_map/ppermute | solution.py:302
  5.9 29.7 %collective-permute-start.11 = (bf16[128,2048]{1,0:T(8,128)(2,1)}, bf16[128,2048]{1,0:T(8,128)(2,1)S(1)}, u32[]{:S(2)}, u32[]{:S(2)}) collective-permute-start(bf16[128,2048]{1,0:T(8,128)(2,1)} %refs_13_.1), channel_id=1, source_target_pairs={{0,2},{1,3},{2,0},{3,1},{4,6},{5,7},{6,4},{7,5},{8,10},{9,11},{10,... | collective-permute-start | bytes 1572872 | tf_op jit(solution)/shard_map/ppermute | solution.py:302
  10.0 25.6 %collective-permute-start.10 = (bf16[128,2048]{1,0:T(8,128)(2,1)}, bf16[128,2048]{1,0:T(8,128)(2,1)S(1)}, u32[]{:S(2)}, u32[]{:S(2)}) collective-permute-start(bf16[128,2048]{1,0:T(8,128)(2,1)} %refs_13_.1), channel_id=1, source_target_pairs={{0,1},{1,0},{2,3},{3,2},{4,5},{5,4},{6,7},{7,6},{8,9},{9,8},{10,11... | collective-permute-start | bytes 1572872 | tf_op jit(solution)/shard_map/ppermute | solution.py:302
  11.8 8.3 %copy-start = (bf16[2,64,64]{2,1,0:T(8,128)(2,1)S(1)}, bf16[2,64,64]{2,1,0:T(8,128)(2,1)}, u32[]{:S(2)}) copy-start(bf16[2,64,64]{2,1,0:T(8,128)(2,1)} %w_value.1) | copy-start | bytes 49156
  11.8 5.8 %collective-permute-start.1 = (bf16[144,256]{1,0:T(8,128)(2,1)S(1)}, bf16[144,256]{1,0:T(8,128)(2,1)S(1)}, u32[]{:S(2)}, u32[]{:S(2)}) collective-permute-start(bf16[144,256]{1,0:T(8,128)(2,1)S(1)} %get-tuple-element.65), channel_id=1, source_target_pairs={{0,8},{4,12},{8,0},{12,4},{16,24},{20,28},{24,16},{28,20},{1,9},{5... | collective-permute-start | bytes 221192 | tf_op jit(solution)/shard_map/ppermute | solution.py:302
  13.3 4.4 %collective-permute-start.2 = (bf16[144,256]{1,0:T(8,128)(2,1)S(1)}, bf16[144,256]{1,0:T(8,128)(2,1)S(1)}, u32[]{:S(2)}, u32[]{:S(2)}) collective-permute-start(bf16[144,256]{1,0:T(8,128)(2,1)S(1)} %get-tuple-element.66), channel_id=1, source_target_pairs={{0,16},{4,20},{8,24},{12,28},{16,0},{20,4},{24,8},{28,12},{1,17},{... | collective-permute-start | bytes 221192 | tf_op jit(solution)/shard_map/ppermute | solution.py:302
  14.8 5.3 %collective-permute-start.3 = (bf16[144,256]{1,0:T(8,128)(2,1)S(1)}, bf16[144,256]{1,0:T(8,128)(2,1)S(1)}, u32[]{:S(2)}, u32[]{:S(2)}) collective-permute-start(bf16[144,256]{1,0:T(8,128)(2,1)S(1)} %get-tuple-element.67), channel_id=1, source_target_pairs={{0,24},{4,28},{8,16},{12,20},{16,8},{20,12},{24,0},{28,4},{1,25},{... | collective-permute-start | bytes 221192 | tf_op jit(solution)/shard_map/ppermute | solution.py:302
  29.2 1.4 %copy-start.6 = (bf16[3,128,4,512]{3,2,1,0:T(4,128)(2,1)S(1)}, bf16[3,128,4,512]{3,2,1,0:T(4,128)(2,1)}, u32[]{:S(2)}) copy-start(bf16[3,128,4,512]{3,2,1,0:T(4,128)(2,1)} %param.20) | copy-start | bytes 4718596
  31.0 6.6 %copy-start.11 = (bf16[3,128,2]{1,2,0:T(2,128)(2,1)S(1)}, bf16[3,128,2]{1,2,0:T(2,128)(2,1)}, u32[]{:S(2)}) copy-start(bf16[3,128,2]{1,2,0:T(2,128)(2,1)} %param.21) | copy-start | bytes 4612
  31.0 8.0 %copy-start.12 = (s32[16,2]{0,1:T(2,128)S(1)}, s32[16,2]{0,1:T(2,128)}, u32[]{:S(2)}) copy-start(s32[16,2]{0,1:T(2,128)} %param.27) | copy-start | bytes 388
  31.1 12.3 %collective-permute-start.4 = (bf16[128,256]{1,0:T(8,128)(2,1)S(1)}, bf16[128,256]{1,0:T(8,128)(2,1)S(1)}, u32[]{:S(2)}, u32[]{:S(2)}) collective-permute-start(bf16[128,256]{1,0:T(8,128)(2,1)S(1)} %shard_map.140.refs_0_), channel_id=1, source_target_pairs={{0,1},{1,0},{2,3},{3,2},{4,5},{5,4},{6,7},{7,6},{8,9},{9,8},{10,11... | collective-permute-start | bytes 196616 | tf_op jit(solution)/shard_map/ppermute | solution.py:302
  31.6 11.8 %collective-permute-start.5 = (bf16[128,256]{1,0:T(8,128)(2,1)S(1)}, bf16[128,256]{1,0:T(8,128)(2,1)S(1)}, u32[]{:S(2)}, u32[]{:S(2)}) collective-permute-start(bf16[128,256]{1,0:T(8,128)(2,1)S(1)} %shard_map.140.refs_0_), channel_id=1, source_target_pairs={{0,2},{1,3},{2,0},{3,1},{4,6},{5,7},{6,4},{7,5},{8,10},{9,11},{10,... | collective-permute-start | bytes 196616 | tf_op jit(solution)/shard_map/ppermute | solution.py:302
  32.9 10.5 %collective-permute-start.6 = (bf16[128,256]{1,0:T(8,128)(2,1)S(1)}, bf16[128,256]{1,0:T(8,128)(2,1)}, u32[]{:S(2)}, u32[]{:S(2)}) collective-permute-start(bf16[128,256]{1,0:T(8,128)(2,1)S(1)} %shard_map.140.refs_0_), channel_id=1, source_target_pairs={{0,3},{1,2},{2,1},{3,0},{4,7},{5,6},{6,5},{7,4},{8,11},{9,10},{10,... | collective-permute-start | bytes 196616 | tf_op jit(solution)/shard_map/ppermute | solution.py:302
  35.6 12.7 %collective-permute-start.12 = (bf16[128,2048]{1,0:T(8,128)(2,1)}, bf16[128,2048]{1,0:T(8,128)(2,1)S(1)}, u32[]{:S(2)}, u32[]{:S(2)}) collective-permute-start(bf16[128,2048]{1,0:T(8,128)(2,1)} %refs_13_.1), channel_id=1, source_target_pairs={{1,2},{2,1},{5,6},{6,5},{9,10},{10,9},{13,14},{14,13},{17,18},{18,... | collective-permute-start | bytes 1572872 | tf_op jit(solution)/shard_map/ppermute | solution.py:413
  36.3 15.3 %collective-permute-start.13 = (bf16[128,2048]{1,0:T(8,128)(2,1)S(1)}, bf16[128,2048]{1,0:T(8,128)(2,1)}, u32[]{:S(2)}, u32[]{:S(2)}) collective-permute-start(bf16[128,2048]{1,0:T(8,128)(2,1)S(1)} %collective-permute-done.11.refs_2_), channel_id=1, source_target_pairs={{1,0},{2,3},{5,4},{6,7},{9,8},{10,11},{13,12},{14,15},{17,16},{18,... | collective-permute-start | bytes 1572872 | tf_op jit(solution)/shard_map/ppermute | solution.py:412
  40.5 1.6 %copy-start.1 = (bf16[16,4,128,128]{3,2,1,0:T(8,128)(2,1)S(1)}, bf16[16,4,128,128]{3,2,1,0:T(8,128)(2,1)}, u32[]{:S(2)}) copy-start(bf16[16,4,128,128]{3,2,1,0:T(8,128)(2,1)} %adj) | copy-start | bytes 6291460
  44.6 8.3 %collective-permute-start.8 = (bf16[384,256]{1,0:T(8,128)(2,1)S(1)}, bf16[384,256]{1,0:T(8,128)(2,1)S(1)}, u32[]{:S(2)}, u32[]{:S(2)}) collective-permute-start(bf16[384,256]{1,0:T(8,128)(2,1)S(1)} %shard_map.142.refs_0_), channel_id=1, source_target_pairs={{0,8},{4,12},{8,0},{12,4},{16,24},{20,28},{24,16},{28,20},{1,9},{5... | collective-permute-start | bytes 589832 | tf_op jit(solution)/shard_map/ppermute | solution.py:302
  46.2 6.7 %collective-permute-start.9 = (bf16[384,256]{1,0:T(8,128)(2,1)S(1)}, bf16[384,256]{1,0:T(8,128)(2,1)S(1)}, u32[]{:S(2)}, u32[]{:S(2)}) collective-permute-start(bf16[384,256]{1,0:T(8,128)(2,1)S(1)} %shard_map.142.refs_0_), channel_id=1, source_target_pairs={{0,16},{4,20},{8,24},{12,28},{16,0},{20,4},{24,8},{28,12},{1,17},{... | collective-permute-start | bytes 589832 | tf_op jit(solution)/shard_map/ppermute | solution.py:302
  48.3 19.9 %collective-permute-start.7 = (bf16[384,256]{1,0:T(8,128)(2,1)S(1)}, bf16[384,256]{1,0:T(8,128)(2,1)S(1)}, u32[]{:S(2)}, u32[]{:S(2)}) collective-permute-start(bf16[384,256]{1,0:T(8,128)(2,1)S(1)} %shard_map.142.refs_0_), channel_id=1, source_target_pairs={{0,4},{4,0},{8,12},{12,8},{16,20},{20,16},{24,28},{28,24},{1,5},{5... | collective-permute-start | bytes 589832 | tf_op jit(solution)/shard_map/ppermute | solution.py:302
  52.9 13.9 %collective-permute-start.17 = (bf16[704,256]{1,0:T(8,128)(2,1)S(1)}, bf16[704,256]{1,0:T(8,128)(2,1)S(1)}, u32[]{:S(2)}, u32[]{:S(2)}) collective-permute-start(bf16[704,256]{1,0:T(8,128)(2,1)S(1)} %get-tuple-element.104), channel_id=1, source_target_pairs={{0,4},{4,8},{8,12},{12,16},{16,20},{20,24},{24,28},{28,0},{1,5},{5... | collective-permute-start | bytes 1081352 | tf_op jit(solution)/shard_map/ppermute | solution.py:445
  53.0 13.9 %collective-permute-start.18 = (bf16[704,256]{1,0:T(8,128)(2,1)S(1)}, bf16[704,256]{1,0:T(8,128)(2,1)S(1)}, u32[]{:S(2)}, u32[]{:S(2)}) collective-permute-start(bf16[704,256]{1,0:T(8,128)(2,1)S(1)} %get-tuple-element.105), channel_id=1, source_target_pairs={{4,0},{8,4},{12,8},{16,12},{20,16},{24,20},{28,24},{0,28},{5,1},{9... | collective-permute-start | bytes 1081352 | tf_op jit(solution)/shard_map/ppermute | solution.py:446
  55.6 6.9 %collective-permute-start.14 = (bf16[192,256]{1,0:T(8,128)(2,1)S(1)}, bf16[192,256]{1,0:T(8,128)(2,1)S(1)}, u32[]{:S(2)}, u32[]{:S(2)}) collective-permute-start(bf16[192,256]{1,0:T(8,128)(2,1)S(1)} %slice.19), channel_id=1, source_target_pairs={{0,16},{4,20},{8,24},{12,28},{16,0},{20,4},{24,8},{28,12},{1,17},{... | collective-permute-start | bytes 294920 | tf_op jit(solution)/shard_map/ppermute | solution.py:302
  57.2 9.5 %collective-permute-start.15 = (bf16[192,256]{1,0:T(8,128)(2,1)S(1)}, bf16[192,256]{1,0:T(8,128)(2,1)S(1)}, u32[]{:S(2)}, u32[]{:S(2)}) collective-permute-start(bf16[192,256]{1,0:T(8,128)(2,1)S(1)} %slice.20), channel_id=1, source_target_pairs={{0,8},{4,12},{8,0},{12,4},{16,24},{20,28},{24,16},{28,20},{1,9},{5... | collective-permute-start | bytes 294920 | tf_op jit(solution)/shard_map/ppermute | solution.py:302
  66.7 2.1 %collective-permute-start.16 = (bf16[1152,256]{1,0:T(8,128)(2,1)S(1)}, bf16[1152,256]{1,0:T(8,128)(2,1)S(1)}, u32[]{:S(2)}, u32[]{:S(2)}) collective-permute-start(bf16[1152,256]{1,0:T(8,128)(2,1)S(1)} %pad_maximum_fusion), channel_id=1, source_target_pairs={{0,4},{4,0},{8,12},{12,8},{16,20},{20,16},{24,28},{28,24},{1,5},{5... | collective-permute-start | bytes 1769480 | tf_op jit(solution)/shard_map/ppermute | solution.py:302
  66.8 2.0 %copy-start.2 = (bf16[16,2,128,128]{3,2,1,0:T(8,128)(2,1)S(1)}, bf16[16,2,128,128]{3,2,1,0:T(8,128)(2,1)}, u32[]{:S(2)}) copy-start(bf16[16,2,128,128]{3,2,1,0:T(8,128)(2,1)} %refs_7_.1) | copy-start | bytes 3145732
  66.9 2.0 %copy-start.4 = (s32[2048]{0:T(1024)S(1)}, s32[2048]{0:T(1024)}, u32[]{:S(2)}) copy-start(s32[2048]{0:T(1024)} %param.19) | copy-start | bytes 24580
  66.9 2.0 %copy-start.5 = (bf16[2,2048]{1,0:T(2,128)(2,1)S(1)}, bf16[2,2048]{1,0:T(2,128)(2,1)}, u32[]{:S(2)}) copy-start(bf16[2,2048]{1,0:T(2,128)(2,1)} %refs_12_.1) | copy-start | bytes 24580

commit v5 on v4

--- a/solution.py
+++ b/solution.py
@@ -15,7 +15,7 @@
 
 
 def call(kernel, outs, ins, scratch=(), flops=0, bytes_accessed=0, mib=16):
-    specs = [SMEM if x.dtype == jnp.int32 and x.ndim == 1 else VMEM for x in ins]
+    specs = [SMEM if x.dtype == jnp.int32 and x.size < 1024 else VMEM for x in ins]
     return pl.pallas_call(
         kernel,
         out_shape=outs,
@@ -253,7 +253,7 @@
     def mix(t, _):
         picked = jnp.concatenate(
             [
-                coarse[:, pl.ds(pl.multiple_of(ccols[t * kc + k] * tile, tile), tile)]
+                coarse[:, pl.ds(pl.multiple_of(ccols[k, t] * tile, tile), tile)]
                 for k in range(kc)
             ],
             axis=1,
@@ -401,8 +401,8 @@
     every_value = lax.all_gather(values, "dom", axis=0)
     own_coarse = call(attend_kernel, sds((channels, share), BF), [every_value, weights, pooled])
 
-    own_coarse, w_gates, adj_tiles, w_input, coarse_cols = lax.optimization_barrier(
-        (own_coarse, w_gates, adj_tiles, w_input, coarse_cols)
+    own_coarse, w_gates, adj_cols, w_input, coarse_cols = lax.optimization_barrier(
+        (own_coarse, w_gates, adj_cols, w_input, coarse_cols)
     )
     coarse_blocks = [own_coarse] + [swap(own_coarse, "feat", k) for k in range(1, n_feat)]
     if line:
@@ -424,7 +424,7 @@
         [pltpu.VMEM((3 * tile, tile), F32)],
         flops=10**9,
     )
-    coarse_at = coarse_cols.reshape(-1)
+    coarse_at = coarse_cols.T
     ready = (w_own, w_coarse, band, terms, coarse_at)
     coarse_blocks, ready = lax.optimization_barrier((coarse_blocks, ready))
     w_own, w_coarse, band, terms, coarse_at = ready

time: 76.6 us -> 76.2 us (level)
  waiting for transfers between devices: 10.6 us -> 12.7 us
  local copies, waits for them, and re-layouts: 6.38 us -> 4.93 us
    ppermute x1, waiting for transfers between devices: 3.31 us -> 5.32 us  [body(): outer = lax.ppermute(blocks[2], 'feat', [(1, 0), (2, 3)])]
    reshape x1 -> x0, local copies, waits for them, and re-layouts: 0.78 us -> none  [body(): coarse_at = coarse_cols.reshape(-1)]
    unnamed x28 -> x25, local copies, waits for them, and re-layouts: 3.34 us -> 3.26 us
  transfers between devices with their start and end apart: 19 -> 19, of which waited for: 5 -> 5; matrix products, arithmetic and copies ran while one was open for 5% -> 2% of each run, Pallas kernels for 18% -> 18%
where the time goes in v5:
time: 76.2 us; the launch traced here: 75.7 us
  Pallas kernels  24.3 us (32%)
  starting transfers between devices  23.7 us (31%)
  waiting for transfers between devices  12.7 us (17%)
  blocking collectives  8.89 us (12%)
  local copies, waits for them, and re-layouts  4.93 us (6%)
  between operations  1.03 us (1%)
    pallas_call x11, Pallas kernels, call(): pl.pallas_call(kernel, out_shape=outs, in_specs=specs, out_specs=jax.tree...  24.3 us
    ppermute x15, starting transfers between devices, swap(): return lax.ppermute(array, axis, flip(lax.axis_size(axis), b))  19.1 us
    all_gather x1, blocking collectives, body(): every_value = lax.all_gather(values, 'dom', axis=0)  8.89 us
    ppermute x15, waiting for transfers between devices, swap(): return lax.ppermute(array, axis, flip(lax.axis_size(axis), b))  7.37 us
    ppermute x1, waiting for transfers between devices, body(): outer = lax.ppermute(blocks[2], 'feat', [(1, 0), (2, 3)])  5.32 us
    unnamed x25, local copies, waits for them, and re-layouts  3.26 us
    ppermute x1, starting transfers between devices, body(): right = lax.ppermute(first, 'dom', [(j, i) for i, j in up])  2.63 us
  transfers between devices with their start and end apart: 19, of which 5 were waited for; matrix products, arithmetic and copies ran while one was open for 2% of the time, Pallas kernels for 18%

profile of v5, /device:TPU:0, one launch (start us, length us, event | category | flops | bytes accessed | tf_op | source)
XLA Modules:
  0.0 75.7 jit_solution(13621725283896420422)
XLA Ops:
  0.7 0.1 pad_add_fusion.meta
  0.7 0.7 copy-done.3
  1.4 3.9 %shard_map.136 = (f32[4,144,256]{2,1,0:T(8,128)S(1)}, bf16[4,144,256]{2,1,0:T(8,128)(2,1)S(1)}) custom-call(s32[3]{0:T(128)S(1)} %pad_add_fusion.meta, bf16[128,2048]{1,0:T(8,128)(2,1)} %refs_13_.1, s32[1,2048]{1,0:T(1,128)S(1)} %bitcast.23), custom_call_target="tpu_custom_call" | custom-call | flops 3221225472 | bytes 2097152 | tf_op jit(solution)/shard_map/pallas_call | solution.py:19
  5.4 0.0 copy-start.9
  5.4 0.5 collective-permute-start
  5.9 3.7 %collective-permute-start.11 = (bf16[128,2048]{1,0:T(8,128)(2,1)}, bf16[128,2048]{1,0:T(8,128)(2,1)S(1)}, u32[]{:S(2)}, u32[]{:S(2)}) collective-permute-start(bf16[128,2048]{1,0:T(8,128)(2,1)} %refs_13_.1), channel_id=1, source_target_pairs={{0,2},{1,3},{2,0},{3,1},{4,6},{5,7},{6,4},{7,5},{8,10},{9,11},{10,... | collective-permute-start | bytes 1572872 | tf_op jit(solution)/shard_map/ppermute | solution.py:302
  9.6 0.0 collective-permute-done.arrived
  9.6 0.1 shard_map.137
  9.7 0.1 copy.32
  9.8 1.6 %collective-permute-start.10 = (bf16[128,2048]{1,0:T(8,128)(2,1)}, bf16[128,2048]{1,0:T(8,128)(2,1)S(1)}, u32[]{:S(2)}, u32[]{:S(2)}) collective-permute-start(bf16[128,2048]{1,0:T(8,128)(2,1)} %refs_13_.1), channel_id=1, source_target_pairs={{0,1},{1,0},{2,3},{3,2},{4,5},{5,4},{6,7},{7,6},{8,9},{9,8},{10,11... | collective-permute-start | bytes 1572872 | tf_op jit(solution)/shard_map/ppermute | solution.py:302
  11.4 0.1 copy.33
  11.6 0.0 copy-start
  11.6 1.6 %collective-permute-start.1 = (bf16[144,256]{1,0:T(8,128)(2,1)S(1)}, bf16[144,256]{1,0:T(8,128)(2,1)S(1)}, u32[]{:S(2)}, u32[]{:S(2)}) collective-permute-start(bf16[144,256]{1,0:T(8,128)(2,1)S(1)} %get-tuple-element.65), channel_id=1, source_target_pairs={{0,8},{4,12},{8,0},{12,4},{16,24},{20,28},{24,16},{28,20},{1,9},{5... | collective-permute-start | bytes 221192 | tf_op jit(solution)/shard_map/ppermute | solution.py:302
  13.1 1.5 %collective-permute-start.2 = (bf16[144,256]{1,0:T(8,128)(2,1)S(1)}, bf16[144,256]{1,0:T(8,128)(2,1)S(1)}, u32[]{:S(2)}, u32[]{:S(2)}) collective-permute-start(bf16[144,256]{1,0:T(8,128)(2,1)S(1)} %get-tuple-element.66), channel_id=1, source_target_pairs={{0,16},{4,20},{8,24},{12,28},{16,0},{20,4},{24,8},{28,12},{1,17},{... | collective-permute-start | bytes 221192 | tf_op jit(solution)/shard_map/ppermute | solution.py:302
  14.7 0.5 collective-permute-start.3
  15.1 2.2 %shard_map.138.weights = bf16[2,2048,256]{2,1,0:T(8,128)(2,1)S(1)} custom-call(f32[2,16,256]{2,1,0:T(8,128)S(1)} %pad.8.source, f32[2,16,2048]{2,1,0:T(8,128)S(1)} %pad.9.target), custom_call_target="tpu_custom_call" | custom-call | flops 4194304000 | tf_op jit(solution)/shard_map/pallas_call | solution.py:19
  17.4 0.0 collective-permute-done.1.refs_1_
  17.4 0.1 collective-permute-done.2.refs_2_
  17.5 2.4 %collective-permute-done.3.refs_3_ = bf16[144,256]{1,0:T(8,128)(2,1)S(1)} collective-permute-done((bf16[144,256]{1,0:T(8,128)(2,1)S(1)}, bf16[144,256]{1,0:T(8,128)(2,1)S(1)}, u32[]{:S(2)}, u32[]{:S(2)}) %collective-permute-start.3) | collective-permute-done | bytes 73760 | tf_op jit(solution)/shard_map/ppermute | solution.py:302
  19.9 0.2 shard_map.139
  20.1 8.9 %all-gather = bf16[1024,256]{1,0:T(8,128)(2,1)S(1)} all-gather(bf16[128,256]{1,0:T(8,128)(2,1)S(1)} %get-tuple-element.74), channel_id=2, replica_groups=mesh['dom'=8,'feat'=4] {'dom'}, dimensions={0}, use_global_device_ids=true | all-gather | bytes 589824 | tf_op jit(solution)/shard_map/all_gather | solution.py:401
  29.0 0.5 shard_map.140.refs_0_
  29.5 0.9 %copy-done.7 = bf16[3,128,4,512]{3,2,1,0:T(4,128)(2,1)S(1)} copy-done((bf16[3,128,4,512]{3,2,1,0:T(4,128)(2,1)S(1)}, bf16[3,128,4,512]{3,2,1,0:T(4,128)(2,1)}, u32[]{:S(2)}) %copy-start.7) | copy-done | bytes 1572888
  30.4 0.3 copy.41
  30.8 0.0 copy-start.11
  30.8 0.1 slice.21
  30.9 0.5 collective-permute-start.4
  31.4 1.5 %collective-permute-start.5 = (bf16[128,256]{1,0:T(8,128)(2,1)S(1)}, bf16[128,256]{1,0:T(8,128)(2,1)S(1)}, u32[]{:S(2)}, u32[]{:S(2)}) collective-permute-start(bf16[128,256]{1,0:T(8,128)(2,1)S(1)} %shard_map.140.refs_0_), channel_id=1, source_target_pairs={{0,2},{1,3},{2,0},{3,1},{4,6},{5,7},{6,4},{7,5},{8,10},{9,11},{10,... | collective-permute-start | bytes 196616 | tf_op jit(solution)/shard_map/ppermute | solution.py:302
  32.9 2.5 %collective-permute-start.6 = (bf16[128,256]{1,0:T(8,128)(2,1)S(1)}, bf16[128,256]{1,0:T(8,128)(2,1)}, u32[]{:S(2)}, u32[]{:S(2)}) collective-permute-start(bf16[128,256]{1,0:T(8,128)(2,1)S(1)} %shard_map.140.refs_0_), channel_id=1, source_target_pairs={{0,3},{1,2},{2,1},{3,0},{4,7},{5,6},{6,5},{7,4},{8,11},{9,10},{10,... | collective-permute-start | bytes 196616 | tf_op jit(solution)/shard_map/ppermute | solution.py:302
  35.4 0.0 collective-permute-done.11.refs_2_
  35.4 0.0 collective-permute-done.10.refs_1_
  35.4 0.7 collective-permute-start.12
  36.1 1.3 %collective-permute-start.13 = (bf16[128,2048]{1,0:T(8,128)(2,1)S(1)}, bf16[128,2048]{1,0:T(8,128)(2,1)}, u32[]{:S(2)}, u32[]{:S(2)}) collective-permute-start(bf16[128,2048]{1,0:T(8,128)(2,1)S(1)} %collective-permute-done.11.refs_2_), channel_id=1, source_target_pairs={{1,0},{2,3},{5,4},{6,7},{9,8},{10,11},{13,12},{14,15},{17,16},{18,... | collective-permute-start | bytes 1572872 | tf_op jit(solution)/shard_map/ppermute | solution.py:412
  37.4 0.1 copy.37.terms
  37.5 0.8 %copy.35 = s32[16,4]{1,0:T(8,128)S(1)} copy(s32[16,4]{0,1:T(4,128)} %param.17) | data formatting | bytes 512 | tf_op jit(solution)/shard_map/optimization_barrier | solution.py:404
  38.3 0.1 reshape.13.cols
  38.4 0.0 copy-start.1
  38.4 1.6 %copy-done.1 = bf16[16,4,128,128]{3,2,1,0:T(8,128)(2,1)S(1)} copy-done((bf16[16,4,128,128]{3,2,1,0:T(8,128)(2,1)S(1)}, bf16[16,4,128,128]{3,2,1,0:T(8,128)(2,1)}, u32[]{:S(2)}) %copy-start.1) | copy-done | bytes 2097176
  40.0 1.3 %shard_map.141 = (bf16[16,384,128]{2,1,0:T(8,128)(2,1)S(1)}, bf16[192,256]{1,0:T(8,128)(2,1)S(1)}, bf16[192,256]{1,0:T(8,128)(2,1)S(1)}, f32[384,3]{1,0:T(8,128)S(1)}) custom-call(s32[3]{0:T(128)S(1)} %pad_add_fusion.meta, s32[64]{0:T(128)S(1)} %reshape.13.cols, bf16[16,4,128,128]{3,2,1,0:T(8,128)(2,1)S(1)} %copy-done.1, f32[384,3]{1,0:T(8,128)S(1)} %copy.37.terms), custom_call_target="tpu_custom_call" | custom-call | flops 1000000000 | tf_op jit(solution)/shard_map/pallas_call | solution.py:19
  41.3 0.0 collective-permute-done.4.refs_1_
  41.4 0.0 collective-permute-done.6.refs_3_
  41.4 1.1 %shard_map.142.refs_0_ = bf16[384,256]{1,0:T(8,128)(2,1)S(1)} custom-call(s32[3]{0:T(128)S(1)} %pad_add_fusion.meta, bf16[128,256]{1,0:T(8,128)(2,1)S(1)} %shard_map.140.refs_0_, bf16[128,256]{1,0:T(8,128)(2,1)S(1)} %collective-permute-done.4.refs_1_, bf16[128,256]{1,0:T(8,128)(2,1)S(1)} %collective-permute-done.5.refs_2_, ...), custom_call_target="tpu_custom_call" | custom-call | tf_op jit(solution)/shard_map/pallas_call | solution.py:19
  42.5 1.6 %collective-permute-start.8 = (bf16[384,256]{1,0:T(8,128)(2,1)S(1)}, bf16[384,256]{1,0:T(8,128)(2,1)S(1)}, u32[]{:S(2)}, u32[]{:S(2)}) collective-permute-start(bf16[384,256]{1,0:T(8,128)(2,1)S(1)} %shard_map.142.refs_0_), channel_id=1, source_target_pairs={{0,8},{4,12},{8,0},{12,4},{16,24},{20,28},{24,16},{28,20},{1,9},{5... | collective-permute-start | bytes 589832 | tf_op jit(solution)/shard_map/ppermute | solution.py:302
  44.1 2.0 %collective-permute-start.9 = (bf16[384,256]{1,0:T(8,128)(2,1)S(1)}, bf16[384,256]{1,0:T(8,128)(2,1)S(1)}, u32[]{:S(2)}, u32[]{:S(2)}) collective-permute-start(bf16[384,256]{1,0:T(8,128)(2,1)S(1)} %shard_map.142.refs_0_), channel_id=1, source_target_pairs={{0,16},{4,20},{8,24},{12,28},{16,0},{20,4},{24,8},{28,12},{1,17},{... | collective-permute-start | bytes 589832 | tf_op jit(solution)/shard_map/ppermute | solution.py:302
  46.1 5.3 %collective-permute-done.13.refs_4_ = bf16[128,2048]{1,0:T(8,128)(2,1)} collective-permute-done((bf16[128,2048]{1,0:T(8,128)(2,1)S(1)}, bf16[128,2048]{1,0:T(8,128)(2,1)}, u32[]{:S(2)}, u32[]{:S(2)}) %collective-permute-start.13) | collective-permute-done | bytes 524320 | tf_op jit(solution)/shard_map/ppermute | solution.py:412
  51.4 1.3 %shard_map.143 = (bf16[704,256]{1,0:T(8,128)(2,1)S(1)}, bf16[704,256]{1,0:T(8,128)(2,1)S(1)}) custom-call(s32[3]{0:T(128)S(1)} %pad_add_fusion.meta, bf16[128,2048]{1,0:T(8,128)(2,1)} %refs_13_.1, bf16[128,2048]{1,0:T(8,128)(2,1)S(1)} %collective-permute-done.10.refs_1_, bf16[128,2048]{1,0:T(8,128)(2,1)S(1)} %collective-permute-done.11.refs_2_, ...), custom_call_target="tpu_custom_call" | custom-call | tf_op jit(solution)/shard_map/pallas_call | solution.py:19
  52.7 0.0 collective-permute-done.8.refs_2_
  52.7 0.0 collective-permute-done.9.refs_3_
  52.7 0.1 collective-permute-start.17
  52.8 2.6 %collective-permute-start.18 = (bf16[704,256]{1,0:T(8,128)(2,1)S(1)}, bf16[704,256]{1,0:T(8,128)(2,1)S(1)}, u32[]{:S(2)}, u32[]{:S(2)}) collective-permute-start(bf16[704,256]{1,0:T(8,128)(2,1)S(1)} %get-tuple-element.105), channel_id=1, source_target_pairs={{4,0},{8,4},{12,8},{16,12},{20,16},{24,20},{28,24},{0,28},{5,1},{9... | collective-permute-start | bytes 1081352 | tf_op jit(solution)/shard_map/ppermute | solution.py:446
  55.4 1.5 %collective-permute-start.14 = (bf16[192,256]{1,0:T(8,128)(2,1)S(1)}, bf16[192,256]{1,0:T(8,128)(2,1)S(1)}, u32[]{:S(2)}, u32[]{:S(2)}) collective-permute-start(bf16[192,256]{1,0:T(8,128)(2,1)S(1)} %slice.19), channel_id=1, source_target_pairs={{0,16},{4,20},{8,24},{12,28},{16,0},{20,4},{24,8},{28,12},{1,17},{... | collective-permute-start | bytes 294920 | tf_op jit(solution)/shard_map/ppermute | solution.py:302
  57.0 0.1 collective-permute-start.15
  57.0 5.2 %shard_map.144 = (f32[384,1536]{1,0:T(8,128)S(1)}, bf16[512,512]{1,0:T(8,128)(2,1)S(1)}, bf16[512,512]{1,0:T(8,128)(2,1)S(1)}) custom-call(s32[3]{0:T(128)S(1)} %pad_add_fusion.meta, bf16[128,2048]{1,0:T(8,128)(2,1)} %refs_13_.1, bf16[128,2048]{1,0:T(8,128)(2,1)S(1)} %collective-permute-done.10.refs_1_, ...), custom_call_target="tpu_custom_call" | custom-call | flops 4563402752 | bytes 8388608 | tf_op jit(solution)/shard_map/pallas_call | solution.py:19
  62.2 4.2 %collective-permute-done.15.refs_5_ = bf16[192,256]{1,0:T(8,128)(2,1)S(1)} collective-permute-done((bf16[192,256]{1,0:T(8,128)(2,1)S(1)}, bf16[192,256]{1,0:T(8,128)(2,1)S(1)}, u32[]{:S(2)}, u32[]{:S(2)}) %collective-permute-start.15) | collective-permute-done | bytes 98336 | tf_op jit(solution)/shard_map/ppermute | solution.py:302
  66.5 0.1 collective-permute-start.16
  66.6 0.0 collective-permute-done.18.right
  66.6 0.0 copy-start.2
  66.6 0.0 copy-start.4
  66.7 0.0 copy-start.5
  66.7 0.0 copy-start.6
  66.7 1.3 %shard_map.145.refs_10_ = f32[384,512]{1,0:T(8,128)S(1)} custom-call(bf16[704,256]{1,0:T(8,128)(2,1)S(1)} %collective-permute-done.17.left, bf16[704,256]{1,0:T(8,128)(2,1)S(1)} %collective-permute-done.18.right, bf16[512,512]{1,0:T(8,128)(2,1)S(1)} %get-tuple-element.106.state_rim, bf16[512,512]{1,0:T(8,128)(2,1)S(1)} %get-tuple-element.107.one_rim, ...), custom_call_target="tpu_custom_call" | custom-call | flops 12079595520 | bytes 1048576 | tf_op jit(solution)/shard_map/pallas_call | solution.py:19
  68.0 0.0 collective-permute-done.7.refs_1_
  68.0 0.6 collective-permute-done.16.refs_6_
  68.6 7.1 %shard_map.146 = bf16[128,2048]{1,0:T(8,128)(2,1)} custom-call(s32[3]{0:T(128)S(1)} %pad_add_fusion.meta, s32[2,16]{1,0:T(2,128)S(1)} %bitcast.25, bf16[384,256]{1,0:T(8,128)(2,1)S(1)} %shard_map.142.refs_0_, bf16[384,256]{1,0:T(8,128)(2,1)S(1)} %collective-permute-done.7.refs_1_, bf16[384,256]{1,0:T(8,128)(2,1)S(1)} %collective-permute-done.8.refs_2_, ...), custom_call_target="tpu_custom_call" | custom-call | flops 3221225472 | bytes 6291456 | tf_op jit(solution)/shard_map/pallas_call | solution.py:19
  (28 shorter events, 0.2 us)
Async XLA Ops:
  0.7 0.7 copy-start.3
  1.4 8.1 %copy-start.10 = (f32[3,128]{1,0:T(4,128)S(1)}, f32[3,128]{1,0:T(4,128)}, u32[]{:S(2)}) copy-start(f32[3,128]{1,0:T(4,128)} %param.22) | copy-start | bytes 4612
  1.4 8.2 %copy-start.8 = (f32[2,10,2048]{2,0,1:T(2,128)S(1)}, f32[2,10,2048]{2,0,1:T(2,128)}, u32[]{:S(2)}) copy-start(f32[2,10,2048]{2,0,1:T(2,128)} %param.24) | copy-start | bytes 491524
  5.4 6.1 %copy-start.9 = (f32[2,10,2048]{2,0,1:T(2,128)S(1)}, f32[2,10,2048]{2,0,1:T(2,128)}, u32[]{:S(2)}) copy-start(f32[2,10,2048]{2,0,1:T(2,128)} %param.25) | copy-start | bytes 491524
  5.4 4.2 %collective-permute-start = (bf16[4,144,256]{2,1,0:T(8,128)(2,1)S(1)}, bf16[4,144,256]{2,1,0:T(8,128)(2,1)S(1)}, u32[]{:S(2)}, u32[]{:S(2)}) collective-permute-start(bf16[4,144,256]{2,1,0:T(8,128)(2,1)S(1)} %get-tuple-element.59), channel_id=1, source_target_pairs={{0,4},{4,0},{8,12},{12,8},{16,20},{20,16},{24,28},{28,24},{1,5},{5... | collective-permute-start | bytes 884744 | tf_op jit(solution)/shard_map/ppermute | solution.py:302
  5.9 29.5 %collective-permute-start.11 = (bf16[128,2048]{1,0:T(8,128)(2,1)}, bf16[128,2048]{1,0:T(8,128)(2,1)S(1)}, u32[]{:S(2)}, u32[]{:S(2)}) collective-permute-start(bf16[128,2048]{1,0:T(8,128)(2,1)} %refs_13_.1), channel_id=1, source_target_pairs={{0,2},{1,3},{2,0},{3,1},{4,6},{5,7},{6,4},{7,5},{8,10},{9,11},{10,... | collective-permute-start | bytes 1572872 | tf_op jit(solution)/shard_map/ppermute | solution.py:302
  9.8 25.6 %collective-permute-start.10 = (bf16[128,2048]{1,0:T(8,128)(2,1)}, bf16[128,2048]{1,0:T(8,128)(2,1)S(1)}, u32[]{:S(2)}, u32[]{:S(2)}) collective-permute-start(bf16[128,2048]{1,0:T(8,128)(2,1)} %refs_13_.1), channel_id=1, source_target_pairs={{0,1},{1,0},{2,3},{3,2},{4,5},{5,4},{6,7},{7,6},{8,9},{9,8},{10,11... | collective-permute-start | bytes 1572872 | tf_op jit(solution)/shard_map/ppermute | solution.py:302
  11.6 8.3 %copy-start = (bf16[2,64,64]{2,1,0:T(8,128)(2,1)S(1)}, bf16[2,64,64]{2,1,0:T(8,128)(2,1)}, u32[]{:S(2)}) copy-start(bf16[2,64,64]{2,1,0:T(8,128)(2,1)} %w_value.1) | copy-start | bytes 49156
  11.6 5.8 %collective-permute-start.1 = (bf16[144,256]{1,0:T(8,128)(2,1)S(1)}, bf16[144,256]{1,0:T(8,128)(2,1)S(1)}, u32[]{:S(2)}, u32[]{:S(2)}) collective-permute-start(bf16[144,256]{1,0:T(8,128)(2,1)S(1)} %get-tuple-element.65), channel_id=1, source_target_pairs={{0,8},{4,12},{8,0},{12,4},{16,24},{20,28},{24,16},{28,20},{1,9},{5... | collective-permute-start | bytes 221192 | tf_op jit(solution)/shard_map/ppermute | solution.py:302
  13.1 4.4 %collective-permute-start.2 = (bf16[144,256]{1,0:T(8,128)(2,1)S(1)}, bf16[144,256]{1,0:T(8,128)(2,1)S(1)}, u32[]{:S(2)}, u32[]{:S(2)}) collective-permute-start(bf16[144,256]{1,0:T(8,128)(2,1)S(1)} %get-tuple-element.66), channel_id=1, source_target_pairs={{0,16},{4,20},{8,24},{12,28},{16,0},{20,4},{24,8},{28,12},{1,17},{... | collective-permute-start | bytes 221192 | tf_op jit(solution)/shard_map/ppermute | solution.py:302
  14.7 5.3 %collective-permute-start.3 = (bf16[144,256]{1,0:T(8,128)(2,1)S(1)}, bf16[144,256]{1,0:T(8,128)(2,1)S(1)}, u32[]{:S(2)}, u32[]{:S(2)}) collective-permute-start(bf16[144,256]{1,0:T(8,128)(2,1)S(1)} %get-tuple-element.67), channel_id=1, source_target_pairs={{0,24},{4,28},{8,16},{12,20},{16,8},{20,12},{24,0},{28,4},{1,25},{... | collective-permute-start | bytes 221192 | tf_op jit(solution)/shard_map/ppermute | solution.py:302
  29.0 1.4 %copy-start.7 = (bf16[3,128,4,512]{3,2,1,0:T(4,128)(2,1)S(1)}, bf16[3,128,4,512]{3,2,1,0:T(4,128)(2,1)}, u32[]{:S(2)}) copy-start(bf16[3,128,4,512]{3,2,1,0:T(4,128)(2,1)} %param.20) | copy-start | bytes 4718596
  30.8 6.6 %copy-start.11 = (bf16[3,128,2]{1,2,0:T(2,128)(2,1)S(1)}, bf16[3,128,2]{1,2,0:T(2,128)(2,1)}, u32[]{:S(2)}) copy-start(bf16[3,128,2]{1,2,0:T(2,128)(2,1)} %param.21) | copy-start | bytes 4612
  30.9 10.4 %collective-permute-start.4 = (bf16[128,256]{1,0:T(8,128)(2,1)S(1)}, bf16[128,256]{1,0:T(8,128)(2,1)S(1)}, u32[]{:S(2)}, u32[]{:S(2)}) collective-permute-start(bf16[128,256]{1,0:T(8,128)(2,1)S(1)} %shard_map.140.refs_0_), channel_id=1, source_target_pairs={{0,1},{1,0},{2,3},{3,2},{4,5},{5,4},{6,7},{7,6},{8,9},{9,8},{10,11... | collective-permute-start | bytes 196616 | tf_op jit(solution)/shard_map/ppermute | solution.py:302
  31.4 9.9 %collective-permute-start.5 = (bf16[128,256]{1,0:T(8,128)(2,1)S(1)}, bf16[128,256]{1,0:T(8,128)(2,1)S(1)}, u32[]{:S(2)}, u32[]{:S(2)}) collective-permute-start(bf16[128,256]{1,0:T(8,128)(2,1)S(1)} %shard_map.140.refs_0_), channel_id=1, source_target_pairs={{0,2},{1,3},{2,0},{3,1},{4,6},{5,7},{6,4},{7,5},{8,10},{9,11},{10,... | collective-permute-start | bytes 196616 | tf_op jit(solution)/shard_map/ppermute | solution.py:302
  32.9 8.5 %collective-permute-start.6 = (bf16[128,256]{1,0:T(8,128)(2,1)S(1)}, bf16[128,256]{1,0:T(8,128)(2,1)}, u32[]{:S(2)}, u32[]{:S(2)}) collective-permute-start(bf16[128,256]{1,0:T(8,128)(2,1)S(1)} %shard_map.140.refs_0_), channel_id=1, source_target_pairs={{0,3},{1,2},{2,1},{3,0},{4,7},{5,6},{6,5},{7,4},{8,11},{9,10},{10,... | collective-permute-start | bytes 196616 | tf_op jit(solution)/shard_map/ppermute | solution.py:302
  35.4 10.7 %collective-permute-start.12 = (bf16[128,2048]{1,0:T(8,128)(2,1)}, bf16[128,2048]{1,0:T(8,128)(2,1)S(1)}, u32[]{:S(2)}, u32[]{:S(2)}) collective-permute-start(bf16[128,2048]{1,0:T(8,128)(2,1)} %refs_13_.1), channel_id=1, source_target_pairs={{1,2},{2,1},{5,6},{6,5},{9,10},{10,9},{13,14},{14,13},{17,18},{18,... | collective-permute-start | bytes 1572872 | tf_op jit(solution)/shard_map/ppermute | solution.py:413
  36.1 15.3 %collective-permute-start.13 = (bf16[128,2048]{1,0:T(8,128)(2,1)S(1)}, bf16[128,2048]{1,0:T(8,128)(2,1)}, u32[]{:S(2)}, u32[]{:S(2)}) collective-permute-start(bf16[128,2048]{1,0:T(8,128)(2,1)S(1)} %collective-permute-done.11.refs_2_), channel_id=1, source_target_pairs={{1,0},{2,3},{5,4},{6,7},{9,8},{10,11},{13,12},{14,15},{17,16},{18,... | collective-permute-start | bytes 1572872 | tf_op jit(solution)/shard_map/ppermute | solution.py:412
  38.4 1.6 %copy-start.1 = (bf16[16,4,128,128]{3,2,1,0:T(8,128)(2,1)S(1)}, bf16[16,4,128,128]{3,2,1,0:T(8,128)(2,1)}, u32[]{:S(2)}) copy-start(bf16[16,4,128,128]{3,2,1,0:T(8,128)(2,1)} %adj.1) | copy-start | bytes 6291460
  42.5 10.2 %collective-permute-start.8 = (bf16[384,256]{1,0:T(8,128)(2,1)S(1)}, bf16[384,256]{1,0:T(8,128)(2,1)S(1)}, u32[]{:S(2)}, u32[]{:S(2)}) collective-permute-start(bf16[384,256]{1,0:T(8,128)(2,1)S(1)} %shard_map.142.refs_0_), channel_id=1, source_target_pairs={{0,8},{4,12},{8,0},{12,4},{16,24},{20,28},{24,16},{28,20},{1,9},{5... | collective-permute-start | bytes 589832 | tf_op jit(solution)/shard_map/ppermute | solution.py:302
  44.1 8.6 %collective-permute-start.9 = (bf16[384,256]{1,0:T(8,128)(2,1)S(1)}, bf16[384,256]{1,0:T(8,128)(2,1)S(1)}, u32[]{:S(2)}, u32[]{:S(2)}) collective-permute-start(bf16[384,256]{1,0:T(8,128)(2,1)S(1)} %shard_map.142.refs_0_), channel_id=1, source_target_pairs={{0,16},{4,20},{8,24},{12,28},{16,0},{20,4},{24,8},{28,12},{1,17},{... | collective-permute-start | bytes 589832 | tf_op jit(solution)/shard_map/ppermute | solution.py:302
  46.1 21.9 %collective-permute-start.7 = (bf16[384,256]{1,0:T(8,128)(2,1)S(1)}, bf16[384,256]{1,0:T(8,128)(2,1)S(1)}, u32[]{:S(2)}, u32[]{:S(2)}) collective-permute-start(bf16[384,256]{1,0:T(8,128)(2,1)S(1)} %shard_map.142.refs_0_), channel_id=1, source_target_pairs={{0,4},{4,0},{8,12},{12,8},{16,20},{20,16},{24,28},{28,24},{1,5},{5... | collective-permute-start | bytes 589832 | tf_op jit(solution)/shard_map/ppermute | solution.py:302
  52.7 13.9 %collective-permute-start.17 = (bf16[704,256]{1,0:T(8,128)(2,1)S(1)}, bf16[704,256]{1,0:T(8,128)(2,1)S(1)}, u32[]{:S(2)}, u32[]{:S(2)}) collective-permute-start(bf16[704,256]{1,0:T(8,128)(2,1)S(1)} %get-tuple-element.104), channel_id=1, source_target_pairs={{0,4},{4,8},{8,12},{12,16},{16,20},{20,24},{24,28},{28,0},{1,5},{5... | collective-permute-start | bytes 1081352 | tf_op jit(solution)/shard_map/ppermute | solution.py:445
  52.8 13.9 %collective-permute-start.18 = (bf16[704,256]{1,0:T(8,128)(2,1)S(1)}, bf16[704,256]{1,0:T(8,128)(2,1)S(1)}, u32[]{:S(2)}, u32[]{:S(2)}) collective-permute-start(bf16[704,256]{1,0:T(8,128)(2,1)S(1)} %get-tuple-element.105), channel_id=1, source_target_pairs={{4,0},{8,4},{12,8},{16,12},{20,16},{24,20},{28,24},{0,28},{5,1},{9... | collective-permute-start | bytes 1081352 | tf_op jit(solution)/shard_map/ppermute | solution.py:446
  55.4 6.8 %collective-permute-start.14 = (bf16[192,256]{1,0:T(8,128)(2,1)S(1)}, bf16[192,256]{1,0:T(8,128)(2,1)S(1)}, u32[]{:S(2)}, u32[]{:S(2)}) collective-permute-start(bf16[192,256]{1,0:T(8,128)(2,1)S(1)} %slice.19), channel_id=1, source_target_pairs={{0,16},{4,20},{8,24},{12,28},{16,0},{20,4},{24,8},{28,12},{1,17},{... | collective-permute-start | bytes 294920 | tf_op jit(solution)/shard_map/ppermute | solution.py:302
  57.0 9.5 %collective-permute-start.15 = (bf16[192,256]{1,0:T(8,128)(2,1)S(1)}, bf16[192,256]{1,0:T(8,128)(2,1)S(1)}, u32[]{:S(2)}, u32[]{:S(2)}) collective-permute-start(bf16[192,256]{1,0:T(8,128)(2,1)S(1)} %slice.20), channel_id=1, source_target_pairs={{0,8},{4,12},{8,0},{12,4},{16,24},{20,28},{24,16},{28,20},{1,9},{5... | collective-permute-start | bytes 294920 | tf_op jit(solution)/shard_map/ppermute | solution.py:302
  66.5 2.1 %collective-permute-start.16 = (bf16[1152,256]{1,0:T(8,128)(2,1)S(1)}, bf16[1152,256]{1,0:T(8,128)(2,1)S(1)}, u32[]{:S(2)}, u32[]{:S(2)}) collective-permute-start(bf16[1152,256]{1,0:T(8,128)(2,1)S(1)} %pad_maximum_fusion), channel_id=1, source_target_pairs={{0,4},{4,0},{8,12},{12,8},{16,20},{20,16},{24,28},{28,24},{1,5},{5... | collective-permute-start | bytes 1769480 | tf_op jit(solution)/shard_map/ppermute | solution.py:302
  66.6 2.0 %copy-start.2 = (bf16[16,2,128,128]{3,2,1,0:T(8,128)(2,1)S(1)}, bf16[16,2,128,128]{3,2,1,0:T(8,128)(2,1)}, u32[]{:S(2)}) copy-start(bf16[16,2,128,128]{3,2,1,0:T(8,128)(2,1)} %refs_7_.1) | copy-start | bytes 3145732
  66.6 2.0 %copy-start.4 = (s32[2048]{0:T(1024)S(1)}, s32[2048]{0:T(1024)}, u32[]{:S(2)}) copy-start(s32[2048]{0:T(1024)} %param.19) | copy-start | bytes 24580
  66.7 2.0 %copy-start.5 = (bf16[2,2048]{1,0:T(2,128)(2,1)S(1)}, bf16[2,2048]{1,0:T(2,128)(2,1)}, u32[]{:S(2)}) copy-start(bf16[2,2048]{1,0:T(2,128)(2,1)} %refs_12_.1) | copy-start | bytes 24580
  66.7 1.9 %copy-start.6 = (s32[16,2]{0,1:T(2,128)S(1)}, s32[16,2]{0,1:T(2,128)}, u32[]{:S(2)}) copy-start(s32[16,2]{0,1:T(2,128)} %param.27) | copy-start | bytes 388

commit v6 on v5

--- a/solution.py
+++ b/solution.py
@@ -316,7 +316,8 @@
     (beside, behind), ready = lax.optimization_barrier(((beside, behind), ready))
     top = send(beside[:half], 4)
     bottom = send(behind[half:], 2)
-    other = send(jnp.concatenate([beside, behind, top, bottom], axis=0), 1)
+    other = send(jnp.concatenate([beside, behind], axis=0), 1)
+    corner = send(jnp.concatenate([top, bottom], axis=0), 1)
     places = [
         (0, 0, 0, rows, 0, False),
         (1, 0, 0, rows, 1, False),
@@ -326,9 +327,9 @@
         (5, 0, half, half, 6, False),
         (6, 0, 0, rows, 3, False),
         (6, rows, 0, rows, 5, False),
-        (6, 2 * rows, 0, rows, 7, False),
+        (7, 0, 0, rows, 7, False),
     ]
-    return [block, core, beside, behind, top, bottom, other], places, *ready
+    return [block, core, beside, behind, top, bottom, other, corner], places, *ready
 
 
 def body(

time: 76.2 us -> 74.8 us (0.982)
  waiting for transfers between devices: 12.7 us -> 11.6 us
  local copies, waits for them, and re-layouts: 4.93 us -> 4.01 us
    unnamed x25, local copies, waits for them, and re-layouts: 3.26 us -> 2.34 us
    ppermute x1, waiting for transfers between devices: 5.32 us -> 4.43 us  [body(): outer = lax.ppermute(blocks[2], 'feat', [(1, 0), (2, 3)])]
    ppermute x15 -> x16, starting transfers between devices: 19.1 us -> 19.5 us  [swap(): return lax.ppermute(array, axis, flip(lax.axis_size(axis), b))]
    ppermute x15 -> x16, waiting for transfers between devices: 7.37 us -> 7.16 us  [swap(): return lax.ppermute(array, axis, flip(lax.axis_size(axis), b))]
  transfers between devices with their start and end apart: 19 -> 20, of which waited for: 5 -> 5; matrix products, arithmetic and copies ran while one was open for 2% -> 2% of each run, Pallas kernels for 18% -> 18%
where the time goes in v6:
time: 74.8 us; the launch traced here: 74.4 us
  Pallas kernels  24.4 us (33%)
  starting transfers between devices  24.2 us (32%)
  waiting for transfers between devices  11.6 us (16%)
  blocking collectives  9.01 us (12%)
  local copies, waits for them, and re-layouts  4.01 us (5%)
  between operations  1.07 us (1%)
    pallas_call x11, Pallas kernels, call(): pl.pallas_call(kernel, out_shape=outs, in_specs=specs, out_specs=jax.tree...  24.4 us
    ppermute x16, starting transfers between devices, swap(): return lax.ppermute(array, axis, flip(lax.axis_size(axis), b))  19.5 us
    all_gather x1, blocking collectives, body(): every_value = lax.all_gather(values, 'dom', axis=0)  9.01 us
    ppermute x16, waiting for transfers between devices, swap(): return lax.ppermute(array, axis, flip(lax.axis_size(axis), b))  7.16 us
    ppermute x1, waiting for transfers between devices, body(): outer = lax.ppermute(blocks[2], 'feat', [(1, 0), (2, 3)])  4.43 us
    ppermute x1, starting transfers between devices, body(): right = lax.ppermute(first, 'dom', [(j, i) for i, j in up])  2.63 us
    unnamed x25, local copies, waits for them, and re-layouts  2.34 us
  transfers between devices with their start and end apart: 20, of which 5 were waited for; matrix products, arithmetic and copies ran while one was open for 2% of the time, Pallas kernels for 18%

profile of v6, /device:TPU:0, one launch (start us, length us, event | category | flops | bytes accessed | tf_op | source)
XLA Modules:
  0.0 74.4 jit_solution(3418191060869203615)
XLA Ops:
  0.7 0.1 pad_add_fusion.meta
  0.7 0.7 copy-done.3
  1.4 3.9 %shard_map.136 = (f32[4,144,256]{2,1,0:T(8,128)S(1)}, bf16[4,144,256]{2,1,0:T(8,128)(2,1)S(1)}) custom-call(s32[3]{0:T(128)S(1)} %pad_add_fusion.meta, bf16[128,2048]{1,0:T(8,128)(2,1)} %refs_14_.1, s32[1,2048]{1,0:T(1,128)S(1)} %bitcast.23), custom_call_target="tpu_custom_call" | custom-call | flops 3221225472 | bytes 2097152 | tf_op jit(solution)/shard_map/pallas_call | solution.py:19
  5.4 0.5 collective-permute-start
  5.9 3.7 %collective-permute-start.11 = (bf16[128,2048]{1,0:T(8,128)(2,1)}, bf16[128,2048]{1,0:T(8,128)(2,1)S(1)}, u32[]{:S(2)}, u32[]{:S(2)}) collective-permute-start(bf16[128,2048]{1,0:T(8,128)(2,1)} %refs_14_.1), channel_id=1, source_target_pairs={{0,2},{1,3},{2,0},{3,1},{4,6},{5,7},{6,4},{7,5},{8,10},{9,11},{10,... | collective-permute-start | bytes 1572872 | tf_op jit(solution)/shard_map/ppermute | solution.py:302
  9.6 0.0 collective-permute-done.arrived
  9.6 0.1 shard_map.137
  9.7 0.1 copy.32
  9.8 1.6 %collective-permute-start.10 = (bf16[128,2048]{1,0:T(8,128)(2,1)}, bf16[128,2048]{1,0:T(8,128)(2,1)S(1)}, u32[]{:S(2)}, u32[]{:S(2)}) collective-permute-start(bf16[128,2048]{1,0:T(8,128)(2,1)} %refs_14_.1), channel_id=1, source_target_pairs={{0,1},{1,0},{2,3},{3,2},{4,5},{5,4},{6,7},{7,6},{8,9},{9,8},{10,11... | collective-permute-start | bytes 1572872 | tf_op jit(solution)/shard_map/ppermute | solution.py:302
  11.4 0.1 copy.33
  11.6 0.0 copy-start
  11.6 1.6 %collective-permute-start.1 = (bf16[144,256]{1,0:T(8,128)(2,1)S(1)}, bf16[144,256]{1,0:T(8,128)(2,1)S(1)}, u32[]{:S(2)}, u32[]{:S(2)}) collective-permute-start(bf16[144,256]{1,0:T(8,128)(2,1)S(1)} %get-tuple-element.65), channel_id=1, source_target_pairs={{0,8},{4,12},{8,0},{12,4},{16,24},{20,28},{24,16},{28,20},{1,9},{5... | collective-permute-start | bytes 221192 | tf_op jit(solution)/shard_map/ppermute | solution.py:302
  13.1 1.5 %collective-permute-start.2 = (bf16[144,256]{1,0:T(8,128)(2,1)S(1)}, bf16[144,256]{1,0:T(8,128)(2,1)S(1)}, u32[]{:S(2)}, u32[]{:S(2)}) collective-permute-start(bf16[144,256]{1,0:T(8,128)(2,1)S(1)} %get-tuple-element.66), channel_id=1, source_target_pairs={{0,16},{4,20},{8,24},{12,28},{16,0},{20,4},{24,8},{28,12},{1,17},{... | collective-permute-start | bytes 221192 | tf_op jit(solution)/shard_map/ppermute | solution.py:302
  14.7 0.5 collective-permute-start.3
  15.1 2.2 %shard_map.138.weights = bf16[2,2048,256]{2,1,0:T(8,128)(2,1)S(1)} custom-call(f32[2,16,256]{2,1,0:T(8,128)S(1)} %pad.8.source, f32[2,16,2048]{2,1,0:T(8,128)S(1)} %pad.9.target), custom_call_target="tpu_custom_call" | custom-call | flops 4194304000 | tf_op jit(solution)/shard_map/pallas_call | solution.py:19
  17.4 0.1 collective-permute-done.2.refs_2_
  17.5 2.4 %collective-permute-done.3.refs_3_ = bf16[144,256]{1,0:T(8,128)(2,1)S(1)} collective-permute-done((bf16[144,256]{1,0:T(8,128)(2,1)S(1)}, bf16[144,256]{1,0:T(8,128)(2,1)S(1)}, u32[]{:S(2)}, u32[]{:S(2)}) %collective-permute-start.3) | collective-permute-done | bytes 73760 | tf_op jit(solution)/shard_map/ppermute | solution.py:302
  19.9 0.2 shard_map.139
  20.2 0.0 copy-start.7
  20.2 9.0 %all-gather = bf16[1024,256]{1,0:T(8,128)(2,1)S(1)} all-gather(bf16[128,256]{1,0:T(8,128)(2,1)S(1)} %get-tuple-element.74), channel_id=2, replica_groups=mesh['dom'=8,'feat'=4] {'dom'}, dimensions={0}, use_global_device_ids=true | all-gather | bytes 589824 | tf_op jit(solution)/shard_map/all_gather | solution.py:402
  29.2 0.5 shard_map.140.refs_0_
  29.7 0.3 copy.41
  30.0 0.0 copy-start.11
  30.0 0.1 slice.21
  30.2 0.5 collective-permute-start.4
  30.7 1.5 %collective-permute-start.5 = (bf16[128,256]{1,0:T(8,128)(2,1)S(1)}, bf16[128,256]{1,0:T(8,128)(2,1)S(1)}, u32[]{:S(2)}, u32[]{:S(2)}) collective-permute-start(bf16[128,256]{1,0:T(8,128)(2,1)S(1)} %shard_map.140.refs_0_), channel_id=1, source_target_pairs={{0,2},{1,3},{2,0},{3,1},{4,6},{5,7},{6,4},{7,5},{8,10},{9,11},{10,... | collective-permute-start | bytes 196616 | tf_op jit(solution)/shard_map/ppermute | solution.py:302
  32.2 2.4 %collective-permute-start.6 = (bf16[128,256]{1,0:T(8,128)(2,1)S(1)}, bf16[128,256]{1,0:T(8,128)(2,1)}, u32[]{:S(2)}, u32[]{:S(2)}) collective-permute-start(bf16[128,256]{1,0:T(8,128)(2,1)S(1)} %shard_map.140.refs_0_), channel_id=1, source_target_pairs={{0,3},{1,2},{2,1},{3,0},{4,7},{5,6},{6,5},{7,4},{8,11},{9,10},{10,... | collective-permute-start | bytes 196616 | tf_op jit(solution)/shard_map/ppermute | solution.py:302
  34.6 0.0 collective-permute-done.11.refs_2_
  34.6 1.0 %collective-permute-done.10.refs_1_ = bf16[128,2048]{1,0:T(8,128)(2,1)S(1)} collective-permute-done((bf16[128,2048]{1,0:T(8,128)(2,1)}, bf16[128,2048]{1,0:T(8,128)(2,1)S(1)}, u32[]{:S(2)}, u32[]{:S(2)}) %collective-permute-start.10) | collective-permute-done | bytes 524320 | tf_op jit(solution)/shard_map/ppermute | solution.py:302
  35.6 0.7 collective-permute-start.12
  36.3 1.3 %collective-permute-start.13 = (bf16[128,2048]{1,0:T(8,128)(2,1)S(1)}, bf16[128,2048]{1,0:T(8,128)(2,1)}, u32[]{:S(2)}, u32[]{:S(2)}) collective-permute-start(bf16[128,2048]{1,0:T(8,128)(2,1)S(1)} %collective-permute-done.11.refs_2_), channel_id=1, source_target_pairs={{1,0},{2,3},{5,4},{6,7},{9,8},{10,11},{13,12},{14,15},{17,16},{18,... | collective-permute-start | bytes 1572872 | tf_op jit(solution)/shard_map/ppermute | solution.py:413
  37.6 0.1 copy.37.terms
  37.8 0.8 %copy.35 = s32[16,4]{1,0:T(8,128)S(1)} copy(s32[16,4]{0,1:T(4,128)} %param.17) | data formatting | bytes 512 | tf_op jit(solution)/shard_map/optimization_barrier | solution.py:405
  38.5 0.1 reshape.13.cols
  38.6 0.0 copy-start.1
  38.6 1.6 %copy-done.1 = bf16[16,4,128,128]{3,2,1,0:T(8,128)(2,1)S(1)} copy-done((bf16[16,4,128,128]{3,2,1,0:T(8,128)(2,1)S(1)}, bf16[16,4,128,128]{3,2,1,0:T(8,128)(2,1)}, u32[]{:S(2)}) %copy-start.1) | copy-done | bytes 2097176
  40.2 1.3 %shard_map.141 = (bf16[16,384,128]{2,1,0:T(8,128)(2,1)S(1)}, bf16[192,256]{1,0:T(8,128)(2,1)S(1)}, bf16[192,256]{1,0:T(8,128)(2,1)S(1)}, f32[384,3]{1,0:T(8,128)S(1)}) custom-call(s32[3]{0:T(128)S(1)} %pad_add_fusion.meta, s32[64]{0:T(128)S(1)} %reshape.13.cols, bf16[16,4,128,128]{3,2,1,0:T(8,128)(2,1)S(1)} %copy-done.1, f32[384,3]{1,0:T(8,128)S(1)} %copy.37.terms), custom_call_target="tpu_custom_call" | custom-call | flops 1000000000 | tf_op jit(solution)/shard_map/pallas_call | solution.py:19
  41.6 0.0 collective-permute-done.5.refs_2_
  41.6 0.0 collective-permute-done.6.refs_3_
  41.6 1.1 %shard_map.142.refs_0_ = bf16[384,256]{1,0:T(8,128)(2,1)S(1)} custom-call(s32[3]{0:T(128)S(1)} %pad_add_fusion.meta, bf16[128,256]{1,0:T(8,128)(2,1)S(1)} %shard_map.140.refs_0_, bf16[128,256]{1,0:T(8,128)(2,1)S(1)} %collective-permute-done.4.refs_1_, bf16[128,256]{1,0:T(8,128)(2,1)S(1)} %collective-permute-done.5.refs_2_, ...), custom_call_target="tpu_custom_call" | custom-call | tf_op jit(solution)/shard_map/pallas_call | solution.py:19
  42.7 1.7 %collective-permute-start.8 = (bf16[384,256]{1,0:T(8,128)(2,1)S(1)}, bf16[384,256]{1,0:T(8,128)(2,1)S(1)}, u32[]{:S(2)}, u32[]{:S(2)}) collective-permute-start(bf16[384,256]{1,0:T(8,128)(2,1)S(1)} %shard_map.142.refs_0_), channel_id=1, source_target_pairs={{0,8},{4,12},{8,0},{12,4},{16,24},{20,28},{24,16},{28,20},{1,9},{5... | collective-permute-start | bytes 589832 | tf_op jit(solution)/shard_map/ppermute | solution.py:302
  44.4 1.8 %collective-permute-start.9 = (bf16[384,256]{1,0:T(8,128)(2,1)S(1)}, bf16[384,256]{1,0:T(8,128)(2,1)S(1)}, u32[]{:S(2)}, u32[]{:S(2)}) collective-permute-start(bf16[384,256]{1,0:T(8,128)(2,1)S(1)} %shard_map.142.refs_0_), channel_id=1, source_target_pairs={{0,16},{4,20},{8,24},{12,28},{16,0},{20,4},{24,8},{28,12},{1,17},{... | collective-permute-start | bytes 589832 | tf_op jit(solution)/shard_map/ppermute | solution.py:302
  46.2 0.0 collective-permute-start.7
  46.2 0.0 collective-permute-done.12.refs_3_
  46.2 4.4 %collective-permute-done.13.refs_4_ = bf16[128,2048]{1,0:T(8,128)(2,1)} collective-permute-done((bf16[128,2048]{1,0:T(8,128)(2,1)S(1)}, bf16[128,2048]{1,0:T(8,128)(2,1)}, u32[]{:S(2)}, u32[]{:S(2)}) %collective-permute-start.13) | collective-permute-done | bytes 524320 | tf_op jit(solution)/shard_map/ppermute | solution.py:413
  50.6 1.3 %shard_map.143 = (bf16[704,256]{1,0:T(8,128)(2,1)S(1)}, bf16[704,256]{1,0:T(8,128)(2,1)S(1)}) custom-call(s32[3]{0:T(128)S(1)} %pad_add_fusion.meta, bf16[128,2048]{1,0:T(8,128)(2,1)} %refs_14_.1, bf16[128,2048]{1,0:T(8,128)(2,1)S(1)} %collective-permute-done.10.refs_1_, bf16[128,2048]{1,0:T(8,128)(2,1)S(1)} %collective-permute-done.11.refs_2_, ...), custom_call_target="tpu_custom_call" | custom-call | tf_op jit(solution)/shard_map/pallas_call | solution.py:19
  51.9 0.0 collective-permute-done.8.refs_2_
  51.9 0.0 collective-permute-done.9.refs_3_
  51.9 0.1 collective-permute-start.18
  52.0 2.6 %collective-permute-start.19 = (bf16[704,256]{1,0:T(8,128)(2,1)S(1)}, bf16[704,256]{1,0:T(8,128)(2,1)S(1)}, u32[]{:S(2)}, u32[]{:S(2)}) collective-permute-start(bf16[704,256]{1,0:T(8,128)(2,1)S(1)} %get-tuple-element.105), channel_id=1, source_target_pairs={{4,0},{8,4},{12,8},{16,12},{20,16},{24,20},{28,24},{0,28},{5,1},{9... | collective-permute-start | bytes 1081352 | tf_op jit(solution)/shard_map/ppermute | solution.py:447
  54.7 1.6 %collective-permute-start.14 = (bf16[192,256]{1,0:T(8,128)(2,1)S(1)}, bf16[192,256]{1,0:T(8,128)(2,1)S(1)}, u32[]{:S(2)}, u32[]{:S(2)}) collective-permute-start(bf16[192,256]{1,0:T(8,128)(2,1)S(1)} %slice.19), channel_id=1, source_target_pairs={{0,16},{4,20},{8,24},{12,28},{16,0},{20,4},{24,8},{28,12},{1,17},{... | collective-permute-start | bytes 294920 | tf_op jit(solution)/shard_map/ppermute | solution.py:302
  56.2 0.6 collective-permute-start.15
  56.8 5.3 %shard_map.144 = (f32[384,1536]{1,0:T(8,128)S(1)}, bf16[512,512]{1,0:T(8,128)(2,1)S(1)}, bf16[512,512]{1,0:T(8,128)(2,1)S(1)}) custom-call(s32[3]{0:T(128)S(1)} %pad_add_fusion.meta, bf16[128,2048]{1,0:T(8,128)(2,1)} %refs_14_.1, bf16[128,2048]{1,0:T(8,128)(2,1)S(1)} %collective-permute-done.10.refs_1_, ...), custom_call_target="tpu_custom_call" | custom-call | flops 4563402752 | bytes 8388608 | tf_op jit(solution)/shard_map/pallas_call | solution.py:19
  62.1 0.1 collective-permute-start.16
  62.2 3.6 %collective-permute-done.15.refs_5_ = bf16[192,256]{1,0:T(8,128)(2,1)S(1)} collective-permute-done((bf16[192,256]{1,0:T(8,128)(2,1)S(1)}, bf16[192,256]{1,0:T(8,128)(2,1)S(1)}, u32[]{:S(2)}, u32[]{:S(2)}) %collective-permute-start.15) | collective-permute-done | bytes 98336 | tf_op jit(solution)/shard_map/ppermute | solution.py:302
  65.8 0.1 collective-permute-start.17
  65.8 0.0 collective-permute-done.18.left
  65.9 0.0 copy-start.2
  65.9 0.0 copy-start.4
  65.9 0.0 copy-start.5
  65.9 0.0 copy-start.6
  65.9 1.3 %shard_map.145.refs_11_ = f32[384,512]{1,0:T(8,128)S(1)} custom-call(bf16[704,256]{1,0:T(8,128)(2,1)S(1)} %collective-permute-done.18.left, bf16[704,256]{1,0:T(8,128)(2,1)S(1)} %collective-permute-done.19.right, bf16[512,512]{1,0:T(8,128)(2,1)S(1)} %get-tuple-element.106.state_rim, bf16[512,512]{1,0:T(8,128)(2,1)S(1)} %get-tuple-element.107.one_rim, ...), custom_call_target="tpu_custom_call" | custom-call | flops 12079595520 | bytes 1048576 | tf_op jit(solution)/shard_map/pallas_call | solution.py:19
  67.3 0.0 collective-permute-done.17.refs_7_
  67.3 7.0 %shard_map.146 = bf16[128,2048]{1,0:T(8,128)(2,1)} custom-call(s32[3]{0:T(128)S(1)} %pad_add_fusion.meta, s32[2,16]{1,0:T(2,128)S(1)} %bitcast.25, bf16[384,256]{1,0:T(8,128)(2,1)S(1)} %shard_map.142.refs_0_, bf16[384,256]{1,0:T(8,128)(2,1)S(1)} %collective-permute-done.7.refs_1_, bf16[384,256]{1,0:T(8,128)(2,1)S(1)} %collective-permute-done.8.refs_2_, ...), custom_call_target="tpu_custom_call" | custom-call | flops 3221225472 | bytes 6291456 | tf_op jit(solution)/shard_map/pallas_call | solution.py:19
  (31 shorter events, 0.2 us)
Async XLA Ops:
  0.7 0.7 copy-start.3
  1.4 8.1 %copy-start.10 = (f32[3,128]{1,0:T(4,128)S(1)}, f32[3,128]{1,0:T(4,128)}, u32[]{:S(2)}) copy-start(f32[3,128]{1,0:T(4,128)} %param.22) | copy-start | bytes 4612
  1.4 8.2 %copy-start.8 = (f32[2,10,2048]{2,0,1:T(2,128)S(1)}, f32[2,10,2048]{2,0,1:T(2,128)}, u32[]{:S(2)}) copy-start(f32[2,10,2048]{2,0,1:T(2,128)} %param.24) | copy-start | bytes 491524
  1.4 10.0 %copy-start.9 = (f32[2,10,2048]{2,0,1:T(2,128)S(1)}, f32[2,10,2048]{2,0,1:T(2,128)}, u32[]{:S(2)}) copy-start(f32[2,10,2048]{2,0,1:T(2,128)} %param.25) | copy-start | bytes 491524
  5.4 4.2 %collective-permute-start = (bf16[4,144,256]{2,1,0:T(8,128)(2,1)S(1)}, bf16[4,144,256]{2,1,0:T(8,128)(2,1)S(1)}, u32[]{:S(2)}, u32[]{:S(2)}) collective-permute-start(bf16[4,144,256]{2,1,0:T(8,128)(2,1)S(1)} %get-tuple-element.59), channel_id=1, source_target_pairs={{0,4},{4,0},{8,12},{12,8},{16,20},{20,16},{24,28},{28,24},{1,5},{5... | collective-permute-start | bytes 884744 | tf_op jit(solution)/shard_map/ppermute | solution.py:302
  5.9 28.7 %collective-permute-start.11 = (bf16[128,2048]{1,0:T(8,128)(2,1)}, bf16[128,2048]{1,0:T(8,128)(2,1)S(1)}, u32[]{:S(2)}, u32[]{:S(2)}) collective-permute-start(bf16[128,2048]{1,0:T(8,128)(2,1)} %refs_14_.1), channel_id=1, source_target_pairs={{0,2},{1,3},{2,0},{3,1},{4,6},{5,7},{6,4},{7,5},{8,10},{9,11},{10,... | collective-permute-start | bytes 1572872 | tf_op jit(solution)/shard_map/ppermute | solution.py:302
  9.8 25.8 %collective-permute-start.10 = (bf16[128,2048]{1,0:T(8,128)(2,1)}, bf16[128,2048]{1,0:T(8,128)(2,1)S(1)}, u32[]{:S(2)}, u32[]{:S(2)}) collective-permute-start(bf16[128,2048]{1,0:T(8,128)(2,1)} %refs_14_.1), channel_id=1, source_target_pairs={{0,1},{1,0},{2,3},{3,2},{4,5},{5,4},{6,7},{7,6},{8,9},{9,8},{10,11... | collective-permute-start | bytes 1572872 | tf_op jit(solution)/shard_map/ppermute | solution.py:302
  11.6 8.3 %copy-start = (bf16[2,64,64]{2,1,0:T(8,128)(2,1)S(1)}, bf16[2,64,64]{2,1,0:T(8,128)(2,1)}, u32[]{:S(2)}) copy-start(bf16[2,64,64]{2,1,0:T(8,128)(2,1)} %w_value.1) | copy-start | bytes 49156
  11.6 5.8 %collective-permute-start.1 = (bf16[144,256]{1,0:T(8,128)(2,1)S(1)}, bf16[144,256]{1,0:T(8,128)(2,1)S(1)}, u32[]{:S(2)}, u32[]{:S(2)}) collective-permute-start(bf16[144,256]{1,0:T(8,128)(2,1)S(1)} %get-tuple-element.65), channel_id=1, source_target_pairs={{0,8},{4,12},{8,0},{12,4},{16,24},{20,28},{24,16},{28,20},{1,9},{5... | collective-permute-start | bytes 221192 | tf_op jit(solution)/shard_map/ppermute | solution.py:302
  13.1 4.4 %collective-permute-start.2 = (bf16[144,256]{1,0:T(8,128)(2,1)S(1)}, bf16[144,256]{1,0:T(8,128)(2,1)S(1)}, u32[]{:S(2)}, u32[]{:S(2)}) collective-permute-start(bf16[144,256]{1,0:T(8,128)(2,1)S(1)} %get-tuple-element.66), channel_id=1, source_target_pairs={{0,16},{4,20},{8,24},{12,28},{16,0},{20,4},{24,8},{28,12},{1,17},{... | collective-permute-start | bytes 221192 | tf_op jit(solution)/shard_map/ppermute | solution.py:302
  14.7 5.3 %collective-permute-start.3 = (bf16[144,256]{1,0:T(8,128)(2,1)S(1)}, bf16[144,256]{1,0:T(8,128)(2,1)S(1)}, u32[]{:S(2)}, u32[]{:S(2)}) collective-permute-start(bf16[144,256]{1,0:T(8,128)(2,1)S(1)} %get-tuple-element.67), channel_id=1, source_target_pairs={{0,24},{4,28},{8,16},{12,20},{16,8},{20,12},{24,0},{28,4},{1,25},{... | collective-permute-start | bytes 221192 | tf_op jit(solution)/shard_map/ppermute | solution.py:302
  20.2 9.5 %copy-start.7 = (bf16[3,128,4,512]{3,2,1,0:T(4,128)(2,1)S(1)}, bf16[3,128,4,512]{3,2,1,0:T(4,128)(2,1)}, u32[]{:S(2)}) copy-start(bf16[3,128,4,512]{3,2,1,0:T(4,128)(2,1)} %param.20) | copy-start | bytes 4718596
  30.0 7.6 %copy-start.11 = (bf16[3,128,2]{1,2,0:T(2,128)(2,1)S(1)}, bf16[3,128,2]{1,2,0:T(2,128)(2,1)}, u32[]{:S(2)}) copy-start(bf16[3,128,2]{1,2,0:T(2,128)(2,1)} %param.21) | copy-start | bytes 4612
  30.2 11.4 %collective-permute-start.4 = (bf16[128,256]{1,0:T(8,128)(2,1)S(1)}, bf16[128,256]{1,0:T(8,128)(2,1)S(1)}, u32[]{:S(2)}, u32[]{:S(2)}) collective-permute-start(bf16[128,256]{1,0:T(8,128)(2,1)S(1)} %shard_map.140.refs_0_), channel_id=1, source_target_pairs={{0,1},{1,0},{2,3},{3,2},{4,5},{5,4},{6,7},{7,6},{8,9},{9,8},{10,11... | collective-permute-start | bytes 196616 | tf_op jit(solution)/shard_map/ppermute | solution.py:302
  30.7 10.9 %collective-permute-start.5 = (bf16[128,256]{1,0:T(8,128)(2,1)S(1)}, bf16[128,256]{1,0:T(8,128)(2,1)S(1)}, u32[]{:S(2)}, u32[]{:S(2)}) collective-permute-start(bf16[128,256]{1,0:T(8,128)(2,1)S(1)} %shard_map.140.refs_0_), channel_id=1, source_target_pairs={{0,2},{1,3},{2,0},{3,1},{4,6},{5,7},{6,4},{7,5},{8,10},{9,11},{10,... | collective-permute-start | bytes 196616 | tf_op jit(solution)/shard_map/ppermute | solution.py:302
  32.2 9.4 %collective-permute-start.6 = (bf16[128,256]{1,0:T(8,128)(2,1)S(1)}, bf16[128,256]{1,0:T(8,128)(2,1)}, u32[]{:S(2)}, u32[]{:S(2)}) collective-permute-start(bf16[128,256]{1,0:T(8,128)(2,1)S(1)} %shard_map.140.refs_0_), channel_id=1, source_target_pairs={{0,3},{1,2},{2,1},{3,0},{4,7},{5,6},{6,5},{7,4},{8,11},{9,10},{10,... | collective-permute-start | bytes 196616 | tf_op jit(solution)/shard_map/ppermute | solution.py:302
  35.6 10.6 %collective-permute-start.12 = (bf16[128,2048]{1,0:T(8,128)(2,1)}, bf16[128,2048]{1,0:T(8,128)(2,1)S(1)}, u32[]{:S(2)}, u32[]{:S(2)}) collective-permute-start(bf16[128,2048]{1,0:T(8,128)(2,1)} %refs_14_.1), channel_id=1, source_target_pairs={{1,2},{2,1},{5,6},{6,5},{9,10},{10,9},{13,14},{14,13},{17,18},{18,... | collective-permute-start | bytes 1572872 | tf_op jit(solution)/shard_map/ppermute | solution.py:414
  36.3 14.3 %collective-permute-start.13 = (bf16[128,2048]{1,0:T(8,128)(2,1)S(1)}, bf16[128,2048]{1,0:T(8,128)(2,1)}, u32[]{:S(2)}, u32[]{:S(2)}) collective-permute-start(bf16[128,2048]{1,0:T(8,128)(2,1)S(1)} %collective-permute-done.11.refs_2_), channel_id=1, source_target_pairs={{1,0},{2,3},{5,4},{6,7},{9,8},{10,11},{13,12},{14,15},{17,16},{18,... | collective-permute-start | bytes 1572872 | tf_op jit(solution)/shard_map/ppermute | solution.py:413
  38.6 1.6 %copy-start.1 = (bf16[16,4,128,128]{3,2,1,0:T(8,128)(2,1)S(1)}, bf16[16,4,128,128]{3,2,1,0:T(8,128)(2,1)}, u32[]{:S(2)}) copy-start(bf16[16,4,128,128]{3,2,1,0:T(8,128)(2,1)} %adj.1) | copy-start | bytes 6291460
  42.7 9.2 %collective-permute-start.8 = (bf16[384,256]{1,0:T(8,128)(2,1)S(1)}, bf16[384,256]{1,0:T(8,128)(2,1)S(1)}, u32[]{:S(2)}, u32[]{:S(2)}) collective-permute-start(bf16[384,256]{1,0:T(8,128)(2,1)S(1)} %shard_map.142.refs_0_), channel_id=1, source_target_pairs={{0,8},{4,12},{8,0},{12,4},{16,24},{20,28},{24,16},{28,20},{1,9},{5... | collective-permute-start | bytes 589832 | tf_op jit(solution)/shard_map/ppermute | solution.py:302
  44.4 7.5 %collective-permute-start.9 = (bf16[384,256]{1,0:T(8,128)(2,1)S(1)}, bf16[384,256]{1,0:T(8,128)(2,1)S(1)}, u32[]{:S(2)}, u32[]{:S(2)}) collective-permute-start(bf16[384,256]{1,0:T(8,128)(2,1)S(1)} %shard_map.142.refs_0_), channel_id=1, source_target_pairs={{0,16},{4,20},{8,24},{12,28},{16,0},{20,4},{24,8},{28,12},{1,17},{... | collective-permute-start | bytes 589832 | tf_op jit(solution)/shard_map/ppermute | solution.py:302
  46.2 21.0 %collective-permute-start.7 = (bf16[384,256]{1,0:T(8,128)(2,1)S(1)}, bf16[384,256]{1,0:T(8,128)(2,1)S(1)}, u32[]{:S(2)}, u32[]{:S(2)}) collective-permute-start(bf16[384,256]{1,0:T(8,128)(2,1)S(1)} %shard_map.142.refs_0_), channel_id=1, source_target_pairs={{0,4},{4,0},{8,12},{12,8},{16,20},{20,16},{24,28},{28,24},{1,5},{5... | collective-permute-start | bytes 589832 | tf_op jit(solution)/shard_map/ppermute | solution.py:302
  51.9 13.9 %collective-permute-start.18 = (bf16[704,256]{1,0:T(8,128)(2,1)S(1)}, bf16[704,256]{1,0:T(8,128)(2,1)S(1)}, u32[]{:S(2)}, u32[]{:S(2)}) collective-permute-start(bf16[704,256]{1,0:T(8,128)(2,1)S(1)} %get-tuple-element.104), channel_id=1, source_target_pairs={{0,4},{4,8},{8,12},{12,16},{16,20},{20,24},{24,28},{28,0},{1,5},{5... | collective-permute-start | bytes 1081352 | tf_op jit(solution)/shard_map/ppermute | solution.py:446
  52.0 13.8 %collective-permute-start.19 = (bf16[704,256]{1,0:T(8,128)(2,1)S(1)}, bf16[704,256]{1,0:T(8,128)(2,1)S(1)}, u32[]{:S(2)}, u32[]{:S(2)}) collective-permute-start(bf16[704,256]{1,0:T(8,128)(2,1)S(1)} %get-tuple-element.105), channel_id=1, source_target_pairs={{4,0},{8,4},{12,8},{16,12},{20,16},{24,20},{28,24},{0,28},{5,1},{9... | collective-permute-start | bytes 1081352 | tf_op jit(solution)/shard_map/ppermute | solution.py:447
  54.7 7.4 %collective-permute-start.14 = (bf16[192,256]{1,0:T(8,128)(2,1)S(1)}, bf16[192,256]{1,0:T(8,128)(2,1)S(1)}, u32[]{:S(2)}, u32[]{:S(2)}) collective-permute-start(bf16[192,256]{1,0:T(8,128)(2,1)S(1)} %slice.19), channel_id=1, source_target_pairs={{0,16},{4,20},{8,24},{12,28},{16,0},{20,4},{24,8},{28,12},{1,17},{... | collective-permute-start | bytes 294920 | tf_op jit(solution)/shard_map/ppermute | solution.py:302
  56.2 9.5 %collective-permute-start.15 = (bf16[192,256]{1,0:T(8,128)(2,1)S(1)}, bf16[192,256]{1,0:T(8,128)(2,1)S(1)}, u32[]{:S(2)}, u32[]{:S(2)}) collective-permute-start(bf16[192,256]{1,0:T(8,128)(2,1)S(1)} %slice.20), channel_id=1, source_target_pairs={{0,8},{4,12},{8,0},{12,4},{16,24},{20,28},{24,16},{28,20},{1,9},{5... | collective-permute-start | bytes 294920 | tf_op jit(solution)/shard_map/ppermute | solution.py:302
  62.1 5.2 %collective-permute-start.16 = (bf16[768,256]{1,0:T(8,128)(2,1)S(1)}, bf16[768,256]{1,0:T(8,128)(2,1)S(1)}, u32[]{:S(2)}, u32[]{:S(2)}) collective-permute-start(bf16[768,256]{1,0:T(8,128)(2,1)S(1)} %pad_maximum_fusion), channel_id=1, source_target_pairs={{0,4},{4,0},{8,12},{12,8},{16,20},{20,16},{24,28},{28,24},{1,5},{5... | collective-permute-start | bytes 1179656 | tf_op jit(solution)/shard_map/ppermute | solution.py:302
  65.8 1.5 %collective-permute-start.17 = (bf16[384,256]{1,0:T(8,128)(2,1)S(1)}, bf16[384,256]{1,0:T(8,128)(2,1)S(1)}, u32[]{:S(2)}, u32[]{:S(2)}) collective-permute-start(bf16[384,256]{1,0:T(8,128)(2,1)S(1)} %pad_maximum_fusion.1), channel_id=1, source_target_pairs={{0,4},{4,0},{8,12},{12,8},{16,20},{20,16},{24,28},{28,24},{1,5},{5... | collective-permute-start | bytes 589832 | tf_op jit(solution)/shard_map/ppermute | solution.py:302
  65.9 1.4 %copy-start.2 = (bf16[16,2,128,128]{3,2,1,0:T(8,128)(2,1)S(1)}, bf16[16,2,128,128]{3,2,1,0:T(8,128)(2,1)}, u32[]{:S(2)}) copy-start(bf16[16,2,128,128]{3,2,1,0:T(8,128)(2,1)} %refs_8_.1) | copy-start | bytes 3145732
  65.9 1.4 %copy-start.4 = (s32[2048]{0:T(1024)S(1)}, s32[2048]{0:T(1024)}, u32[]{:S(2)}) copy-start(s32[2048]{0:T(1024)} %param.19) | copy-start | bytes 24580
  65.9 1.4 %copy-start.5 = (bf16[2,2048]{1,0:T(2,128)(2,1)S(1)}, bf16[2,2048]{1,0:T(2,128)(2,1)}, u32[]{:S(2)}) copy-start(bf16[2,2048]{1,0:T(2,128)(2,1)} %refs_13_.1) | copy-start | bytes 24580
  65.9 1.4 %copy-start.6 = (s32[16,2]{0,1:T(2,128)S(1)}, s32[16,2]{0,1:T(2,128)}, u32[]{:S(2)}) copy-start(s32[16,2]{0,1:T(2,128)} %param.27) | copy-start | bytes 388
